TPU v7x, 768 devices: a whole 4x8x12 slice. The times are simulated.
768 devices in a mesh: blk: 64 (over y, x, core), grp: 12 (over z).
Axes of the slice: x: 4, y: 8, z: 12, core: 2. Of those that a mesh axis runs over, the one named last changes fastest.
Arguments:
- image_feats: bfloat16 [12288, 1536], P(('blk', 'grp')), may hold values from -6 to 6
- text_feats: bfloat16 [12288, 1024], P(('blk', 'grp')), may hold values from -6 to 6
- image_proj: bfloat16 [1536, 1152], replicated, may hold values from -0.15625 to 0.15625
- text_proj: bfloat16 [1024, 1152], replicated, may hold values from -0.1875 to 0.1875
- log_temp: float32 [1], replicated, may hold values from 4 to 4.8
- logit_bias: float32 [1], replicated, may hold values from -4 to -1
Outputs:
- image_grad: float32 [12288, 1536], P(('blk', 'grp'))
- text_grad: float32 [12288, 1024], P(('blk', 'grp'))
All inputs are finite; a program needn't handle non-finite values.
Results may differ from a plain program's by a relative error of at most 0.0085.
Values may be sent and summed in bfloat16 or wider, within the bound.
No kernel may reach another device: no remote copies, remote signals or barrier semaphores. Data moves between devices by JAX's collectives and lax.ppermute only.
A program may use at most 64 MiB of HBM per device.

v0:
```python
import jax
import jax.numpy as jnp
from jax import lax
from jax.sharding import PartitionSpec as P

loss_scale = 65536.0
eps = 1e-06


def shifted(shard, axis, by):
    devices = lax.axis_size(axis)
    return lax.ppermute(shard, axis, [(i, (i + by) % devices) for i in range(devices)])


def embed(feats, proj):
    emb = jnp.dot(feats, proj, preferred_element_type=jnp.float32)
    inv = lax.rsqrt(jnp.sum(emb * emb, axis=1, keepdims=True) + eps)
    return (emb * inv, inv)


def backprop(unit, inv, grad_unit, proj):
    delta = inv * (grad_unit - unit * jnp.sum(unit * grad_unit, axis=1, keepdims=True))
    return jnp.dot(delta.astype(jnp.bfloat16), proj.T, preferred_element_type=jnp.float32)


def shards(image_feats, text_feats, image_proj, text_proj, log_temp, logit_bias):
    tok = text_feats.shape[0]
    width = image_proj.shape[1]
    nblk = lax.axis_size("blk")
    ngrp = lax.axis_size("grp")
    my_blk = lax.axis_index("blk")
    my_grp = lax.axis_index("grp")
    img_unit, img_inv = embed(image_feats, image_proj)
    txt_unit, txt_inv = embed(text_feats, text_proj)
    own_text = txt_unit.astype(jnp.bfloat16)
    image_block = lax.all_gather(img_unit.astype(jnp.bfloat16), "grp", axis=0, tiled=True)
    rows_blk = image_block.shape[0]
    total = tok * nblk * ngrp
    span = nblk * tok
    temp = jnp.exp(log_temp[0])
    bias = logit_bias[0]
    factor = loss_scale / total * temp
    img_ids = my_blk * rows_blk + jnp.arange(rows_blk, dtype=jnp.int32)

    def text_ids(first_row, count):
        local = first_row + jnp.arange(count, dtype=jnp.int32)
        return (local // tok * ngrp + my_grp) * tok + local % tok

    def coefficients(piece, ids):
        logits = (
            jnp.einsum("ik,jk->ij", image_block, piece, preferred_element_type=jnp.float32) * temp
            + bias
        )
        diag = (img_ids[:, None] == ids[None, :]).astype(jnp.float32)
        return (factor * (jax.nn.sigmoid(logits) - diag)).astype(jnp.bfloat16)

    def text_term(coef):
        return jnp.einsum("ij,ik->jk", coef, image_block, preferred_element_type=jnp.float32)

    def stash(coefs, texts, coef, piece, first_row):
        coefs = lax.dynamic_update_slice_in_dim(coefs, coef, first_row, 1)
        texts = lax.dynamic_update_slice_in_dim(texts, piece, first_row, 0)
        return (coefs, texts)

    def visit(piece, sums, coefs, texts, anchor):
        first_row = anchor * tok
        coef = coefficients(piece, text_ids(first_row, tok))
        coefs, texts = stash(coefs, texts, coef, piece, first_row)
        return (sums + text_term(coef), coefs, texts)

    coefs_init = jnp.zeros((rows_blk, span), jnp.bfloat16)
    texts_init = jnp.zeros((span, width), jnp.bfloat16)
    sums_init = jnp.zeros((tok, width), jnp.float32)

    def turn(step, state):
        piece, sums, coefs, texts = state
        sums, coefs, texts = visit(piece, sums, coefs, texts, (my_blk - step) % nblk)
        piece = shifted(piece, "blk", 1)
        sums = shifted(sums, "blk", 1)
        return (piece, sums, coefs, texts)

    final = lax.fori_loop(0, nblk, turn, (own_text, sums_init, coefs_init, texts_init))
    txt_du = final[1]
    coefs = final[2]
    texts = final[3]
    image_terms = jnp.dot(coefs, texts, preferred_element_type=jnp.float32)
    img_du = lax.psum_scatter(image_terms, "grp", scatter_dimension=0, tiled=True)
    image_grad = backprop(img_unit, img_inv, img_du, image_proj)
    text_grad = backprop(txt_unit, txt_inv, txt_du, text_proj)
    return (image_grad, text_grad)


def solution(mesh):
    placed = (P(("blk", "grp"), None), P(("blk", "grp"), None), P(), P(), P(), P())
    return jax.shard_map(
        shards,
        mesh=mesh,
        in_specs=placed,
        out_specs=(P(("blk", "grp"), None), P(("blk", "grp"), None)),
        check_vma=False,
    )
```

profile of v0, /device:TPU:6, one launch (start us, length us, event | category | flops | bytes accessed | tf_op | source)
XLA Modules:
  0.0 1209.4 jit_solution(3268160575385572558)
XLA Ops:
  12.0 36.6 %all_gather.3 = bf16[192,1152]{1,0:T(8,128)(2,1)} all-gather(bf16[16,1152]{1,0:T(8,128)(2,1)S(1)} %multiply_convert_fusion.2), channel_id=1, replica_groups=mesh['blk'=64,'grp'=12] {'grp'}, dimensions={0}, use_global_device_ids=true | all-gather | bytes 479232 | tf_op jit(solution)/shard_map/all_gather | solution.py:36
  53.2 1059.9 %while.23 = (s32[]{:T(128)}, bf16[16,1152]{1,0:T(8,128)(2,1)}, f32[16,1152]{1,0:T(8,128)}, bf16[192,1024]{0,1:T(8,128)(2,1)}, bf16[1024,1152]{1,0:T(8,128)(2,1)}...) while((s32[]{:T(128)}, bf16[16,1152]{1,0:T(8,128)(2,1)}, ...), condition=%wide.region_3.4_spmd.clone, body=%wide.region_2.3_spmd.clone.sunk | while | flops 14205522 | bytes 1682992 | solution.py:82
  89.8 6.4 collective-permute-start.1
  105.6 6.4 collective-permute-start.1
  121.5 6.4 collective-permute-start.1
  137.3 6.4 collective-permute-start.1
  153.2 6.4 collective-permute-start.1
  169.0 6.4 collective-permute-start.1
  184.9 6.4 collective-permute-start.1
  200.7 6.4 collective-permute-start.1
  216.6 6.4 collective-permute-start.1
  232.4 6.4 collective-permute-start.1
  248.3 6.4 collective-permute-start.1
  264.1 6.4 collective-permute-start.1
  280.0 6.4 collective-permute-start.1
  295.8 6.4 collective-permute-start.1
  311.7 6.4 collective-permute-start.1
  327.5 6.4 collective-permute-start.1
  343.4 6.4 collective-permute-start.1
  359.2 6.4 collective-permute-start.1
  375.0 6.4 collective-permute-start.1
  390.9 6.4 collective-permute-start.1
  406.7 6.4 collective-permute-start.1
  422.6 6.4 collective-permute-start.1
  438.6 6.2 collective-permute-start.1
  510.1 6.0 collective-permute-done.1
  527.2 6.0 collective-permute-done.1
  561.3 6.0 collective-permute-done.1
  578.3 6.0 collective-permute-done.1
  595.4 6.0 collective-permute-done.1
  629.5 6.1 collective-permute-done.1
  680.7 6.0 collective-permute-done.1
  697.7 6.0 collective-permute-done.1
  714.8 6.0 collective-permute-done.1
  748.9 6.1 collective-permute-done.1
  783.0 6.0 collective-permute-done.1
  817.1 6.0 collective-permute-done.1
  851.2 6.0 collective-permute-done.1
  868.3 6.0 collective-permute-done.1
  902.4 6.1 collective-permute-done.1
  936.6 6.0 collective-permute-done.1
  953.6 6.0 collective-permute-done.1
  970.7 6.0 collective-permute-done.1
  1004.8 6.0 collective-permute-done.1
  1021.9 6.0 collective-permute-done.1
  1056.0 6.0 collective-permute-done.1
  1073.1 6.0 collective-permute-done.1
  1120.9 78.0 %reduce-scatter.2.cloned.1.call-done = f32[16,1152]{1,0:T(8,128)} async-done(((f32[192,1152]{1,0:T(8,128)}), f32[16,1152]{1,0:T(8,128)}) %reduce-scatter.2.cloned.1.call-update) | async-done | bytes 73744 | tf_op jit(solution)/shard_map/reduce_scatter | solution.py:87
  (619 shorter events, 797.4 us)
Async XLA Ops:
  7.2 1191.7 %reduce-scatter.2.cloned.1.call-start = ((), (), s32[]{:S(2)}) async-start(), calls=%async_computation.1 | async-start | bytes 958464 | tf_op jit(solution)/shard_map/reduce_scatter | solution.py:87
  54.6 11.3 collective-permute-start
  68.3 13.4 %collective-permute-start = (bf16[16,1152]{1,0:T(8,128)(2,1)}, bf16[16,1152]{1,0:T(8,128)(2,1)}, u32[]{:S(2)}, u32[]{:S(2)}) collective-permute-start(bf16[16,1152]{1,0:T(8,128)(2,1)} %copy.16), channel_id=1, source_target_pairs={{0,12},{12,24},{24,36},{36,48},{48,60},{60,72},{72,84},{84,96},{96... | collective-permute-start | bytes 110600 | tf_op jit(solution)/shard_map/while/body/eval_jaxpr/ppermute | solution.py:12
  83.1 14.4 %collective-permute-start = (bf16[16,1152]{1,0:T(8,128)(2,1)}, bf16[16,1152]{1,0:T(8,128)(2,1)}, u32[]{:S(2)}, u32[]{:S(2)}) collective-permute-start(bf16[16,1152]{1,0:T(8,128)(2,1)} %copy.16), channel_id=1, source_target_pairs={{0,12},{12,24},{24,36},{36,48},{48,60},{60,72},{72,84},{84,96},{96... | collective-permute-start | bytes 110600 | tf_op jit(solution)/shard_map/while/body/eval_jaxpr/ppermute | solution.py:12
  98.9 14.5 %collective-permute-start = (bf16[16,1152]{1,0:T(8,128)(2,1)}, bf16[16,1152]{1,0:T(8,128)(2,1)}, u32[]{:S(2)}, u32[]{:S(2)}) collective-permute-start(bf16[16,1152]{1,0:T(8,128)(2,1)} %copy.16), channel_id=1, source_target_pairs={{0,12},{12,24},{24,36},{36,48},{48,60},{60,72},{72,84},{84,96},{96... | collective-permute-start | bytes 110600 | tf_op jit(solution)/shard_map/while/body/eval_jaxpr/ppermute | solution.py:12
  114.8 14.5 %collective-permute-start = (bf16[16,1152]{1,0:T(8,128)(2,1)}, bf16[16,1152]{1,0:T(8,128)(2,1)}, u32[]{:S(2)}, u32[]{:S(2)}) collective-permute-start(bf16[16,1152]{1,0:T(8,128)(2,1)} %copy.16), channel_id=1, source_target_pairs={{0,12},{12,24},{24,36},{36,48},{48,60},{60,72},{72,84},{84,96},{96... | collective-permute-start | bytes 110600 | tf_op jit(solution)/shard_map/while/body/eval_jaxpr/ppermute | solution.py:12
  130.6 14.5 %collective-permute-start = (bf16[16,1152]{1,0:T(8,128)(2,1)}, bf16[16,1152]{1,0:T(8,128)(2,1)}, u32[]{:S(2)}, u32[]{:S(2)}) collective-permute-start(bf16[16,1152]{1,0:T(8,128)(2,1)} %copy.16), channel_id=1, source_target_pairs={{0,12},{12,24},{24,36},{36,48},{48,60},{60,72},{72,84},{84,96},{96... | collective-permute-start | bytes 110600 | tf_op jit(solution)/shard_map/while/body/eval_jaxpr/ppermute | solution.py:12
  146.5 14.4 %collective-permute-start = (bf16[16,1152]{1,0:T(8,128)(2,1)}, bf16[16,1152]{1,0:T(8,128)(2,1)}, u32[]{:S(2)}, u32[]{:S(2)}) collective-permute-start(bf16[16,1152]{1,0:T(8,128)(2,1)} %copy.16), channel_id=1, source_target_pairs={{0,12},{12,24},{24,36},{36,48},{48,60},{60,72},{72,84},{84,96},{96... | collective-permute-start | bytes 110600 | tf_op jit(solution)/shard_map/while/body/eval_jaxpr/ppermute | solution.py:12
  162.3 14.5 %collective-permute-start = (bf16[16,1152]{1,0:T(8,128)(2,1)}, bf16[16,1152]{1,0:T(8,128)(2,1)}, u32[]{:S(2)}, u32[]{:S(2)}) collective-permute-start(bf16[16,1152]{1,0:T(8,128)(2,1)} %copy.16), channel_id=1, source_target_pairs={{0,12},{12,24},{24,36},{36,48},{48,60},{60,72},{72,84},{84,96},{96... | collective-permute-start | bytes 110600 | tf_op jit(solution)/shard_map/while/body/eval_jaxpr/ppermute | solution.py:12
  178.2 14.5 %collective-permute-start = (bf16[16,1152]{1,0:T(8,128)(2,1)}, bf16[16,1152]{1,0:T(8,128)(2,1)}, u32[]{:S(2)}, u32[]{:S(2)}) collective-permute-start(bf16[16,1152]{1,0:T(8,128)(2,1)} %copy.16), channel_id=1, source_target_pairs={{0,12},{12,24},{24,36},{36,48},{48,60},{60,72},{72,84},{84,96},{96... | collective-permute-start | bytes 110600 | tf_op jit(solution)/shard_map/while/body/eval_jaxpr/ppermute | solution.py:12
  194.0 14.4 %collective-permute-start = (bf16[16,1152]{1,0:T(8,128)(2,1)}, bf16[16,1152]{1,0:T(8,128)(2,1)}, u32[]{:S(2)}, u32[]{:S(2)}) collective-permute-start(bf16[16,1152]{1,0:T(8,128)(2,1)} %copy.16), channel_id=1, source_target_pairs={{0,12},{12,24},{24,36},{36,48},{48,60},{60,72},{72,84},{84,96},{96... | collective-permute-start | bytes 110600 | tf_op jit(solution)/shard_map/while/body/eval_jaxpr/ppermute | solution.py:12
  209.9 14.5 %collective-permute-start = (bf16[16,1152]{1,0:T(8,128)(2,1)}, bf16[16,1152]{1,0:T(8,128)(2,1)}, u32[]{:S(2)}, u32[]{:S(2)}) collective-permute-start(bf16[16,1152]{1,0:T(8,128)(2,1)} %copy.16), channel_id=1, source_target_pairs={{0,12},{12,24},{24,36},{36,48},{48,60},{60,72},{72,84},{84,96},{96... | collective-permute-start | bytes 110600 | tf_op jit(solution)/shard_map/while/body/eval_jaxpr/ppermute | solution.py:12
  225.7 14.5 %collective-permute-start = (bf16[16,1152]{1,0:T(8,128)(2,1)}, bf16[16,1152]{1,0:T(8,128)(2,1)}, u32[]{:S(2)}, u32[]{:S(2)}) collective-permute-start(bf16[16,1152]{1,0:T(8,128)(2,1)} %copy.16), channel_id=1, source_target_pairs={{0,12},{12,24},{24,36},{36,48},{48,60},{60,72},{72,84},{84,96},{96... | collective-permute-start | bytes 110600 | tf_op jit(solution)/shard_map/while/body/eval_jaxpr/ppermute | solution.py:12
  241.6 14.5 %collective-permute-start = (bf16[16,1152]{1,0:T(8,128)(2,1)}, bf16[16,1152]{1,0:T(8,128)(2,1)}, u32[]{:S(2)}, u32[]{:S(2)}) collective-permute-start(bf16[16,1152]{1,0:T(8,128)(2,1)} %copy.16), channel_id=1, source_target_pairs={{0,12},{12,24},{24,36},{36,48},{48,60},{60,72},{72,84},{84,96},{96... | collective-permute-start | bytes 110600 | tf_op jit(solution)/shard_map/while/body/eval_jaxpr/ppermute | solution.py:12
  257.4 14.5 %collective-permute-start = (bf16[16,1152]{1,0:T(8,128)(2,1)}, bf16[16,1152]{1,0:T(8,128)(2,1)}, u32[]{:S(2)}, u32[]{:S(2)}) collective-permute-start(bf16[16,1152]{1,0:T(8,128)(2,1)} %copy.16), channel_id=1, source_target_pairs={{0,12},{12,24},{24,36},{36,48},{48,60},{60,72},{72,84},{84,96},{96... | collective-permute-start | bytes 110600 | tf_op jit(solution)/shard_map/while/body/eval_jaxpr/ppermute | solution.py:12
  273.3 14.4 %collective-permute-start = (bf16[16,1152]{1,0:T(8,128)(2,1)}, bf16[16,1152]{1,0:T(8,128)(2,1)}, u32[]{:S(2)}, u32[]{:S(2)}) collective-permute-start(bf16[16,1152]{1,0:T(8,128)(2,1)} %copy.16), channel_id=1, source_target_pairs={{0,12},{12,24},{24,36},{36,48},{48,60},{60,72},{72,84},{84,96},{96... | collective-permute-start | bytes 110600 | tf_op jit(solution)/shard_map/while/body/eval_jaxpr/ppermute | solution.py:12
  289.1 14.5 %collective-permute-start = (bf16[16,1152]{1,0:T(8,128)(2,1)}, bf16[16,1152]{1,0:T(8,128)(2,1)}, u32[]{:S(2)}, u32[]{:S(2)}) collective-permute-start(bf16[16,1152]{1,0:T(8,128)(2,1)} %copy.16), channel_id=1, source_target_pairs={{0,12},{12,24},{24,36},{36,48},{48,60},{60,72},{72,84},{84,96},{96... | collective-permute-start | bytes 110600 | tf_op jit(solution)/shard_map/while/body/eval_jaxpr/ppermute | solution.py:12
  305.0 14.5 %collective-permute-start = (bf16[16,1152]{1,0:T(8,128)(2,1)}, bf16[16,1152]{1,0:T(8,128)(2,1)}, u32[]{:S(2)}, u32[]{:S(2)}) collective-permute-start(bf16[16,1152]{1,0:T(8,128)(2,1)} %copy.16), channel_id=1, source_target_pairs={{0,12},{12,24},{24,36},{36,48},{48,60},{60,72},{72,84},{84,96},{96... | collective-permute-start | bytes 110600 | tf_op jit(solution)/shard_map/while/body/eval_jaxpr/ppermute | solution.py:12
  320.8 14.4 %collective-permute-start = (bf16[16,1152]{1,0:T(8,128)(2,1)}, bf16[16,1152]{1,0:T(8,128)(2,1)}, u32[]{:S(2)}, u32[]{:S(2)}) collective-permute-start(bf16[16,1152]{1,0:T(8,128)(2,1)} %copy.16), channel_id=1, source_target_pairs={{0,12},{12,24},{24,36},{36,48},{48,60},{60,72},{72,84},{84,96},{96... | collective-permute-start | bytes 110600 | tf_op jit(solution)/shard_map/while/body/eval_jaxpr/ppermute | solution.py:12
  336.7 14.5 %collective-permute-start = (bf16[16,1152]{1,0:T(8,128)(2,1)}, bf16[16,1152]{1,0:T(8,128)(2,1)}, u32[]{:S(2)}, u32[]{:S(2)}) collective-permute-start(bf16[16,1152]{1,0:T(8,128)(2,1)} %copy.16), channel_id=1, source_target_pairs={{0,12},{12,24},{24,36},{36,48},{48,60},{60,72},{72,84},{84,96},{96... | collective-permute-start | bytes 110600 | tf_op jit(solution)/shard_map/while/body/eval_jaxpr/ppermute | solution.py:12
  352.5 14.4 %collective-permute-start = (bf16[16,1152]{1,0:T(8,128)(2,1)}, bf16[16,1152]{1,0:T(8,128)(2,1)}, u32[]{:S(2)}, u32[]{:S(2)}) collective-permute-start(bf16[16,1152]{1,0:T(8,128)(2,1)} %copy.16), channel_id=1, source_target_pairs={{0,12},{12,24},{24,36},{36,48},{48,60},{60,72},{72,84},{84,96},{96... | collective-permute-start | bytes 110600 | tf_op jit(solution)/shard_map/while/body/eval_jaxpr/ppermute | solution.py:12
  368.4 14.5 %collective-permute-start = (bf16[16,1152]{1,0:T(8,128)(2,1)}, bf16[16,1152]{1,0:T(8,128)(2,1)}, u32[]{:S(2)}, u32[]{:S(2)}) collective-permute-start(bf16[16,1152]{1,0:T(8,128)(2,1)} %copy.16), channel_id=1, source_target_pairs={{0,12},{12,24},{24,36},{36,48},{48,60},{60,72},{72,84},{84,96},{96... | collective-permute-start | bytes 110600 | tf_op jit(solution)/shard_map/while/body/eval_jaxpr/ppermute | solution.py:12
  384.2 14.5 %collective-permute-start = (bf16[16,1152]{1,0:T(8,128)(2,1)}, bf16[16,1152]{1,0:T(8,128)(2,1)}, u32[]{:S(2)}, u32[]{:S(2)}) collective-permute-start(bf16[16,1152]{1,0:T(8,128)(2,1)} %copy.16), channel_id=1, source_target_pairs={{0,12},{12,24},{24,36},{36,48},{48,60},{60,72},{72,84},{84,96},{96... | collective-permute-start | bytes 110600 | tf_op jit(solution)/shard_map/while/body/eval_jaxpr/ppermute | solution.py:12
  400.1 14.5 %collective-permute-start = (bf16[16,1152]{1,0:T(8,128)(2,1)}, bf16[16,1152]{1,0:T(8,128)(2,1)}, u32[]{:S(2)}, u32[]{:S(2)}) collective-permute-start(bf16[16,1152]{1,0:T(8,128)(2,1)} %copy.16), channel_id=1, source_target_pairs={{0,12},{12,24},{24,36},{36,48},{48,60},{60,72},{72,84},{84,96},{96... | collective-permute-start | bytes 110600 | tf_op jit(solution)/shard_map/while/body/eval_jaxpr/ppermute | solution.py:12
  415.9 14.4 %collective-permute-start = (bf16[16,1152]{1,0:T(8,128)(2,1)}, bf16[16,1152]{1,0:T(8,128)(2,1)}, u32[]{:S(2)}, u32[]{:S(2)}) collective-permute-start(bf16[16,1152]{1,0:T(8,128)(2,1)} %copy.16), channel_id=1, source_target_pairs={{0,12},{12,24},{24,36},{36,48},{48,60},{60,72},{72,84},{84,96},{96... | collective-permute-start | bytes 110600 | tf_op jit(solution)/shard_map/while/body/eval_jaxpr/ppermute | solution.py:12
  432.2 14.0 %collective-permute-start = (bf16[16,1152]{1,0:T(8,128)(2,1)}, bf16[16,1152]{1,0:T(8,128)(2,1)}, u32[]{:S(2)}, u32[]{:S(2)}) collective-permute-start(bf16[16,1152]{1,0:T(8,128)(2,1)} %copy.16), channel_id=1, source_target_pairs={{0,12},{12,24},{24,36},{36,48},{48,60},{60,72},{72,84},{84,96},{96... | collective-permute-start | bytes 110600 | tf_op jit(solution)/shard_map/while/body/eval_jaxpr/ppermute | solution.py:12
  449.2 12.8 %collective-permute-start = (bf16[16,1152]{1,0:T(8,128)(2,1)}, bf16[16,1152]{1,0:T(8,128)(2,1)}, u32[]{:S(2)}, u32[]{:S(2)}) collective-permute-start(bf16[16,1152]{1,0:T(8,128)(2,1)} %copy.16), channel_id=1, source_target_pairs={{0,12},{12,24},{24,36},{36,48},{48,60},{60,72},{72,84},{84,96},{96... | collective-permute-start | bytes 110600 | tf_op jit(solution)/shard_map/while/body/eval_jaxpr/ppermute | solution.py:12
  466.3 11.6 collective-permute-start
  483.4 10.4 collective-permute-start
  500.4 9.7 collective-permute-start
  517.5 9.7 collective-permute-start
  534.5 9.7 collective-permute-start
  619.8 9.7 collective-permute-start
  636.9 9.7 collective-permute-start
  653.9 9.7 collective-permute-start
  705.1 9.7 collective-permute-start
  722.2 9.7 collective-permute-start
  756.4 9.7 collective-permute-start
  790.4 9.7 collective-permute-start
  875.7 9.7 collective-permute-start
  909.9 9.7 collective-permute-start
  926.9 9.7 collective-permute-start
  961.0 9.7 collective-permute-start
  1012.2 9.7 collective-permute-start
  1029.3 9.7 collective-permute-start
  1063.4 9.7 collective-permute-start
  1080.5 9.7 collective-permute-start
  1097.5 9.7 collective-permute-start
  (85 other events, 731.1 us)
Sparse Core Ops, SparseCore 0:
  1116.8 82.0 reduce-scatter.1
where the time goes:
time: 1220 us; the launch traced here: 1210 us
  starting transfers between devices  365 us (30%)
  waiting for transfers between devices  309 us (25%)
  matrix products  293 us (24%)
  local copies, waits for them, and re-layouts  182 us (15%)
  blocking collectives  36.6 us (3%)
  between operations  14.9 us (1%)
    ppermute x128, starting transfers between devices, shifted(): lax.ppermute(shard, axis, [(i, (i + by) % devices) for i in range(devices)])  365 us
    ppermute x128, waiting for transfers between devices, shifted(): lax.ppermute(shard, axis, [(i, (i + by) % devices) for i in range(devices)])  231 us
    dot_general x64, matrix products, coefficients(): jnp.einsum('ik,jk->ij', image_block, piece, preferred_element_type=jnp.fl...  163 us
    dot_general x64, matrix products, text_term(): jnp.einsum('ij,ik->jk', coef, image_block, preferred_element_type=jnp.flo...  118 us
    while x64, local copies, waits for them, and re-layouts  88.8 us
    dynamic_update_slice x64, local copies, waits for them, and re-layouts, stash(): texts = lax.dynamic_update_slice_in_dim(texts, piece, first_row, 0)  88.7 us
    reduce_scatter x1, waiting for transfers between devices, shards(): lax.psum_scatter(image_terms, 'grp', scatter_dimension=0, tiled=True)  78 us
    all_gather x1, blocking collectives, shards(): lax.all_gather(img_unit.astype(jnp.bfloat16), 'grp', axis=0, tiled=True)  36.6 us
  transfers between devices with their start and end apart: 129, of which 43 were waited for; matrix products, arithmetic and copies ran while one was open for 31% of the time, Pallas kernels for 0%

commit v1 on v0

v1 whole, which is shorter than its diff:
```python
import functools

import jax
import jax.numpy as jnp
import numpy as np
from jax import lax
from jax.experimental import pallas as pl
from jax.experimental.pallas import tpu as pltpu
from jax.sharding import Mesh
from jax.sharding import PartitionSpec as P

loss_scale = 65536.0
eps = 1e-06
f32 = jnp.float32
bf16 = jnp.bfloat16


def gathered(rows, axis):
    n = lax.axis_size(axis)
    copies = jnp.broadcast_to(rows[None], (n,) + rows.shape)
    return lax.all_to_all(copies, axis, 0, 0, tiled=True).reshape((-1,) + rows.shape[1:])


def scattered(parts, axis):
    n = lax.axis_size(axis)
    cut = parts.astype(bf16).reshape((n, -1) + parts.shape[1:])
    return jnp.sum(lax.all_to_all(cut, axis, 0, 0, tiled=True).astype(f32), axis=0)


def embed(feats, proj):
    emb = jnp.dot(feats, proj, preferred_element_type=f32)
    inv = lax.rsqrt(jnp.sum(emb * emb, axis=1, keepdims=True) + eps)
    return (emb * inv, inv)


def backprop(unit, inv, grad_unit, proj):
    delta = inv * (grad_unit - unit * jnp.sum(unit * grad_unit, axis=1, keepdims=True))
    return jnp.dot(delta.astype(bf16), proj.T, preferred_element_type=f32)


def tile_kernel(own, first, scalars, img_ref, txt_ref, img_out, txt_out):
    temp = scalars[0]
    bias = scalars[1]
    factor = scalars[2]
    img = img_ref[...]
    txt = txt_ref[...]
    logits = (
        lax.dot_general(img, txt, (((1,), (1,)), ((), ())), preferred_element_type=f32) * temp + bias
    )
    rows = lax.broadcasted_iota(jnp.int32, logits.shape, 0) - first[0]
    cols = lax.broadcasted_iota(jnp.int32, logits.shape, 1) - first[1]
    diag = ((rows == cols) & (rows >= 0) & (rows < own)).astype(f32)
    coef = (factor * (jax.nn.sigmoid(logits) - diag)).astype(bf16)
    img_out[...] = jnp.dot(coef, txt, preferred_element_type=f32).astype(img_out.dtype)
    txt_out[...] = lax.dot_general(
        coef, img, (((0,), (0,)), ((), ())), preferred_element_type=f32
    ).astype(txt_out.dtype)


def tile(own, first, scalars, img, txt):
    vmem = pl.BlockSpec(memory_space=pltpu.VMEM)
    smem = pl.BlockSpec(memory_space=pltpu.SMEM)
    n, m, w = img.shape[0], txt.shape[0], img.shape[1]
    return pl.pallas_call(
        functools.partial(tile_kernel, own),
        out_shape=[jax.ShapeDtypeStruct(img.shape, bf16), jax.ShapeDtypeStruct(txt.shape, bf16)],
        in_specs=[smem, smem, vmem, vmem],
        out_specs=[vmem, vmem],
        cost_estimate=pl.CostEstimate(
            flops=6 * n * m * w, bytes_accessed=4 * (n + m) * w, transcendentals=n * m
        ),
        compiler_params=pltpu.CompilerParams(vmem_limit_bytes=32 * 2**20),
    )(first, scalars, img, txt)


def shards(image_feats, text_feats, image_proj, text_proj, log_temp, logit_bias):
    own = text_feats.shape[0]
    total = own * lax.axis_size(("y", "x", "core", "z"))
    img_unit, img_inv = embed(image_feats, image_proj)
    txt_unit, txt_inv = embed(text_feats, text_proj)
    img_rows = lax.all_gather(gathered(img_unit.astype(bf16), "z"), "core", tiled=True)
    txt_rows = gathered(gathered(txt_unit.astype(bf16), "y"), "x")
    temp = jnp.exp(log_temp[0])
    scalars = jnp.stack([temp, logit_bias[0], loss_scale / total * temp])
    first = own * jnp.stack([lax.axis_index(("core", "z")), lax.axis_index(("x", "y"))])
    img_terms, txt_terms = tile(own, first, scalars, img_rows, txt_rows)
    img_du = scattered(scattered(img_terms, "core"), "z")
    txt_du = scattered(scattered(txt_terms, "x"), "y")
    image_grad = backprop(img_unit, img_inv, img_du, image_proj)
    text_grad = backprop(txt_unit, txt_inv, txt_du, text_proj)
    return (image_grad, text_grad)


def solution(mesh):
    blk, grp = mesh.devices.shape
    sizes = (blk // 8, 4, 2, grp)
    fine = Mesh(np.asarray(mesh.devices).reshape(sizes), ("y", "x", "core", "z"))
    rows = P(("y", "x", "core", "z"), None)
    return jax.shard_map(
        shards,
        mesh=fine,
        in_specs=(rows, rows, P(), P(), P(), P()),
        out_specs=(rows, rows),
        check_vma=False,
    )
```

time: 1220 us -> 162 us (0.13)
  the two profiles are of different devices: /device:TPU:6 before, /device:TPU:64 now
where the time goes in v1:
time: 162 us; the launch traced here: 160 us
  waiting for transfers between devices  62.2 us (38%)
  blocking collectives  43.8 us (27%)
  starting transfers between devices  23.9 us (15%)
  other arithmetic  9.6 us (6%)
  matrix products  9.48 us (6%)
  local copies, waits for them, and re-layouts  6.05 us (4%)
  Pallas kernels  3.32 us (2%)
  between operations  2.08 us (1%)
    all_to_all x3, waiting for transfers between devices, scattered(): lax.all_to_all(cut, axis, 0, 0, tiled=True).astype(f32)  41.5 us
    all_to_all x1, blocking collectives, gathered(): lax.all_to_all(copies, axis, 0, 0, tiled=True)  34.4 us
    all_to_all x2, waiting for transfers between devices, gathered(): lax.all_to_all(copies, axis, 0, 0, tiled=True)  20.8 us
    all_to_all x3, starting transfers between devices, scattered(): lax.all_to_all(cut, axis, 0, 0, tiled=True).astype(f32)  12.5 us
    all_to_all x2, starting transfers between devices, gathered(): lax.all_to_all(copies, axis, 0, 0, tiled=True)  11.4 us
    reduce_sum x4, other arithmetic, scattered(): jnp.sum(lax.all_to_all(cut, axis, 0, 0, tiled=True).astype(f32), axis=0)  6.52 us
    dot_general x2, matrix products, backprop(): return jnp.dot(delta.astype(bf16), proj.T, preferred_element_type=f32)  5.64 us
    all_to_all x1, blocking collectives, scattered(): lax.all_to_all(cut, axis, 0, 0, tiled=True).astype(f32)  5.22 us
  transfers between devices with their start and end apart: 5, of which 5 were waited for; matrix products, arithmetic and copies ran while one was open for 7% of the time, Pallas kernels for 0%

profile of v1, /device:TPU:64, one launch (start us, length us, event | category | flops | bytes accessed | tf_op | source)
XLA Modules:
  0.0 160.4 jit_solution(16862646915481815756)
XLA Ops:
  0.6 0.0 copy-start
  0.6 2.4 %multiply_reduce_fusion.2 = (f32[16]{0:T(128)S(1)}, f32[16,1152]{1,0:T(8,128)S(1)}) fusion(bf16[16,1024]{1,0:T(8,128)(2,1)} %param.7, bf16[1024,1152]{1,0:T(8,128)(2,1)} %param.9), kind=kOutput, calls=%fused_computation.6 | convolution fusion | flops 37785584 | bytes 2465856 | tf_op jit(solution)/shard_map/dot_general | solution.py:31
  3.0 0.0 copy-start.3
  3.0 0.6 copy-done.3
  3.6 0.1 multiply_convert_fusion.2
  3.7 0.7 broadcast_in_dim.9
  4.5 7.1 %all-to-all-start.1 = ((bf16[8,16,1152]{2,1,0:T(8,128)(2,1)}), bf16[8,16,1152]{2,1,0:T(8,128)(2,1)}, u32[]{:S(2)}, u32[]{:S(2)}) async-start(bf16[8,16,1152]{2,1,0:T(8,128)(2,1)} %broadcast_in_dim.9), calls=%async_computation.1 | async-start | bytes 589824 | tf_op jit(solution)/shard_map/all_to_all | solution.py:21
  11.6 0.0 copy-done
  11.6 1.5 multiply_reduce_fusion.3
  13.0 0.0 copy-start.4
  13.1 0.6 copy-done.4
  13.7 0.7 multiply_convert_fusion.3
  14.4 9.9 %all-to-all-done.1 = bf16[8,16,1152]{2,1,0:T(8,128)(2,1)} async-done(((bf16[8,16,1152]{2,1,0:T(8,128)(2,1)}), bf16[8,16,1152]{2,1,0:T(8,128)(2,1)}, u32[]{:S(2)}, u32[]{:S(2)}) %all-to-all-start.1) | async-done | bytes 294944 | tf_op jit(solution)/shard_map/all_to_all | solution.py:21
  24.2 0.8 broadcast_in_dim.8
  25.0 34.4 %all_to_all.35 = bf16[12,16,1152]{2,1,0:T(8,128)(2,1)} all-to-all(bf16[12,16,1152]{2,1,0:T(8,128)(2,1)S(1)} %broadcast_in_dim.8), channel_id=1, replica_groups=mesh['y'=8,'x'=4,'core'=2,'z'=12] {'z'}, dimensions={0} | all-to-all | bytes 884736 | tf_op jit(solution)/shard_map/all_to_all | solution.py:21
  59.5 2.1 %broadcast_in_dim.11 = bf16[4,128,1152]{2,1,0:T(8,128)(2,1)} broadcast(bf16[128,1152]{1,0:T(8,128)(2,1)} %bitcast.3), dimensions={1,2} | broadcast | bytes 1474560 | tf_op jit(solution)/shard_map/broadcast_in_dim | solution.py:20
  61.6 4.3 %all-to-all-start.2 = ((bf16[4,128,1152]{2,1,0:T(8,128)(2,1)}), bf16[4,128,1152]{2,1,0:T(8,128)(2,1)}, u32[]{:S(2)}, u32[]{:S(2)}) async-start(bf16[4,128,1152]{2,1,0:T(8,128)(2,1)} %broadcast_in_dim.11), calls=%async_computation.2 | async-start | bytes 2359296 | tf_op jit(solution)/shard_map/all_to_all | solution.py:21
  67.2 0.1 pad_maximum_fusion.scalars
  67.3 0.1 add_multiply_fusion.first
  67.3 4.1 %all_gather.3.img_ref = bf16[384,1152]{1,0:T(8,128)(2,1)} all-gather(bf16[192,1152]{1,0:T(8,128)(2,1)} %bitcast.18), channel_id=1, replica_groups=mesh['y'=8,'x'=4,'core'=2,'z'=12] {'core'}, dimensions={0}, use_global_device_ids=true | all-gather | bytes 1327104 | tf_op jit(solution)/shard_map/all_gather | solution.py:81
  71.5 10.9 %all-to-all-done.2 = bf16[4,128,1152]{2,1,0:T(8,128)(2,1)} async-done(((bf16[4,128,1152]{2,1,0:T(8,128)(2,1)}), bf16[4,128,1152]{2,1,0:T(8,128)(2,1)}, u32[]{:S(2)}, u32[]{:S(2)}) %all-to-all-start.2) | async-done | bytes 1179680 | tf_op jit(solution)/shard_map/all_to_all | solution.py:21
  82.4 0.0 copy-start.2
  82.4 1.2 copy-done.2
  83.6 3.3 %shard_map.77 = (bf16[384,1152]{1,0:T(8,128)(2,1)S(1)}, bf16[512,1152]{1,0:T(8,128)(2,1)S(1)}) custom-call(s32[2]{0:T(128)S(1)} %add_multiply_fusion.first, f32[3]{0:T(128)S(1)} %pad_maximum_fusion.scalars, bf16[384,1152]{1,0:T(8,128)(2,1)S(1)} %copy-done.2, bf16[512,1152]{1,0:T(8,128)(2,1)} %bitcast.4.txt_ref), custom_call_target="tpu_custom_call" | custom-call | flops 1358954496 | bytes 4128768 | tf_op jit(solution)/shard_map/pallas_call | solution.py:64
  86.9 0.0 copy-start.1
  86.9 5.2 %all_to_all.36 = bf16[2,192,1152]{2,1,0:T(8,128)(2,1)} all-to-all(bf16[2,192,1152]{2,1,0:T(8,128)(2,1)S(1)} %bitcast.16), channel_id=1, replica_groups=mesh['y'=8,'x'=4,'core'=2,'z'=12] {'core'}, dimensions={0} | all-to-all | bytes 1769472 | tf_op jit(solution)/shard_map/all_to_all | solution.py:27
  92.1 0.0 copy-done.1
  92.1 4.3 %all-to-all-start.5 = ((bf16[4,128,1152]{2,1,0:T(8,128)(2,1)}), bf16[4,128,1152]{2,1,0:T(8,128)(2,1)}, u32[]{:S(2)}, u32[]{:S(2)}) async-start(bf16[4,128,1152]{2,1,0:T(8,128)(2,1)} %bitcast.15), calls=%async_computation.5 | async-start | bytes 2359296 | tf_op jit(solution)/shard_map/all_to_all | solution.py:27
  96.4 2.2 %reduce_sum.80 = bf16[192,1152]{1,0:T(8,128)(2,1)} reduce(bf16[2,192,1152]{2,1,0:T(8,128)(2,1)} %all_to_all.36, bf16[]{:T(256)} %constant.31.clone.1), dimensions={0}, to_apply=%region_2.0 | reduce | flops 221184 | bytes 1327106 | tf_op jit(solution)/shard_map/reduce_sum | solution.py:27
  98.6 14.9 %all-to-all-done.5 = bf16[4,128,1152]{2,1,0:T(8,128)(2,1)} async-done(((bf16[4,128,1152]{2,1,0:T(8,128)(2,1)}), bf16[4,128,1152]{2,1,0:T(8,128)(2,1)}, u32[]{:S(2)}, u32[]{:S(2)}) %all-to-all-start.5) | async-done | bytes 1179680 | tf_op jit(solution)/shard_map/all_to_all | solution.py:27
  113.5 4.2 %all-to-all-start.4 = ((bf16[12,16,1152]{2,1,0:T(8,128)(2,1)}), bf16[12,16,1152]{2,1,0:T(8,128)(2,1)}, u32[]{:S(2)}, u32[]{:S(2)}) async-start(bf16[12,16,1152]{2,1,0:T(8,128)(2,1)} %bitcast.17), calls=%async_computation.4 | async-start | bytes 884736 | tf_op jit(solution)/shard_map/all_to_all | solution.py:27
  117.7 2.2 %reduce_sum.83 = bf16[128,1152]{1,0:T(8,128)(2,1)} reduce(bf16[4,128,1152]{2,1,0:T(8,128)(2,1)} %all-to-all-done.5, bf16[]{:T(256)} %constant.31.clone.1), dimensions={0}, to_apply=%region_5.0 | reduce | flops 442368 | bytes 1474562 | tf_op jit(solution)/shard_map/reduce_sum | solution.py:27
  119.9 18.4 %all-to-all-done.4 = bf16[12,16,1152]{2,1,0:T(8,128)(2,1)} async-done(((bf16[12,16,1152]{2,1,0:T(8,128)(2,1)}), bf16[12,16,1152]{2,1,0:T(8,128)(2,1)}, u32[]{:S(2)}, u32[]{:S(2)}) %all-to-all-start.4) | async-done | bytes 442400 | tf_op jit(solution)/shard_map/all_to_all | solution.py:27
  138.3 4.1 %all-to-all-start.6 = ((bf16[8,16,1152]{2,1,0:T(8,128)(2,1)}), bf16[8,16,1152]{2,1,0:T(8,128)(2,1)}, u32[]{:S(2)}, u32[]{:S(2)}) async-start(bf16[8,16,1152]{2,1,0:T(8,128)(2,1)} %bitcast.19), calls=%async_computation.6 | async-start | bytes 589824 | tf_op jit(solution)/shard_map/all_to_all | solution.py:27
  142.4 1.1 convert_reduce_fusion
  143.5 1.1 multiply_reduce_fusion.1
  144.6 2.6 %fusion = f32[16,1536]{1,0:T(8,128)} fusion(bf16[1536,1152]{1,0:T(8,128)(2,1)S(1)} %copy-done, f32[16,1152]{1,0:T(8,128)S(1)} %convert_reduce_fusion, f32[16,1152]{1,0:T(8,128)} %copy-done.4, f32[16]{0:T(128)S(1)} %multiply_reduce_fusion.1, f32[16]{0:T(128)S(1)} %add_rsqrt_fusion.1), kind=kOutput, calls=%fused_computation.10 | convolution fusion | flops 56715264 | bytes 3784832 | tf_op jit(solution)/shard_map/dot_general | solution.py:38
  147.1 8.1 %all-to-all-done.6 = bf16[8,16,1152]{2,1,0:T(8,128)(2,1)} async-done(((bf16[8,16,1152]{2,1,0:T(8,128)(2,1)}), bf16[8,16,1152]{2,1,0:T(8,128)(2,1)}, u32[]{:S(2)}, u32[]{:S(2)}) %all-to-all-start.6) | async-done | bytes 294944 | tf_op jit(solution)/shard_map/all_to_all | solution.py:27
  155.2 1.0 convert_reduce_fusion.1
  156.2 1.1 multiply_reduce_fusion
  157.3 3.1 %fusion.1 = f32[16,1024]{1,0:T(8,128)} fusion(bf16[1024,1152]{1,0:T(8,128)(2,1)} %param.9, f32[16,1152]{1,0:T(8,128)S(1)} %convert_reduce_fusion.1, f32[16,1152]{1,0:T(8,128)} %copy-done.3, f32[16]{0:T(128)S(1)} %multiply_reduce_fusion, f32[16]{0:T(128)S(1)} %add_rsqrt_fusion), kind=kOutput, calls=%fused_computation.11 | convolution fusion | flops 37840896 | bytes 2572416 | tf_op jit(solution)/shard_map/dot_general | solution.py:38
  (2 shorter events, 0.0 us)
Async XLA Ops:
  0.6 10.9 %copy-start = (bf16[1536,1152]{1,0:T(8,128)(2,1)S(1)}, bf16[1536,1152]{1,0:T(8,128)(2,1)}, u32[]{:S(2)}) copy-start(bf16[1536,1152]{1,0:T(8,128)(2,1)} %param.8) | copy-start | bytes 10616836
  3.0 0.6 copy-start.3
  4.5 19.8 %all-to-all-start.1 = ((bf16[8,16,1152]{2,1,0:T(8,128)(2,1)}), bf16[8,16,1152]{2,1,0:T(8,128)(2,1)}, u32[]{:S(2)}, u32[]{:S(2)}) async-start(bf16[8,16,1152]{2,1,0:T(8,128)(2,1)} %broadcast_in_dim.9), calls=%async_computation.1 | async-start | bytes 589824 | tf_op jit(solution)/shard_map/all_to_all | solution.py:21
  13.0 0.6 copy-start.4
  61.6 20.8 %all-to-all-start.2 = ((bf16[4,128,1152]{2,1,0:T(8,128)(2,1)}), bf16[4,128,1152]{2,1,0:T(8,128)(2,1)}, u32[]{:S(2)}, u32[]{:S(2)}) async-start(bf16[4,128,1152]{2,1,0:T(8,128)(2,1)} %broadcast_in_dim.11), calls=%async_computation.2 | async-start | bytes 2359296 | tf_op jit(solution)/shard_map/all_to_all | solution.py:21
  82.4 1.2 copy-start.2
  86.9 5.2 %copy-start.1 = (bf16[512,1152]{1,0:T(8,128)(2,1)}, bf16[512,1152]{1,0:T(8,128)(2,1)S(1)}, u32[]{:S(2)}) copy-start(bf16[512,1152]{1,0:T(8,128)(2,1)S(1)} %get-tuple-element.5) | copy-start | bytes 3538948
  92.1 21.4 %all-to-all-start.5 = ((bf16[4,128,1152]{2,1,0:T(8,128)(2,1)}), bf16[4,128,1152]{2,1,0:T(8,128)(2,1)}, u32[]{:S(2)}, u32[]{:S(2)}) async-start(bf16[4,128,1152]{2,1,0:T(8,128)(2,1)} %bitcast.15), calls=%async_computation.5 | async-start | bytes 2359296 | tf_op jit(solution)/shard_map/all_to_all | solution.py:27
  113.5 24.8 %all-to-all-start.4 = ((bf16[12,16,1152]{2,1,0:T(8,128)(2,1)}), bf16[12,16,1152]{2,1,0:T(8,128)(2,1)}, u32[]{:S(2)}, u32[]{:S(2)}) async-start(bf16[12,16,1152]{2,1,0:T(8,128)(2,1)} %bitcast.17), calls=%async_computation.4 | async-start | bytes 884736 | tf_op jit(solution)/shard_map/all_to_all | solution.py:27
  138.3 16.9 %all-to-all-start.6 = ((bf16[8,16,1152]{2,1,0:T(8,128)(2,1)}), bf16[8,16,1152]{2,1,0:T(8,128)(2,1)}, u32[]{:S(2)}, u32[]{:S(2)}) async-start(bf16[8,16,1152]{2,1,0:T(8,128)(2,1)} %bitcast.19), calls=%async_computation.6 | async-start | bytes 589824 | tf_op jit(solution)/shard_map/all_to_all | solution.py:27

commit v2 on v1

v2 whole, which is shorter than its diff:
```python
import functools

import jax
import jax.numpy as jnp
import numpy as np
from jax import lax
from jax.experimental import pallas as pl
from jax.experimental.pallas import tpu as pltpu
from jax.sharding import Mesh
from jax.sharding import PartitionSpec as P

loss_scale = 65536.0
eps = 1e-06
f32 = jnp.float32
bf16 = jnp.bfloat16


def shift(axis, by):
    n = lax.axis_size(axis)
    return [(i, (i + by) % n) for i in range(n)]


def gathered(rows, axis):
    n = lax.axis_size(axis)
    copies = jnp.broadcast_to(rows[None], (n,) + rows.shape)
    return lax.all_to_all(copies, axis, 0, 0, tiled=True).reshape((-1,) + rows.shape[1:])


def scattered(parts, axis):
    n = lax.axis_size(axis)
    cut = parts.astype(bf16).reshape((n, -1) + parts.shape[1:])
    return jnp.sum(lax.all_to_all(cut, axis, 0, 0, tiled=True).astype(f32), axis=0)


ahead = (0, 4, 8, 2, 6, 10, 1, 5, 9, 3, 7, 11)
z_axes = ("z3", "z4")


def reduced_along_z(parts, own):
    for by in (1, 2):
        half = parts.shape[0] // 2
        got = lax.ppermute(parts[half:].astype(bf16), z_axes, shift(z_axes, by))
        parts = parts[:half] + got.astype(f32)
    far = [
        lax.ppermute(parts[k * own : (k + 1) * own].astype(bf16), z_axes, shift(z_axes, 4 * k))
        for k in (1, 2)
    ]
    return parts[:own] + far[0].astype(f32) + far[1].astype(f32)


def embed(feats, proj):
    emb = jnp.dot(feats, proj, preferred_element_type=f32)
    inv = lax.rsqrt(jnp.sum(emb * emb, axis=1, keepdims=True) + eps)
    return (emb * inv, inv)


def backprop(unit, inv, grad_unit, proj):
    delta = inv * (grad_unit - unit * jnp.sum(unit * grad_unit, axis=1, keepdims=True))
    return jnp.dot(delta.astype(bf16), proj.T, preferred_element_type=f32)


def tile_kernel(own, place, scalars, img_ref, txt_ref, near_out, far_out, txt_out, img_buf):
    temp = scalars[0]
    bias = scalars[1]
    factor = scalars[2]
    core = place[0]
    z = place[1]
    half = len(ahead) * own
    for c in range(2):
        for k, by in enumerate(ahead):
            owner = lax.rem(z + by, 12)
            block = lax.rem(core + c, 2) * 12 + lax.rem(owner, 4) * 3 + lax.div(owner, 4)
            img_buf[pl.ds(c * half + k * own, own), :] = img_ref[
                pl.ds(pl.multiple_of(block * own, own), own), :
            ]
    img = img_buf[...]
    txt = txt_ref[...]
    logits = (
        lax.dot_general(img, txt, (((1,), (1,)), ((), ())), preferred_element_type=f32) * temp + bias
    )
    rows = lax.broadcasted_iota(jnp.int32, logits.shape, 0)
    cols = lax.broadcasted_iota(jnp.int32, logits.shape, 1) - place[2]
    diag = ((rows == cols) & (rows < own)).astype(f32)
    coef = (factor * (jax.nn.sigmoid(logits) - diag)).astype(bf16)
    txt_out[...] = lax.dot_general(
        coef, img, (((0,), (0,)), ((), ())), preferred_element_type=f32
    ).astype(bf16)
    img_du = jnp.dot(coef, txt, preferred_element_type=f32)
    near_out[...] = img_du[:half]
    far_out[...] = img_du[half:].astype(bf16)


def tile(own, place, scalars, img, txt):
    vmem = pl.BlockSpec(memory_space=pltpu.VMEM)
    smem = pl.BlockSpec(memory_space=pltpu.SMEM)
    n, m, w = img.shape[0], txt.shape[0], img.shape[1]
    return pl.pallas_call(
        functools.partial(tile_kernel, own),
        out_shape=[
            jax.ShapeDtypeStruct((n // 2, w), f32),
            jax.ShapeDtypeStruct((n // 2, w), bf16),
            jax.ShapeDtypeStruct((m, w), bf16),
        ],
        in_specs=[smem, smem, vmem, vmem],
        out_specs=[vmem, vmem, vmem],
        scratch_shapes=[pltpu.VMEM((n, w), bf16)],
        cost_estimate=pl.CostEstimate(
            flops=6 * n * m * w, bytes_accessed=4 * (n + m) * w, transcendentals=n * m
        ),
        compiler_params=pltpu.CompilerParams(vmem_limit_bytes=32 * 2**20),
    )(place, scalars, img, txt)


def shards(image_feats, text_feats, image_proj, text_proj, log_temp, logit_bias):
    own = text_feats.shape[0]
    total = own * lax.axis_size(("y", "x", "core") + z_axes)
    img_unit, img_inv = embed(image_feats, image_proj)
    txt_unit, txt_inv = embed(text_feats, text_proj)
    img_rows = lax.all_gather(img_unit.astype(bf16), "z3", tiled=True)
    txt_rows = gathered(txt_unit.astype(bf16), "y")
    img_rows, txt_rows = lax.optimization_barrier((img_rows, txt_rows))
    img_rows = lax.all_gather(lax.all_gather(img_rows, "z4", tiled=True), "core", tiled=True)
    txt_rows = gathered(txt_rows, "x")
    temp = jnp.exp(log_temp[0])
    scalars = jnp.stack([temp, logit_bias[0], loss_scale / total * temp])
    place = jnp.stack(
        [lax.axis_index("core"), lax.axis_index(z_axes), own * lax.axis_index(("x", "y"))]
    )
    near, far, txt_terms = tile(own, place, scalars, img_rows, txt_rows)
    near = near + lax.ppermute(far, "core", shift("core", 1)).astype(f32)
    img_du = reduced_along_z(near, own)
    txt_du = scattered(scattered(txt_terms, "x"), "y")
    image_grad = backprop(img_unit, img_inv, img_du, image_proj)
    text_grad = backprop(txt_unit, txt_inv, txt_du, text_proj)
    return (image_grad, text_grad)


def solution(mesh):
    blk, grp = mesh.devices.shape
    sizes = (blk // 8, 4, 2, grp // 4, 4)
    fine = Mesh(np.asarray(mesh.devices).reshape(sizes), ("y", "x", "core") + z_axes)
    rows = P(("y", "x", "core") + z_axes, None)
    return jax.shard_map(
        shards,
        mesh=fine,
        in_specs=(rows, rows, P(), P(), P(), P()),
        out_specs=(rows, rows),
        check_vma=False,
    )
```

time: 162 us -> 133 us (0.82)
  the two profiles are of different devices: /device:TPU:64 before, /device:TPU:6 now
where the time goes in v2:
time: 133 us; the launch traced here: 131 us
  blocking collectives  42 us (32%)
  starting transfers between devices  40.2 us (30%)
  waiting for transfers between devices  18.3 us (14%)
  matrix products  9.51 us (7%)
  other arithmetic  7.67 us (6%)
  local copies, waits for them, and re-layouts  7.64 us (6%)
  Pallas kernels  3.45 us (3%)
  between operations  2.13 us (2%)
    all_gather x1, blocking collectives, shards(): img_rows = lax.all_gather(img_unit.astype(bf16), 'z3', tiled=True)  23.1 us
    all_gather x1, blocking collectives, shards(): lax.all_gather(img_rows, 'z4', tiled=True)  16.3 us
    all_to_all x2, starting transfers between devices, scattered(): lax.all_to_all(cut, axis, 0, 0, tiled=True).astype(f32)  12.1 us
    ppermute x2, waiting for transfers between devices, reduced_along_z(): got = lax.ppermute(parts[half:].astype(bf16), z_axes, shift(z_axes, by))  12.1 us
    all_to_all x2, starting transfers between devices, gathered(): lax.all_to_all(copies, axis, 0, 0, tiled=True)  11.9 us
    ppermute x2, starting transfers between devices, reduced_along_z(): lax.ppermute(parts[k * own:(k + 1) * own].astype(bf16), z_axes, shift(z_a...  9.74 us
    dot_general x2, matrix products, backprop(): return jnp.dot(delta.astype(bf16), proj.T, preferred_element_type=f32)  5.67 us
    ppermute x2, waiting for transfers between devices, reduced_along_z(): lax.ppermute(parts[k * own:(k + 1) * own].astype(bf16), z_axes, shift(z_a...  4.51 us
  transfers between devices with their start and end apart: 9, of which 4 were waited for; matrix products, arithmetic and copies ran while one was open for 6% of the time, Pallas kernels for 0%

profile of v2, /device:TPU:6, one launch (start us, length us, event | category | flops | bytes accessed | tf_op | source)
XLA Modules:
  0.0 130.8 jit_solution(17967242384673293477)
XLA Ops:
  0.6 0.0 copy-start
  0.6 2.4 %multiply_reduce_fusion.2 = (f32[16]{0:T(128)S(1)}, f32[16,1152]{1,0:T(8,128)S(1)}) fusion(bf16[16,1024]{1,0:T(8,128)(2,1)} %param.7, bf16[1024,1152]{1,0:T(8,128)(2,1)} %param.9), kind=kOutput, calls=%fused_computation.12 | convolution fusion | flops 37785584 | bytes 2465856 | tf_op jit(solution)/shard_map/dot_general | solution.py:52
  3.0 0.0 copy-start.4
  3.0 0.6 copy-done.4
  3.6 0.1 multiply_convert_fusion.2
  3.7 0.7 broadcast_in_dim.4
  4.5 7.1 %all-to-all-start = ((bf16[8,16,1152]{2,1,0:T(8,128)(2,1)}), bf16[8,16,1152]{2,1,0:T(8,128)(2,1)}, u32[]{:S(2)}, u32[]{:S(2)}) async-start(bf16[8,16,1152]{2,1,0:T(8,128)(2,1)} %broadcast_in_dim.4), calls=%async_computation | async-start | bytes 589824 | tf_op jit(solution)/shard_map/all_to_all | solution.py:26
  11.6 1.5 %multiply_reduce_fusion.3 = (f32[16]{0:T(128)S(1)}, f32[16,1152]{1,0:T(8,128)S(1)}) fusion(bf16[16,1536]{1,0:T(8,128)(2,1)} %param.6, bf16[1536,1152]{1,0:T(8,128)(2,1)S(1)} %copy-done), kind=kOutput, calls=%fused_computation.13 | convolution fusion | flops 56659952 | bytes 3661888 | tf_op jit(solution)/shard_map/dot_general | solution.py:52
  13.1 0.6 copy-done.5
  13.7 0.1 multiply_convert_fusion.3
  13.8 23.1 %all_gather.9 = bf16[48,1152]{1,0:T(8,128)(2,1)} all-gather(bf16[16,1152]{1,0:T(8,128)(2,1)S(1)} %multiply_convert_fusion.3), channel_id=1, replica_groups=mesh['y'=8,'x'=4,'core'=2,'z3'=3,'z4'=4] {'z3'}, dimensions={0}, use_global_device_ids=true | all-gather | bytes 147456 | tf_op jit(solution)/shard_map/all_gather | solution.py:119
  36.9 0.0 all-to-all-done
  36.9 2.1 %broadcast_in_dim.5 = bf16[4,128,1152]{2,1,0:T(8,128)(2,1)} broadcast(bf16[128,1152]{1,0:T(8,128)(2,1)} %bitcast.3), dimensions={1,2} | broadcast | bytes 1474560 | tf_op jit(solution)/shard_map/broadcast_in_dim | solution.py:25
  39.0 4.8 %all-to-all-start.1 = ((bf16[4,128,1152]{2,1,0:T(8,128)(2,1)}), bf16[4,128,1152]{2,1,0:T(8,128)(2,1)}, u32[]{:S(2)}, u32[]{:S(2)}) async-start(bf16[4,128,1152]{2,1,0:T(8,128)(2,1)} %broadcast_in_dim.5), calls=%async_computation.1 | async-start | bytes 2359296 | tf_op jit(solution)/shard_map/all_to_all | solution.py:26
  45.1 0.1 pad_maximum_fusion.scalars
  45.1 0.1 pad_add_fusion.place
  45.2 16.3 %all_gather.10 = bf16[192,1152]{1,0:T(8,128)(2,1)S(1)} all-gather(bf16[48,1152]{1,0:T(8,128)(2,1)} %all_gather.9), channel_id=1, replica_groups=mesh['y'=8,'x'=4,'core'=2,'z3'=3,'z4'=4] {'z4'}, dimensions={0}, use_global_device_ids=true | all-gather | bytes 552960 | tf_op jit(solution)/shard_map/all_gather | solution.py:122
  61.5 2.6 %all_gather.11.img_ref = bf16[384,1152]{1,0:T(8,128)(2,1)} all-gather(bf16[192,1152]{1,0:T(8,128)(2,1)S(1)} %all_gather.10), channel_id=1, replica_groups=mesh['y'=8,'x'=4,'core'=2,'z3'=3,'z4'=4] {'core'}, dimensions={0}, use_global_device_ids=true | all-gather | bytes 1327104 | tf_op jit(solution)/shard_map/all_gather | solution.py:122
  64.1 0.0 all-to-all-done.1
  64.1 1.2 copy-done.2
  65.2 3.4 %shard_map.77 = (f32[192,1152]{1,0:T(8,128)S(1)}, bf16[192,1152]{1,0:T(8,128)(2,1)S(1)}, bf16[512,1152]{1,0:T(8,128)(2,1)S(1)}) custom-call(s32[3]{0:T(128)S(1)} %pad_add_fusion.place, f32[3]{0:T(128)S(1)} %pad_maximum_fusion.scalars, bf16[384,1152]{1,0:T(8,128)(2,1)S(1)} %copy-done.2, bf16[512,1152]{1,0:T(8,128)(2,1)} %bitcast.4.txt_ref), custom_call_target="tpu_custom_call" | custom-call | flops 1358954496 | bytes 4128768 | tf_op jit(solution)/shard_map/pallas_call | solution.py:97
  68.7 2.0 %collective-permute-start = (bf16[192,1152]{1,0:T(8,128)(2,1)S(1)}, bf16[192,1152]{1,0:T(8,128)(2,1)S(1)}, u32[]{:S(2)}, u32[]{:S(2)}) collective-permute-start(bf16[192,1152]{1,0:T(8,128)(2,1)S(1)} %get-tuple-element.10), channel_id=1, source_target_pairs={{0,12},{12,0},{1,13},{13,1},{2,14},{14,2},{3,15},{15,3},{4,16},{16... | collective-permute-start | bytes 1327112 | tf_op jit(solution)/shard_map/ppermute | solution.py:130
  70.7 1.6 %collective-permute-done = bf16[192,1152]{1,0:T(8,128)(2,1)S(1)} collective-permute-done((bf16[192,1152]{1,0:T(8,128)(2,1)S(1)}, bf16[192,1152]{1,0:T(8,128)(2,1)S(1)}, u32[]{:S(2)}, u32[]{:S(2)}) %collective-permute-start) | collective-permute-done | bytes 442400 | tf_op jit(solution)/shard_map/ppermute | solution.py:130
  72.4 0.1 convert_add_fusion
  72.5 0.0 copy-start.3
  72.5 0.9 copy-done.3
  73.4 0.7 slice.51
  74.1 2.5 %collective-permute-start.1 = (bf16[96,1152]{1,0:T(8,128)(2,1)}, bf16[96,1152]{1,0:T(8,128)(2,1)}, u32[]{:S(2)}, u32[]{:S(2)}) collective-permute-start(bf16[96,1152]{1,0:T(8,128)(2,1)} %slice.51), channel_id=1, source_target_pairs={{0,1},{1,2},{2,3},{3,4},{4,5},{5,6},{6,7},{7,8},{8,9},{9,10},{10,1... | collective-permute-start | bytes 663560 | tf_op jit(solution)/shard_map/ppermute | solution.py:42
  76.6 4.9 %all-to-all-start.2 = ((bf16[4,128,1152]{2,1,0:T(8,128)(2,1)}), bf16[4,128,1152]{2,1,0:T(8,128)(2,1)}, u32[]{:S(2)}, u32[]{:S(2)}) async-start(bf16[4,128,1152]{2,1,0:T(8,128)(2,1)} %bitcast.13), calls=%async_computation.2 | async-start | bytes 2359296 | tf_op jit(solution)/shard_map/all_to_all | solution.py:32
  81.5 3.5 %collective-permute-done.1 = bf16[96,1152]{1,0:T(8,128)(2,1)} collective-permute-done((bf16[96,1152]{1,0:T(8,128)(2,1)}, bf16[96,1152]{1,0:T(8,128)(2,1)}, u32[]{:S(2)}, u32[]{:S(2)}) %collective-permute-start.1) | collective-permute-done | bytes 221216 | tf_op jit(solution)/shard_map/ppermute | solution.py:42
  85.0 1.1 slice_add_fusion
  86.1 1.9 %collective-permute-start.2 = (bf16[48,1152]{1,0:T(8,128)(2,1)S(1)}, bf16[48,1152]{1,0:T(8,128)(2,1)S(1)}, u32[]{:S(2)}, u32[]{:S(2)}) collective-permute-start(bf16[48,1152]{1,0:T(8,128)(2,1)S(1)} %slice.52), channel_id=1, source_target_pairs={{0,2},{1,3},{2,4},{3,5},{4,6},{5,7},{6,8},{7,9},{8,10},{9,11},{10,... | collective-permute-start | bytes 331784 | tf_op jit(solution)/shard_map/ppermute | solution.py:42
  88.0 8.6 %collective-permute-done.2 = bf16[48,1152]{1,0:T(8,128)(2,1)S(1)} collective-permute-done((bf16[48,1152]{1,0:T(8,128)(2,1)S(1)}, bf16[48,1152]{1,0:T(8,128)(2,1)S(1)}, u32[]{:S(2)}, u32[]{:S(2)}) %collective-permute-start.2) | collective-permute-done | bytes 110624 | tf_op jit(solution)/shard_map/ppermute | solution.py:42
  96.7 0.8 fusion.8
  97.4 0.0 all-to-all-done.2
  97.4 2.2 %reduce_sum.60 = bf16[128,1152]{1,0:T(8,128)(2,1)} reduce(bf16[4,128,1152]{2,1,0:T(8,128)(2,1)} %all-to-all-done.2, bf16[]{:T(256)} %constant.34.clone.1), dimensions={0}, to_apply=%region_3.0 | reduce | flops 442368 | bytes 1474562 | tf_op jit(solution)/shard_map/reduce_sum | solution.py:32
  99.6 7.2 %all-to-all-start.3 = ((bf16[8,16,1152]{2,1,0:T(8,128)(2,1)}), bf16[8,16,1152]{2,1,0:T(8,128)(2,1)}, u32[]{:S(2)}, u32[]{:S(2)}) async-start(bf16[8,16,1152]{2,1,0:T(8,128)(2,1)} %bitcast.14), calls=%async_computation.3 | async-start | bytes 589824 | tf_op jit(solution)/shard_map/all_to_all | solution.py:32
  106.9 0.8 fusion.9
  107.7 4.5 %collective-permute-start.3 = (bf16[16,1152]{1,0:T(8,128)(2,1)S(1)}, bf16[16,1152]{1,0:T(8,128)(2,1)S(1)}, u32[]{:S(2)}, u32[]{:S(2)}) collective-permute-start(bf16[16,1152]{1,0:T(8,128)(2,1)S(1)} %get-tuple-element.14), channel_id=1, source_target_pairs={{0,4},{1,5},{2,6},{3,7},{4,8},{5,9},{6,10},{7,11},{8,0},{9,1},{10,... | collective-permute-start | bytes 110600 | tf_op jit(solution)/shard_map/ppermute | solution.py:45
  112.2 5.2 %collective-permute-start.4 = (bf16[16,1152]{1,0:T(8,128)(2,1)S(1)}, bf16[16,1152]{1,0:T(8,128)(2,1)S(1)}, u32[]{:S(2)}, u32[]{:S(2)}) collective-permute-start(bf16[16,1152]{1,0:T(8,128)(2,1)S(1)} %get-tuple-element.15), channel_id=1, source_target_pairs={{0,8},{1,9},{2,10},{3,11},{4,0},{5,1},{6,2},{7,3},{8,4},{9,5},{10,... | collective-permute-start | bytes 110600 | tf_op jit(solution)/shard_map/ppermute | solution.py:45
  117.4 0.0 collective-permute-done.3
  117.4 4.5 %collective-permute-done.4 = bf16[16,1152]{1,0:T(8,128)(2,1)S(1)} collective-permute-done((bf16[16,1152]{1,0:T(8,128)(2,1)S(1)}, bf16[16,1152]{1,0:T(8,128)(2,1)S(1)}, u32[]{:S(2)}, u32[]{:S(2)}) %collective-permute-start.4) | collective-permute-done | bytes 36896 | tf_op jit(solution)/shard_map/ppermute | solution.py:45
  121.9 1.1 multiply_reduce_fusion.1
  123.1 2.6 %fusion.1 = f32[16,1536]{1,0:T(8,128)} fusion(bf16[1536,1152]{1,0:T(8,128)(2,1)S(1)} %copy-done, f32[16,1152]{1,0:T(8,128)} %copy-done.5, f32[16]{0:T(128)S(1)} %multiply_reduce_fusion.1, f32[16]{0:T(128)S(1)} %add_rsqrt_fusion.1, f32[48,1152]{1,0:T(8,128)} %get-tuple-element.13, bf16[16,1152]{1,0:T(8,128)(2,1)S(1)} %collective-permute-done.4, ...), kind=kOutput, calls=%fused_computation.16 | convolution fusion | flops 56788992 | bytes 3858560 | tf_op jit(solution)/shard_map/dot_general | solution.py:59
  125.7 0.0 all-to-all-done.3
  125.7 1.0 convert_reduce_fusion
  126.7 1.1 multiply_reduce_fusion
  127.7 3.1 %fusion.2 = f32[16,1024]{1,0:T(8,128)} fusion(bf16[1024,1152]{1,0:T(8,128)(2,1)} %param.9, f32[16,1152]{1,0:T(8,128)S(1)} %convert_reduce_fusion, f32[16,1152]{1,0:T(8,128)} %copy-done.4, f32[16]{0:T(128)S(1)} %multiply_reduce_fusion, f32[16]{0:T(128)S(1)} %add_rsqrt_fusion), kind=kOutput, calls=%fused_computation.17 | convolution fusion | flops 37840896 | bytes 2572416 | tf_op jit(solution)/shard_map/dot_general | solution.py:59
  (8 shorter events, 0.0 us)
Async XLA Ops:
  0.6 10.9 %copy-start = (bf16[1536,1152]{1,0:T(8,128)(2,1)S(1)}, bf16[1536,1152]{1,0:T(8,128)(2,1)}, u32[]{:S(2)}) copy-start(bf16[1536,1152]{1,0:T(8,128)(2,1)} %param.8) | copy-start | bytes 10616836
  3.0 0.6 copy-start.4
  4.5 32.4 %all-to-all-start = ((bf16[8,16,1152]{2,1,0:T(8,128)(2,1)}), bf16[8,16,1152]{2,1,0:T(8,128)(2,1)}, u32[]{:S(2)}, u32[]{:S(2)}) async-start(bf16[8,16,1152]{2,1,0:T(8,128)(2,1)} %broadcast_in_dim.4), calls=%async_computation | async-start | bytes 589824 | tf_op jit(solution)/shard_map/all_to_all | solution.py:26
  13.0 0.6 copy-start.5
  39.0 25.1 %all-to-all-start.1 = ((bf16[4,128,1152]{2,1,0:T(8,128)(2,1)}), bf16[4,128,1152]{2,1,0:T(8,128)(2,1)}, u32[]{:S(2)}, u32[]{:S(2)}) async-start(bf16[4,128,1152]{2,1,0:T(8,128)(2,1)} %broadcast_in_dim.5), calls=%async_computation.1 | async-start | bytes 2359296 | tf_op jit(solution)/shard_map/all_to_all | solution.py:26
  64.1 1.2 copy-start.2
  68.7 7.9 %copy-start.1 = (bf16[512,1152]{1,0:T(8,128)(2,1)}, bf16[512,1152]{1,0:T(8,128)(2,1)S(1)}, u32[]{:S(2)}) copy-start(bf16[512,1152]{1,0:T(8,128)(2,1)S(1)} %get-tuple-element.11) | copy-start | bytes 3538948
  68.7 3.7 %collective-permute-start = (bf16[192,1152]{1,0:T(8,128)(2,1)S(1)}, bf16[192,1152]{1,0:T(8,128)(2,1)S(1)}, u32[]{:S(2)}, u32[]{:S(2)}) collective-permute-start(bf16[192,1152]{1,0:T(8,128)(2,1)S(1)} %get-tuple-element.10), channel_id=1, source_target_pairs={{0,12},{12,0},{1,13},{13,1},{2,14},{14,2},{3,15},{15,3},{4,16},{16... | collective-permute-start | bytes 1327112 | tf_op jit(solution)/shard_map/ppermute | solution.py:130
  72.5 0.9 copy-start.3
  74.1 10.9 %collective-permute-start.1 = (bf16[96,1152]{1,0:T(8,128)(2,1)}, bf16[96,1152]{1,0:T(8,128)(2,1)}, u32[]{:S(2)}, u32[]{:S(2)}) collective-permute-start(bf16[96,1152]{1,0:T(8,128)(2,1)} %slice.51), channel_id=1, source_target_pairs={{0,1},{1,2},{2,3},{3,4},{4,5},{5,6},{6,7},{7,8},{8,9},{9,10},{10,1... | collective-permute-start | bytes 663560 | tf_op jit(solution)/shard_map/ppermute | solution.py:42
  76.6 20.8 %all-to-all-start.2 = ((bf16[4,128,1152]{2,1,0:T(8,128)(2,1)}), bf16[4,128,1152]{2,1,0:T(8,128)(2,1)}, u32[]{:S(2)}, u32[]{:S(2)}) async-start(bf16[4,128,1152]{2,1,0:T(8,128)(2,1)} %bitcast.13), calls=%async_computation.2 | async-start | bytes 2359296 | tf_op jit(solution)/shard_map/all_to_all | solution.py:32
  86.1 10.6 %collective-permute-start.2 = (bf16[48,1152]{1,0:T(8,128)(2,1)S(1)}, bf16[48,1152]{1,0:T(8,128)(2,1)S(1)}, u32[]{:S(2)}, u32[]{:S(2)}) collective-permute-start(bf16[48,1152]{1,0:T(8,128)(2,1)S(1)} %slice.52), channel_id=1, source_target_pairs={{0,2},{1,3},{2,4},{3,5},{4,6},{5,7},{6,8},{7,9},{8,10},{9,11},{10,... | collective-permute-start | bytes 331784 | tf_op jit(solution)/shard_map/ppermute | solution.py:42
  99.6 26.0 %all-to-all-start.3 = ((bf16[8,16,1152]{2,1,0:T(8,128)(2,1)}), bf16[8,16,1152]{2,1,0:T(8,128)(2,1)}, u32[]{:S(2)}, u32[]{:S(2)}) async-start(bf16[8,16,1152]{2,1,0:T(8,128)(2,1)} %bitcast.14), calls=%async_computation.3 | async-start | bytes 589824 | tf_op jit(solution)/shard_map/all_to_all | solution.py:32
  107.7 9.8 %collective-permute-start.3 = (bf16[16,1152]{1,0:T(8,128)(2,1)S(1)}, bf16[16,1152]{1,0:T(8,128)(2,1)S(1)}, u32[]{:S(2)}, u32[]{:S(2)}) collective-permute-start(bf16[16,1152]{1,0:T(8,128)(2,1)S(1)} %get-tuple-element.14), channel_id=1, source_target_pairs={{0,4},{1,5},{2,6},{3,7},{4,8},{5,9},{6,10},{7,11},{8,0},{9,1},{10,... | collective-permute-start | bytes 110600 | tf_op jit(solution)/shard_map/ppermute | solution.py:45
  112.2 9.8 %collective-permute-start.4 = (bf16[16,1152]{1,0:T(8,128)(2,1)S(1)}, bf16[16,1152]{1,0:T(8,128)(2,1)S(1)}, u32[]{:S(2)}, u32[]{:S(2)}) collective-permute-start(bf16[16,1152]{1,0:T(8,128)(2,1)S(1)} %get-tuple-element.15), channel_id=1, source_target_pairs={{0,8},{1,9},{2,10},{3,11},{4,0},{5,1},{6,2},{7,3},{8,4},{9,5},{10,... | collective-permute-start | bytes 110600 | tf_op jit(solution)/shard_map/ppermute | solution.py:45

commit v3 on v1

v3 whole, which is shorter than its diff:
```python
import functools

import jax
import jax.numpy as jnp
import numpy as np
from jax import lax
from jax.experimental import pallas as pl
from jax.experimental.pallas import tpu as pltpu
from jax.sharding import Mesh
from jax.sharding import PartitionSpec as P

loss_scale = 65536.0
eps = 1e-06
f32 = jnp.float32
bf16 = jnp.bfloat16

vmem = pl.BlockSpec(memory_space=pltpu.VMEM)
smem = pl.BlockSpec(memory_space=pltpu.SMEM)
hbm = pl.BlockSpec(memory_space=pltpu.HBM)
params = pltpu.CompilerParams(vmem_limit_bytes=24 * 2**20)


def cost(flops, moved, transcendentals=0):
    return pl.CostEstimate(flops=flops, bytes_accessed=moved, transcendentals=transcendentals)


def shift(axis, by):
    n = lax.axis_size(axis)
    return [(i, (i + by) % n) for i in range(n)]


def exchanged(copies, axis):
    return lax.all_to_all(copies, axis, 0, 0, tiled=True)


def embed_kernel(feats, proj, unit_out, inv_out, rows_out, acc):
    step = pl.program_id(0)

    @pl.when(step == 0)
    def _():
        acc[...] = jnp.zeros_like(acc)

    acc[...] += jnp.dot(feats[...], proj[...], preferred_element_type=f32)

    @pl.when(step == pl.num_programs(0) - 1)
    def _():
        emb = acc[...]
        inv = lax.rsqrt(jnp.sum(emb * emb, axis=1, keepdims=True) + eps)
        unit = emb * inv
        unit_out[...] = unit
        inv_out[...] = jnp.broadcast_to(inv, inv_out.shape)
        rows_out[...] = unit.astype(bf16)


def embed(feats, proj):
    own, depth = feats.shape
    width = proj.shape[1]
    cut = 512
    whole = lambda shape: pl.BlockSpec(shape, lambda k: (0, 0))
    return pl.pallas_call(
        embed_kernel,
        grid=(depth // cut,),
        out_shape=[
            jax.ShapeDtypeStruct((own, width), f32),
            jax.ShapeDtypeStruct((own, 128), f32),
            jax.ShapeDtypeStruct((own, width), bf16),
        ],
        in_specs=[
            pl.BlockSpec((own, cut), lambda k: (0, k)),
            pl.BlockSpec((cut, width), lambda k: (k, 0)),
        ],
        out_specs=[whole((own, width)), whole((own, 128)), whole((own, width))],
        scratch_shapes=[pltpu.VMEM((own, width), f32)],
        cost_estimate=cost(2 * own * depth * width, 2 * depth * width),
        compiler_params=params,
    )(feats, proj)


def repeat_kernel(rows, out, sems):
    copies = [pltpu.make_async_copy(rows, out.at[k], sems.at[k]) for k in range(out.shape[0])]
    for copy in copies:
        copy.start()
    for copy in copies:
        copy.wait()


def repeated(rows, n):
    return pl.pallas_call(
        repeat_kernel,
        out_shape=jax.ShapeDtypeStruct((n,) + rows.shape, rows.dtype),
        in_specs=[vmem],
        out_specs=hbm,
        scratch_shapes=[pltpu.SemaphoreType.DMA((n,))],
        cost_estimate=cost(0, 4 * n * rows.size),
    )(rows)


def text_kernel(own, place, scalars, near, far, txt, txt_out, coef_out, img, buf, sems):
    temp = scalars[0]
    bias = scalars[1]
    factor = scalars[2]
    half = near.shape[0]
    img[:half] = near[...]
    img[half:] = far[...]
    rows = img[...]
    n = txt_out.shape[0]
    copies = []
    for q in range(n):
        size = txt_out.shape[1]
        part = slice(q * size, (q + 1) * size)
        logits = (
            lax.dot_general(
                txt[part], rows, (((1,), (1,)), ((), ())), preferred_element_type=f32
            )
            * temp
            + bias
        )
        txt_ids = lax.broadcasted_iota(jnp.int32, logits.shape, 0) + (q * size - place[0])
        img_ids = lax.broadcasted_iota(jnp.int32, logits.shape, 1)
        diag = ((txt_ids == img_ids) & (img_ids < own)).astype(f32)
        coef = (factor * (jax.nn.sigmoid(logits) - diag)).astype(bf16)
        coef_out[part] = coef
        buf[q] = jnp.dot(coef, rows, preferred_element_type=f32).astype(bf16)
        copies.append(pltpu.make_async_copy(buf.at[q], txt_out.at[q], sems.at[q]))
        copies[-1].start()
    for copy in copies:
        copy.wait()


def text_terms(own, place, scalars, near, far, txt, n):
    m, w = txt.shape
    i = 2 * near.shape[0]
    return pl.pallas_call(
        functools.partial(text_kernel, own),
        out_shape=[
            jax.ShapeDtypeStruct((n, m // n, w), bf16),
            jax.ShapeDtypeStruct((m, i), bf16),
        ],
        in_specs=[smem, smem, vmem, vmem, vmem],
        out_specs=[hbm, vmem],
        scratch_shapes=[
            pltpu.VMEM((i, w), bf16),
            pltpu.VMEM((n, m // n, w), bf16),
            pltpu.SemaphoreType.DMA((n,)),
        ],
        cost_estimate=cost(4 * i * m * w, 4 * (i + m) * w, i * m),
        compiler_params=params,
    )(place, scalars, near, far, txt)


def image_kernel(coef, txt, near_out, far_out):
    half = near_out.shape[0]
    terms = lax.dot_general(
        coef[...], txt[...], (((0,), (0,)), ((), ())), preferred_element_type=f32
    )
    near_out[...] = terms[:half]
    far_out[...] = terms[half:].astype(bf16)


def image_terms(coef, txt):
    m, i = coef.shape
    w = txt.shape[1]
    return pl.pallas_call(
        image_kernel,
        out_shape=[
            jax.ShapeDtypeStruct((i // 2, w), f32),
            jax.ShapeDtypeStruct((i // 2, w), bf16),
        ],
        in_specs=[vmem, vmem],
        out_specs=[vmem, vmem],
        cost_estimate=cost(2 * i * m * w, 4 * (i + m) * w),
        compiler_params=params,
    )(coef, txt)


def fold_kernel(parts, got, *outs):
    at = 0
    for out in outs:
        rows = slice(at, at + out.shape[0])
        out[...] = (parts[rows] + got[rows].astype(f32)).astype(out.dtype)
        at += out.shape[0]


def fold(parts, got, sends):
    n, w = parts.shape
    sizes = (n - sum(sends),) + tuple(sends)
    return pl.pallas_call(
        fold_kernel,
        out_shape=[
            jax.ShapeDtypeStruct((size, w), f32 if k == 0 else bf16)
            for k, size in enumerate(sizes)
        ],
        in_specs=[vmem, vmem],
        out_specs=[vmem] * len(sizes),
        cost_estimate=cost(n * w, 10 * n * w),
        compiler_params=params,
    )(parts, got)


def sum_kernel(parts, out, buf, sem):
    total = parts[0].astype(f32)
    for k in range(1, parts.shape[0]):
        total += parts[k].astype(f32)
    buf[...] = total.astype(bf16)
    copy = pltpu.make_async_copy(buf, out, sem)
    copy.start()
    copy.wait()


def summed(parts):
    n, m, w = parts.shape
    return pl.pallas_call(
        sum_kernel,
        out_shape=jax.ShapeDtypeStruct((m, w), bf16),
        in_specs=[vmem],
        out_specs=hbm,
        scratch_shapes=[pltpu.VMEM((m, w), bf16), pltpu.SemaphoreType.DMA],
        cost_estimate=cost(n * m * w, 2 * (n + 1) * m * w),
        compiler_params=params,
    )(parts)


def backprop_kernel(unit, inv, proj, *refs):
    *parts, out = refs
    total = 0.0
    for part in parts:
        if len(part.shape) == 2:
            total = total + part[...].astype(f32)
        else:
            for k in range(part.shape[0]):
                total = total + part[k].astype(f32)
    rows = unit[...]
    along = jnp.sum(rows * total, axis=1, keepdims=True)
    delta = (inv[:, :1] * (total - rows * along)).astype(bf16)
    out[...] = lax.dot_general(
        delta, proj[...], (((1,), (1,)), ((), ())), preferred_element_type=f32
    )


def backprop(unit, inv, proj, *parts):
    depth, width = proj.shape
    own = unit.shape[0]
    return pl.pallas_call(
        backprop_kernel,
        out_shape=jax.ShapeDtypeStruct((own, depth), f32),
        in_specs=[vmem] * (3 + len(parts)),
        out_specs=vmem,
        cost_estimate=cost(2 * own * depth * width, 2 * depth * width),
        compiler_params=params,
    )(unit, inv, proj, *parts)


def shards(image_feats, text_feats, image_proj, text_proj, log_temp, logit_bias):
    own = text_feats.shape[0]
    total = own * lax.axis_size(("y", "x", "core", "z"))
    nx, ny = lax.axis_size("x"), lax.axis_size("y")
    send = lambda rows, axis, by: lax.ppermute(rows, axis, shift(axis, by))

    txt_unit, txt_inv, txt_own = embed(text_feats, text_proj)
    img_unit, img_inv, img_own = embed(image_feats, image_proj)
    txt_rows = exchanged(jnp.broadcast_to(txt_own[None], (ny,) + txt_own.shape), "y")
    img_rows = jnp.concatenate([img_own, send(img_own, "z", -4), send(img_own, "z", -8)])
    img_rows, txt_rows = lax.optimization_barrier((img_rows, txt_rows))
    txt_rows = exchanged(repeated(txt_rows.reshape(ny * own, -1), nx), "x")
    txt_rows = txt_rows.reshape(nx * ny * own, -1)
    for by in (2, 1):
        img_rows = jnp.concatenate([img_rows, send(img_rows, "z", -by)])
    img_far = send(img_rows, "core", 1)

    temp = jnp.exp(log_temp[0])
    scalars = jnp.stack([temp, logit_bias[0], loss_scale / total * temp])
    place = jnp.reshape(own * lax.axis_index(("x", "y")), (1,))
    txt_terms, coef = text_terms(own, place, scalars, img_rows, img_far, txt_rows, nx)
    txt_terms = exchanged(txt_terms, "x")
    near, far = image_terms(coef, txt_rows)
    near, away = fold(near, send(far, "core", 1), (6 * own,))
    near, away = fold(near, send(away, "z", 1), (3 * own,))
    near, away4, away8 = fold(near, send(away, "z", 2), (own, own))
    txt_terms, near, away4, away8 = lax.optimization_barrier((txt_terms, near, away4, away8))
    txt_terms = exchanged(summed(txt_terms).reshape(ny, own, -1), "y")
    image_grad = backprop(
        img_unit, img_inv, image_proj, near, send(away4, "z", 4), send(away8, "z", 8)
    )
    text_grad = backprop(txt_unit, txt_inv, text_proj, txt_terms)
    return (image_grad, text_grad)


def solution(mesh):
    blk, grp = mesh.devices.shape
    fine = Mesh(np.asarray(mesh.devices).reshape(blk // 8, 4, 2, grp), ("y", "x", "core", "z"))
    rows = P(("y", "x", "core", "z"), None)
    return jax.shard_map(
        shards,
        mesh=fine,
        in_specs=(rows, rows, P(), P(), P(), P()),
        out_specs=(rows, rows),
        check_vma=False,
    )
```

time: 162 us -> 134 us (0.83)
  the two profiles are of different devices: /device:TPU:64 before, /device:TPU:6 now
where the time goes in v3:
time: 134 us; the launch traced here: 132 us
  starting transfers between devices  68.4 us (51%)
  waiting for transfers between devices  34.2 us (26%)
  Pallas kernels  13.8 us (10%)
  local copies, waits for them, and re-layouts  13.3 us (10%)
  between operations  2.22 us (2%)
    ppermute x10, starting transfers between devices, shards(): send = lambda rows, axis, by: lax.ppermute(rows, axis, shift(axis, by))  44.1 us
    ppermute x10, waiting for transfers between devices, shards(): send = lambda rows, axis, by: lax.ppermute(rows, axis, shift(axis, by))  33.9 us
    all_to_all x4, starting transfers between devices, exchanged(): return lax.all_to_all(copies, axis, 0, 0, tiled=True)  24.3 us
    unnamed x34, local copies, waits for them, and re-layouts  12.6 us
    pallas_call x2, Pallas kernels, backprop(): pl.pallas_call(backprop_kernel, out_shape=jax.ShapeDtypeStruct((own, dept...  4.08 us
    pallas_call x1, Pallas kernels, text_terms(): pl.pallas_call(functools.partial(text_kernel, own), out_shape=[jax.ShapeD...  3.76 us
  transfers between devices with their start and end apart: 14, of which 10 were waited for; matrix products, arithmetic and copies ran while one was open for 0% of the time, Pallas kernels for 4%

profile of v3, /device:TPU:6, one launch (start us, length us, event | category | flops | bytes accessed | tf_op | source)
XLA Modules:
  0.0 132.1 jit_solution(7218888136564056001)
XLA Ops:
  0.6 1.7 %copy-done.2 = bf16[1024,1152]{1,0:T(8,128)(2,1)S(1)} copy-done((bf16[1024,1152]{1,0:T(8,128)(2,1)S(1)}, bf16[1024,1152]{1,0:T(8,128)(2,1)}, u32[]{:S(2)}) %copy-start.2) | copy-done | bytes 2359320
  2.3 0.8 copy-done.12
  3.1 0.7 shard_map.78
  3.7 0.6 copy-done.5
  4.4 0.7 broadcast_in_dim.2
  5.1 7.1 %all-to-all-start = ((bf16[8,16,1152]{2,1,0:T(8,128)(2,1)}), bf16[8,16,1152]{2,1,0:T(8,128)(2,1)S(1)}, u32[]{:S(2)}, u32[]{:S(2)}) async-start(bf16[8,16,1152]{2,1,0:T(8,128)(2,1)} %broadcast_in_dim.2), calls=%async_computation | async-start | bytes 589824 | tf_op jit(solution)/shard_map/all_to_all | solution.py:33
  12.2 2.0 %copy-done = bf16[1536,1152]{1,0:T(8,128)(2,1)S(1)} copy-done((bf16[1536,1152]{1,0:T(8,128)(2,1)S(1)}, bf16[1536,1152]{1,0:T(8,128)(2,1)}, u32[]{:S(2)}) %copy-start) | copy-done | bytes 3538968
  14.2 0.9 shard_map.77
  15.2 0.6 copy-done.7
  15.8 10.9 %collective-permute-start.1 = (bf16[16,1152]{1,0:T(8,128)(2,1)S(1)}, bf16[16,1152]{1,0:T(8,128)(2,1)S(1)}, u32[]{:S(2)}, u32[]{:S(2)}) collective-permute-start(bf16[16,1152]{1,0:T(8,128)(2,1)S(1)} %get-tuple-element.27), channel_id=1, source_target_pairs={{0,4},{1,5},{2,6},{3,7},{4,8},{5,9},{6,10},{7,11},{8,0},{9,1},{10,... | collective-permute-start | bytes 110600 | tf_op jit(solution)/shard_map/ppermute | solution.py:257
  26.7 5.6 %collective-permute-start = (bf16[16,1152]{1,0:T(8,128)(2,1)S(1)}, bf16[16,1152]{1,0:T(8,128)(2,1)S(1)}, u32[]{:S(2)}, u32[]{:S(2)}) collective-permute-start(bf16[16,1152]{1,0:T(8,128)(2,1)S(1)} %get-tuple-element.27), channel_id=1, source_target_pairs={{0,8},{1,9},{2,10},{3,11},{4,0},{5,1},{6,2},{7,3},{8,4},{9,5},{10,... | collective-permute-start | bytes 110600 | tf_op jit(solution)/shard_map/ppermute | solution.py:257
  32.3 0.1 collective-permute-done.1
  32.4 4.8 %collective-permute-done = bf16[16,1152]{1,0:T(8,128)(2,1)S(1)} collective-permute-done((bf16[16,1152]{1,0:T(8,128)(2,1)S(1)}, bf16[16,1152]{1,0:T(8,128)(2,1)S(1)}, u32[]{:S(2)}, u32[]{:S(2)}) %collective-permute-start) | collective-permute-done | bytes 36896 | tf_op jit(solution)/shard_map/ppermute | solution.py:257
  37.2 6.1 %collective-permute-start.2 = (bf16[48,1152]{1,0:T(8,128)(2,1)S(1)}, bf16[48,1152]{1,0:T(8,128)(2,1)S(1)}, u32[]{:S(2)}, u32[]{:S(2)}) collective-permute-start(bf16[48,1152]{1,0:T(8,128)(2,1)S(1)} %pad_maximum_fusion.1), channel_id=1, source_target_pairs={{0,10},{1,11},{2,0},{3,1},{4,2},{5,3},{6,4},{7,5},{8,6},{9,7},{10,... | collective-permute-start | bytes 331784 | tf_op jit(solution)/shard_map/ppermute | solution.py:257
  43.3 2.0 %shard_map.79 = bf16[4,128,1152]{2,1,0:T(8,128)(2,1)} custom-call(bf16[128,1152]{1,0:T(8,128)(2,1)} %bitcast.7), custom_call_target="tpu_custom_call" | custom-call | bytes 2359296 | tf_op jit(solution)/shard_map/pallas_call | solution.py:88
  45.4 4.8 %all-to-all-start.1 = ((bf16[4,128,1152]{2,1,0:T(8,128)(2,1)}), bf16[4,128,1152]{2,1,0:T(8,128)(2,1)S(1)}, u32[]{:S(2)}, u32[]{:S(2)}) async-start(bf16[4,128,1152]{2,1,0:T(8,128)(2,1)} %shard_map.79), calls=%async_computation.1 | async-start | bytes 2359296 | tf_op jit(solution)/shard_map/all_to_all | solution.py:33
  50.2 2.3 %collective-permute-start.3 = (bf16[96,1152]{1,0:T(8,128)(2,1)S(1)}, bf16[96,1152]{1,0:T(8,128)(2,1)S(1)}, u32[]{:S(2)}, u32[]{:S(2)}) collective-permute-start(bf16[96,1152]{1,0:T(8,128)(2,1)S(1)} %pad_maximum_fusion), channel_id=1, source_target_pairs={{0,11},{1,0},{2,1},{3,2},{4,3},{5,4},{6,5},{7,6},{8,7},{9,8},{10,9... | collective-permute-start | bytes 663560 | tf_op jit(solution)/shard_map/ppermute | solution.py:257
  52.5 5.5 %collective-permute-done.3 = bf16[96,1152]{1,0:T(8,128)(2,1)S(1)} collective-permute-done((bf16[96,1152]{1,0:T(8,128)(2,1)S(1)}, bf16[96,1152]{1,0:T(8,128)(2,1)S(1)}, u32[]{:S(2)}, u32[]{:S(2)}) %collective-permute-start.3) | collective-permute-done | bytes 221216 | tf_op jit(solution)/shard_map/ppermute | solution.py:257
  58.0 1.9 %collective-permute-start.4 = (bf16[192,1152]{1,0:T(8,128)(2,1)S(1)}, bf16[192,1152]{1,0:T(8,128)(2,1)S(1)}, u32[]{:S(2)}, u32[]{:S(2)}) collective-permute-start(bf16[192,1152]{1,0:T(8,128)(2,1)S(1)} %constant_dynamic-update-slice_fusion.near), channel_id=1, source_target_pairs={{0,12},{12,0},{1,13},{13,1},{2,14},{14,2},{3,15},{15,3},{4,16},{16... | collective-permute-start | bytes 1327112 | tf_op jit(solution)/shard_map/ppermute | solution.py:257
  61.3 0.1 pad_maximum_fusion.2.scalars
  61.4 0.3 collective-permute-done.4.far
  61.7 0.3 all-to-all-done.1
  62.0 3.8 %shard_map.80 = (bf16[4,128,1152]{2,1,0:T(8,128)(2,1)}, bf16[512,384]{1,0:T(8,128)(2,1)S(1)}) custom-call(s32[1]{0:T(128)} %bitcast.place, f32[3]{0:T(128)S(1)} %pad_maximum_fusion.2.scalars, bf16[192,1152]{1,0:T(8,128)(2,1)S(1)} %constant_dynamic-update-slice_fusion.near, bf16[192,1152]{1,0:T(8,128)(2,1)S(1)} %collective-permute-done.4.far, ...), custom_call_target="tpu_custom_call" | custom-call | flops 905969664 | bytes 4128768 | tf_op jit(solution)/shard_map/pallas_call | solution.py:133
  65.7 6.3 %all-to-all-start.2 = ((bf16[4,128,1152]{2,1,0:T(8,128)(2,1)}), bf16[4,128,1152]{2,1,0:T(8,128)(2,1)}, u32[]{:S(2)}, u32[]{:S(2)}) async-start(bf16[4,128,1152]{2,1,0:T(8,128)(2,1)} %get-tuple-element.31), calls=%async_computation.2 | async-start | bytes 2359296 | tf_op jit(solution)/shard_map/all_to_all | solution.py:33
  72.0 0.7 shard_map.81
  72.7 1.9 %collective-permute-start.5 = (bf16[192,1152]{1,0:T(8,128)(2,1)S(1)}, bf16[192,1152]{1,0:T(8,128)(2,1)S(1)}, u32[]{:S(2)}, u32[]{:S(2)}) collective-permute-start(bf16[192,1152]{1,0:T(8,128)(2,1)S(1)} %get-tuple-element.34), channel_id=1, source_target_pairs={{0,12},{12,0},{1,13},{13,1},{2,14},{14,2},{3,15},{15,3},{4,16},{16... | collective-permute-start | bytes 1327112 | tf_op jit(solution)/shard_map/ppermute | solution.py:257
  74.7 1.8 %collective-permute-done.5.got = bf16[192,1152]{1,0:T(8,128)(2,1)S(1)} collective-permute-done((bf16[192,1152]{1,0:T(8,128)(2,1)S(1)}, bf16[192,1152]{1,0:T(8,128)(2,1)S(1)}, u32[]{:S(2)}, u32[]{:S(2)}) %collective-permute-start.5) | collective-permute-done | bytes 442400 | tf_op jit(solution)/shard_map/ppermute | solution.py:257
  76.4 0.1 shard_map.82
  76.5 3.7 %collective-permute-start.6 = (bf16[96,1152]{1,0:T(8,128)(2,1)S(1)}, bf16[96,1152]{1,0:T(8,128)(2,1)S(1)}, u32[]{:S(2)}, u32[]{:S(2)}) collective-permute-start(bf16[96,1152]{1,0:T(8,128)(2,1)S(1)} %get-tuple-element.36), channel_id=1, source_target_pairs={{0,1},{1,2},{2,3},{3,4},{4,5},{5,6},{6,7},{7,8},{8,9},{9,10},{10,1... | collective-permute-start | bytes 663560 | tf_op jit(solution)/shard_map/ppermute | solution.py:257
  80.2 7.1 %collective-permute-done.6.got = bf16[96,1152]{1,0:T(8,128)(2,1)S(1)} collective-permute-done((bf16[96,1152]{1,0:T(8,128)(2,1)S(1)}, bf16[96,1152]{1,0:T(8,128)(2,1)S(1)}, u32[]{:S(2)}, u32[]{:S(2)}) %collective-permute-start.6) | collective-permute-done | bytes 221216 | tf_op jit(solution)/shard_map/ppermute | solution.py:257
  87.4 2.0 %collective-permute-start.7 = (bf16[48,1152]{1,0:T(8,128)(2,1)S(1)}, bf16[48,1152]{1,0:T(8,128)(2,1)S(1)}, u32[]{:S(2)}, u32[]{:S(2)}) collective-permute-start(bf16[48,1152]{1,0:T(8,128)(2,1)S(1)} %get-tuple-element.38), channel_id=1, source_target_pairs={{0,2},{1,3},{2,4},{3,5},{4,6},{5,7},{6,8},{7,9},{8,10},{9,11},{10,... | collective-permute-start | bytes 331784 | tf_op jit(solution)/shard_map/ppermute | solution.py:257
  89.4 8.7 %collective-permute-done.7.got = bf16[48,1152]{1,0:T(8,128)(2,1)S(1)} collective-permute-done((bf16[48,1152]{1,0:T(8,128)(2,1)S(1)}, bf16[48,1152]{1,0:T(8,128)(2,1)S(1)}, u32[]{:S(2)}, u32[]{:S(2)}) %collective-permute-start.7) | collective-permute-done | bytes 110624 | tf_op jit(solution)/shard_map/ppermute | solution.py:257
  98.1 0.6 copy-done.9
  98.7 0.6 copy-done.13
  99.3 0.6 copy-done.14
  100.0 1.5 %shard_map.86 = bf16[128,1152]{1,0:T(8,128)(2,1)S(1)} custom-call(bf16[4,128,1152]{2,1,0:T(8,128)(2,1)} %all-to-all-done.2.parts), custom_call_target="tpu_custom_call" | custom-call | flops 589824 | bytes 1474560 | tf_op jit(solution)/shard_map/pallas_call | solution.py:212
  101.5 0.7 copy-done.4
  102.2 6.1 %all-to-all-start.3 = ((bf16[8,16,1152]{2,1,0:T(8,128)(2,1)}), bf16[8,16,1152]{2,1,0:T(8,128)(2,1)}, u32[]{:S(2)}, u32[]{:S(2)}) async-start(bf16[8,16,1152]{2,1,0:T(8,128)(2,1)} %bitcast.6), calls=%async_computation.3 | async-start | bytes 589824 | tf_op jit(solution)/shard_map/all_to_all | solution.py:33
  108.3 5.5 %collective-permute-start.8 = (bf16[16,1152]{1,0:T(8,128)(2,1)}, bf16[16,1152]{1,0:T(8,128)(2,1)S(1)}, u32[]{:S(2)}, u32[]{:S(2)}) collective-permute-start(bf16[16,1152]{1,0:T(8,128)(2,1)} %copy-done.14), channel_id=1, source_target_pairs={{0,4},{1,5},{2,6},{3,7},{4,8},{5,9},{6,10},{7,11},{8,0},{9,1},{10,... | collective-permute-start | bytes 110600 | tf_op jit(solution)/shard_map/ppermute | solution.py:257
  113.7 4.3 %collective-permute-start.9 = (bf16[16,1152]{1,0:T(8,128)(2,1)}, bf16[16,1152]{1,0:T(8,128)(2,1)S(1)}, u32[]{:S(2)}, u32[]{:S(2)}) collective-permute-start(bf16[16,1152]{1,0:T(8,128)(2,1)} %copy-done.13), channel_id=1, source_target_pairs={{0,8},{1,9},{2,10},{3,11},{4,0},{5,1},{6,2},{7,3},{8,4},{9,5},{10,... | collective-permute-start | bytes 110600 | tf_op jit(solution)/shard_map/ppermute | solution.py:257
  118.0 0.6 collective-permute-done.8.refs_1_
  118.6 5.1 %collective-permute-done.9.refs_2_ = bf16[16,1152]{1,0:T(8,128)(2,1)S(1)} collective-permute-done((bf16[16,1152]{1,0:T(8,128)(2,1)}, bf16[16,1152]{1,0:T(8,128)(2,1)S(1)}, u32[]{:S(2)}, u32[]{:S(2)}) %collective-permute-start.9) | collective-permute-done | bytes 36896 | tf_op jit(solution)/shard_map/ppermute | solution.py:257
  123.7 0.9 copy-done.8
  124.6 0.9 copy-done.10
  125.5 1.7 %shard_map.85 = f32[16,1536]{1,0:T(8,128)} custom-call(f32[16,1152]{1,0:T(8,128)S(1)} %copy-done.8, f32[16,128]{1,0:T(8,128)S(1)} %get-tuple-element.26.inv, bf16[1536,1152]{1,0:T(8,128)(2,1)S(1)} %copy-done.1, f32[16,1152]{1,0:T(8,128)S(1)} %copy-done.10, bf16[16,1152]{1,0:T(8,128)(2,1)S(1)} %collective-permute-done.8.refs_1_, ...), custom_call_target="tpu_custom_call" | custom-call | flops 56623104 | bytes 3538944 | tf_op jit(solution)/shard_map/pallas_call | solution.py:243
  127.2 1.7 %copy-done.3 = bf16[1024,1152]{1,0:T(8,128)(2,1)S(1)} copy-done((bf16[1024,1152]{1,0:T(8,128)(2,1)S(1)}, bf16[1024,1152]{1,0:T(8,128)(2,1)}, u32[]{:S(2)}) %copy-start.3) | copy-done | bytes 2359320
  128.8 0.9 copy-done.6
  129.7 2.4 %shard_map.87 = f32[16,1024]{1,0:T(8,128)} custom-call(f32[16,1152]{1,0:T(8,128)S(1)} %copy-done.6, f32[16,128]{1,0:T(8,128)S(1)} %get-tuple-element.46.inv, bf16[1024,1152]{1,0:T(8,128)(2,1)S(1)} %copy-done.3, bf16[8,16,1152]{2,1,0:T(8,128)(2,1)} %all-to-all-done.3.refs_0_), custom_call_target="tpu_custom_call" | custom-call | flops 37748736 | bytes 2359296 | tf_op jit(solution)/shard_map/pallas_call | solution.py:243
  (30 shorter events, 0.2 us)
Async XLA Ops:
  0.6 1.7 %copy-start.2 = (bf16[1024,1152]{1,0:T(8,128)(2,1)S(1)}, bf16[1024,1152]{1,0:T(8,128)(2,1)}, u32[]{:S(2)}) copy-start(bf16[1024,1152]{1,0:T(8,128)(2,1)} %proj.7) | copy-start | bytes 7077892
  2.3 0.8 copy-start.12
  3.1 9.1 %copy-start.11 = (bf16[16,1536]{1,0:T(8,128)(2,1)S(1)}, bf16[16,1536]{1,0:T(8,128)(2,1)}, u32[]{:S(2)}) copy-start(bf16[16,1536]{1,0:T(8,128)(2,1)} %feats.2) | copy-start | bytes 147460
  3.7 0.6 copy-start.5
  5.1 32.1 %all-to-all-start = ((bf16[8,16,1152]{2,1,0:T(8,128)(2,1)}), bf16[8,16,1152]{2,1,0:T(8,128)(2,1)S(1)}, u32[]{:S(2)}, u32[]{:S(2)}) async-start(bf16[8,16,1152]{2,1,0:T(8,128)(2,1)} %broadcast_in_dim.2), calls=%async_computation | async-start | bytes 589824 | tf_op jit(solution)/shard_map/all_to_all | solution.py:33
  12.2 2.0 %copy-start = (bf16[1536,1152]{1,0:T(8,128)(2,1)S(1)}, bf16[1536,1152]{1,0:T(8,128)(2,1)}, u32[]{:S(2)}) copy-start(bf16[1536,1152]{1,0:T(8,128)(2,1)} %proj.6) | copy-start | bytes 10616836
  15.2 0.6 copy-start.7
  15.8 16.6 %collective-permute-start.1 = (bf16[16,1152]{1,0:T(8,128)(2,1)S(1)}, bf16[16,1152]{1,0:T(8,128)(2,1)S(1)}, u32[]{:S(2)}, u32[]{:S(2)}) collective-permute-start(bf16[16,1152]{1,0:T(8,128)(2,1)S(1)} %get-tuple-element.27), channel_id=1, source_target_pairs={{0,4},{1,5},{2,6},{3,7},{4,8},{5,9},{6,10},{7,11},{8,0},{9,1},{10,... | collective-permute-start | bytes 110600 | tf_op jit(solution)/shard_map/ppermute | solution.py:257
  26.7 10.5 %collective-permute-start = (bf16[16,1152]{1,0:T(8,128)(2,1)S(1)}, bf16[16,1152]{1,0:T(8,128)(2,1)S(1)}, u32[]{:S(2)}, u32[]{:S(2)}) collective-permute-start(bf16[16,1152]{1,0:T(8,128)(2,1)S(1)} %get-tuple-element.27), channel_id=1, source_target_pairs={{0,8},{1,9},{2,10},{3,11},{4,0},{5,1},{6,2},{7,3},{8,4},{9,5},{10,... | collective-permute-start | bytes 110600 | tf_op jit(solution)/shard_map/ppermute | solution.py:257
  37.2 6.1 %copy-start.15 = (bf16[8,16,1152]{2,1,0:T(8,128)(2,1)}, bf16[8,16,1152]{2,1,0:T(8,128)(2,1)S(1)}, u32[]{:S(2)}) copy-start(bf16[8,16,1152]{2,1,0:T(8,128)(2,1)S(1)} %all-to-all-done) | copy-start | bytes 884740
  37.2 12.9 %collective-permute-start.2 = (bf16[48,1152]{1,0:T(8,128)(2,1)S(1)}, bf16[48,1152]{1,0:T(8,128)(2,1)S(1)}, u32[]{:S(2)}, u32[]{:S(2)}) collective-permute-start(bf16[48,1152]{1,0:T(8,128)(2,1)S(1)} %pad_maximum_fusion.1), channel_id=1, source_target_pairs={{0,10},{1,11},{2,0},{3,1},{4,2},{5,3},{6,4},{7,5},{8,6},{9,7},{10,... | collective-permute-start | bytes 331784 | tf_op jit(solution)/shard_map/ppermute | solution.py:257
  45.4 16.6 %all-to-all-start.1 = ((bf16[4,128,1152]{2,1,0:T(8,128)(2,1)}), bf16[4,128,1152]{2,1,0:T(8,128)(2,1)S(1)}, u32[]{:S(2)}, u32[]{:S(2)}) async-start(bf16[4,128,1152]{2,1,0:T(8,128)(2,1)} %shard_map.79), calls=%async_computation.1 | async-start | bytes 2359296 | tf_op jit(solution)/shard_map/all_to_all | solution.py:33
  50.2 7.8 %collective-permute-start.3 = (bf16[96,1152]{1,0:T(8,128)(2,1)S(1)}, bf16[96,1152]{1,0:T(8,128)(2,1)S(1)}, u32[]{:S(2)}, u32[]{:S(2)}) collective-permute-start(bf16[96,1152]{1,0:T(8,128)(2,1)S(1)} %pad_maximum_fusion), channel_id=1, source_target_pairs={{0,11},{1,0},{2,1},{3,2},{4,3},{5,4},{6,5},{7,6},{8,7},{9,8},{10,9... | collective-permute-start | bytes 663560 | tf_op jit(solution)/shard_map/ppermute | solution.py:257
  58.0 3.7 %collective-permute-start.4 = (bf16[192,1152]{1,0:T(8,128)(2,1)S(1)}, bf16[192,1152]{1,0:T(8,128)(2,1)S(1)}, u32[]{:S(2)}, u32[]{:S(2)}) collective-permute-start(bf16[192,1152]{1,0:T(8,128)(2,1)S(1)} %constant_dynamic-update-slice_fusion.near), channel_id=1, source_target_pairs={{0,12},{12,0},{1,13},{13,1},{2,14},{14,2},{3,15},{15,3},{4,16},{16... | collective-permute-start | bytes 1327112 | tf_op jit(solution)/shard_map/ppermute | solution.py:257
  65.7 34.2 %all-to-all-start.2 = ((bf16[4,128,1152]{2,1,0:T(8,128)(2,1)}), bf16[4,128,1152]{2,1,0:T(8,128)(2,1)}, u32[]{:S(2)}, u32[]{:S(2)}) async-start(bf16[4,128,1152]{2,1,0:T(8,128)(2,1)} %get-tuple-element.31), calls=%async_computation.2 | async-start | bytes 2359296 | tf_op jit(solution)/shard_map/all_to_all | solution.py:33
  72.7 3.7 %collective-permute-start.5 = (bf16[192,1152]{1,0:T(8,128)(2,1)S(1)}, bf16[192,1152]{1,0:T(8,128)(2,1)S(1)}, u32[]{:S(2)}, u32[]{:S(2)}) collective-permute-start(bf16[192,1152]{1,0:T(8,128)(2,1)S(1)} %get-tuple-element.34), channel_id=1, source_target_pairs={{0,12},{12,0},{1,13},{13,1},{2,14},{14,2},{3,15},{15,3},{4,16},{16... | collective-permute-start | bytes 1327112 | tf_op jit(solution)/shard_map/ppermute | solution.py:257
  76.4 47.3 %copy-start.1 = (bf16[1536,1152]{1,0:T(8,128)(2,1)S(1)}, bf16[1536,1152]{1,0:T(8,128)(2,1)}, u32[]{:S(2)}) copy-start(bf16[1536,1152]{1,0:T(8,128)(2,1)} %proj.6) | copy-start | bytes 10616836
  76.5 10.8 %collective-permute-start.6 = (bf16[96,1152]{1,0:T(8,128)(2,1)S(1)}, bf16[96,1152]{1,0:T(8,128)(2,1)S(1)}, u32[]{:S(2)}, u32[]{:S(2)}) collective-permute-start(bf16[96,1152]{1,0:T(8,128)(2,1)S(1)} %get-tuple-element.36), channel_id=1, source_target_pairs={{0,1},{1,2},{2,3},{3,4},{4,5},{5,6},{6,7},{7,8},{8,9},{9,10},{10,1... | collective-permute-start | bytes 663560 | tf_op jit(solution)/shard_map/ppermute | solution.py:257
  87.4 10.6 %collective-permute-start.7 = (bf16[48,1152]{1,0:T(8,128)(2,1)S(1)}, bf16[48,1152]{1,0:T(8,128)(2,1)S(1)}, u32[]{:S(2)}, u32[]{:S(2)}) collective-permute-start(bf16[48,1152]{1,0:T(8,128)(2,1)S(1)} %get-tuple-element.38), channel_id=1, source_target_pairs={{0,2},{1,3},{2,4},{3,5},{4,6},{5,7},{6,8},{7,9},{8,10},{9,11},{10,... | collective-permute-start | bytes 331784 | tf_op jit(solution)/shard_map/ppermute | solution.py:257
  98.1 0.6 copy-start.9
  98.7 0.6 copy-start.13
  99.3 0.6 copy-start.14
  101.4 0.7 copy-start.4
  102.2 25.0 %all-to-all-start.3 = ((bf16[8,16,1152]{2,1,0:T(8,128)(2,1)}), bf16[8,16,1152]{2,1,0:T(8,128)(2,1)}, u32[]{:S(2)}, u32[]{:S(2)}) async-start(bf16[8,16,1152]{2,1,0:T(8,128)(2,1)} %bitcast.6), calls=%async_computation.3 | async-start | bytes 589824 | tf_op jit(solution)/shard_map/all_to_all | solution.py:33
  108.3 10.4 %collective-permute-start.8 = (bf16[16,1152]{1,0:T(8,128)(2,1)}, bf16[16,1152]{1,0:T(8,128)(2,1)S(1)}, u32[]{:S(2)}, u32[]{:S(2)}) collective-permute-start(bf16[16,1152]{1,0:T(8,128)(2,1)} %copy-done.14), channel_id=1, source_target_pairs={{0,4},{1,5},{2,6},{3,7},{4,8},{5,9},{6,10},{7,11},{8,0},{9,1},{10,... | collective-permute-start | bytes 110600 | tf_op jit(solution)/shard_map/ppermute | solution.py:257
  113.7 10.0 %collective-permute-start.9 = (bf16[16,1152]{1,0:T(8,128)(2,1)}, bf16[16,1152]{1,0:T(8,128)(2,1)S(1)}, u32[]{:S(2)}, u32[]{:S(2)}) collective-permute-start(bf16[16,1152]{1,0:T(8,128)(2,1)} %copy-done.13), channel_id=1, source_target_pairs={{0,8},{1,9},{2,10},{3,11},{4,0},{5,1},{6,2},{7,3},{8,4},{9,5},{10,... | collective-permute-start | bytes 110600 | tf_op jit(solution)/shard_map/ppermute | solution.py:257
  123.7 0.9 copy-start.8
  124.6 0.9 copy-start.10
  127.2 1.7 %copy-start.3 = (bf16[1024,1152]{1,0:T(8,128)(2,1)S(1)}, bf16[1024,1152]{1,0:T(8,128)(2,1)}, u32[]{:S(2)}) copy-start(bf16[1024,1152]{1,0:T(8,128)(2,1)} %proj.7) | copy-start | bytes 7077892
  128.8 0.9 copy-start.6

commit v4 on v3

v4 whole, which is shorter than its diff:
```python
import functools

import jax
import jax.numpy as jnp
import numpy as np
from jax import lax
from jax.experimental import pallas as pl
from jax.experimental.pallas import tpu as pltpu
from jax.sharding import Mesh
from jax.sharding import PartitionSpec as P

loss_scale = 65536.0
eps = 1e-06
f32 = jnp.float32
bf16 = jnp.bfloat16

vmem = pl.BlockSpec(memory_space=pltpu.VMEM)
smem = pl.BlockSpec(memory_space=pltpu.SMEM)
hbm = pl.BlockSpec(memory_space=pltpu.HBM)
params = pltpu.CompilerParams(vmem_limit_bytes=24 * 2**20)

anywhere = pl.BlockSpec(memory_space=pl.ANY)

ahead = (0, 4, 8, 2, 6, 10, 1, 5, 9, 3, 7, 11)


def cost(flops, moved, transcendentals=0):
    return pl.CostEstimate(flops=flops, bytes_accessed=moved, transcendentals=transcendentals)


def shift(axis, by):
    n = lax.axis_size(axis)
    return [(i, (i + by) % n) for i in range(n)]


def exchanged(copies, axis):
    return lax.all_to_all(copies, axis, 0, 0, tiled=True)


def embed_kernel(feats, proj, unit_out, inv_out, rows_out, feats_buf, proj_buf, unit_buf, rows_buf, sems, out_sems):
    parts, cut = proj_buf.shape[:2]
    reads = [pltpu.make_async_copy(feats, feats_buf, sems.at[parts])]
    for k in range(parts):
        reads.append(pltpu.make_async_copy(proj.at[pl.ds(k * cut, cut)], proj_buf.at[k], sems.at[k]))
    for read in reads:
        read.start()
    reads[0].wait()
    emb = jnp.zeros(unit_buf.shape, f32)
    for k in range(parts):
        reads[k + 1].wait()
        emb += jnp.dot(
            feats_buf[:, k * cut : (k + 1) * cut], proj_buf[k], preferred_element_type=f32
        )
    inv = lax.rsqrt(jnp.sum(emb * emb, axis=1, keepdims=True) + eps)
    unit = emb * inv
    rows_buf[...] = unit.astype(bf16)
    n = rows_out.shape[0]
    writes = [pltpu.make_async_copy(rows_buf, rows_out.at[k], out_sems.at[k]) for k in range(n)]
    for write in writes:
        write.start()
    unit_buf[...] = unit
    writes.append(pltpu.make_async_copy(unit_buf, unit_out, out_sems.at[n]))
    writes[-1].start()
    inv_out[...] = jnp.broadcast_to(inv, inv_out.shape)
    for write in writes:
        write.wait()


def embed(feats, proj, n):
    own, depth = feats.shape
    width = proj.shape[1]
    cut = 256
    return pl.pallas_call(
        embed_kernel,
        out_shape=[
            jax.ShapeDtypeStruct((own, width), f32),
            jax.ShapeDtypeStruct((own, 128), f32),
            jax.ShapeDtypeStruct((n, own, width), bf16),
        ],
        in_specs=[anywhere, anywhere],
        out_specs=[hbm, vmem, hbm],
        scratch_shapes=[
            pltpu.VMEM((own, depth), bf16),
            pltpu.VMEM((depth // cut, cut, width), bf16),
            pltpu.VMEM((own, width), f32),
            pltpu.VMEM((own, width), bf16),
            pltpu.SemaphoreType.DMA((depth // cut + 1,)),
            pltpu.SemaphoreType.DMA((n + 1,)),
        ],
        cost_estimate=cost(2 * own * depth * width, 2 * depth * width),
        compiler_params=params,
    )(feats, proj)


def text_kernel(own, place, scalars, img, txt, txt_out, coef_out, buf, sems):
    temp = scalars[0]
    bias = scalars[1]
    factor = scalars[2]
    rows = img[...]
    parts, size = buf.shape[:2]
    copies = []
    for q in range(parts):
        part = slice(q * size, (q + 1) * size)
        logits = (
            lax.dot_general(
                txt[part], rows, (((1,), (1,)), ((), ())), preferred_element_type=f32
            )
            * temp
            + bias
        )
        txt_ids = lax.broadcasted_iota(jnp.int32, logits.shape, 0) + (q * size - place[0])
        img_ids = lax.broadcasted_iota(jnp.int32, logits.shape, 1) - place[1]
        diag = ((txt_ids == img_ids) & (img_ids >= 0) & (img_ids < own)).astype(f32)
        coef = (factor * (jax.nn.sigmoid(logits) - diag)).astype(bf16)
        coef_out[part] = coef
        buf[q] = jnp.dot(coef, rows, preferred_element_type=f32).astype(bf16)
        copies.append(
            pltpu.make_async_copy(buf.at[q], txt_out.at[pl.ds(q * size, size)], sems.at[q])
        )
        copies[-1].start()
    for copy in copies:
        copy.wait()


def text_terms(own, place, scalars, img, txt):
    m, w = txt.shape
    i = img.shape[0]
    parts = 4
    return pl.pallas_call(
        functools.partial(text_kernel, own),
        out_shape=[jax.ShapeDtypeStruct((m, w), bf16), jax.ShapeDtypeStruct((m, i), bf16)],
        in_specs=[smem, smem, vmem, vmem],
        out_specs=[hbm, vmem],
        scratch_shapes=[
            pltpu.VMEM((parts, m // parts, w), bf16),
            pltpu.SemaphoreType.DMA((parts,)),
        ],
        cost_estimate=cost(4 * i * m * w, 4 * (i + m) * w, i * m),
        compiler_params=params,
    )(place, scalars, img, txt)


def image_kernel(own, place, coef, txt, near_out, far_out, terms):
    nz = len(ahead)
    half = nz * own
    terms[...] = lax.dot_general(
        coef[...], txt[...], (((0,), (0,)), ((), ())), preferred_element_type=f32
    )
    core = place[2]
    z = place[3]
    for k, by in enumerate(ahead):
        owner = lax.rem(z + by, nz) * own
        near = pl.multiple_of(core * half + owner, own)
        far = pl.multiple_of((1 - core) * half + owner, own)
        near_out[pl.ds(k * own, own)] = terms[pl.ds(near, own)]
        far_out[pl.ds(k * own, own)] = terms[pl.ds(far, own)].astype(bf16)


def image_terms(own, place, coef, txt):
    m, i = coef.shape
    w = txt.shape[1]
    return pl.pallas_call(
        functools.partial(image_kernel, own),
        out_shape=[
            jax.ShapeDtypeStruct((i // 2, w), f32),
            jax.ShapeDtypeStruct((i // 2, w), bf16),
        ],
        in_specs=[smem, vmem, vmem],
        out_specs=[vmem, vmem],
        scratch_shapes=[pltpu.VMEM((i, w), f32)],
        cost_estimate=cost(2 * i * m * w, 4 * (i + m) * w),
        compiler_params=params,
    )(place, coef, txt)


def fold_kernel(parts, got, *outs):
    at = 0
    for out in outs:
        rows = slice(at, at + out.shape[0])
        out[...] = (parts[rows] + got[rows].astype(f32)).astype(out.dtype)
        at += out.shape[0]


def fold(parts, got, sends):
    n, w = parts.shape
    sizes = (n - sum(sends),) + tuple(sends)
    return pl.pallas_call(
        fold_kernel,
        out_shape=[
            jax.ShapeDtypeStruct((size, w), f32 if k == 0 else bf16)
            for k, size in enumerate(sizes)
        ],
        in_specs=[vmem, vmem],
        out_specs=[vmem] * len(sizes),
        cost_estimate=cost(n * w, 10 * n * w),
        compiler_params=params,
    )(parts, got)


def backprop_kernel(unit, inv, proj, *refs):
    *parts, out, unit_buf, proj_buf, sems = refs
    reads = [
        pltpu.make_async_copy(unit, unit_buf, sems.at[0]),
        pltpu.make_async_copy(proj, proj_buf, sems.at[1]),
    ]
    for read in reads:
        read.start()
    total = 0.0
    for part in parts:
        if len(part.shape) == 2:
            total = total + part[...].astype(f32)
        else:
            for k in range(part.shape[0]):
                total = total + part[k].astype(f32)
    reads[0].wait()
    rows = unit_buf[...]
    along = jnp.sum(rows * total, axis=1, keepdims=True)
    delta = (inv[:, :1] * (total - rows * along)).astype(bf16)
    reads[1].wait()
    out[...] = lax.dot_general(
        delta, proj_buf[...], (((1,), (1,)), ((), ())), preferred_element_type=f32
    )


def backprop(unit, inv, proj, *parts):
    depth, width = proj.shape
    own = unit.shape[0]
    return pl.pallas_call(
        backprop_kernel,
        out_shape=jax.ShapeDtypeStruct((own, depth), f32),
        in_specs=[anywhere, vmem, anywhere] + [vmem] * len(parts),
        out_specs=vmem,
        scratch_shapes=[
            pltpu.VMEM(unit.shape, f32),
            pltpu.VMEM(proj.shape, bf16),
            pltpu.SemaphoreType.DMA((2,)),
        ],
        cost_estimate=cost(2 * own * depth * width, 2 * depth * width),
        compiler_params=params,
    )(unit, inv, proj, *parts)


def shards(image_feats, text_feats, image_proj, text_proj, log_temp, logit_bias):
    own = text_feats.shape[0]
    total = own * lax.axis_size(("y", "x", "core", "z"))
    send = lambda rows, axis, by: lax.ppermute(rows, axis, shift(axis, by))

    txt_unit, txt_inv, txt_rows = embed(text_feats, text_proj, lax.axis_size(("y", "x")))
    txt_rows = exchanged(txt_rows, ("y", "x")).reshape(-1, txt_rows.shape[2])
    img_unit, img_inv, img_rows = embed(image_feats, image_proj, 1)
    img_rows = lax.all_gather(img_rows[0], "z", tiled=True)
    img_rows = lax.all_gather(img_rows, "core", tiled=True)

    temp = jnp.exp(log_temp[0])
    scalars = jnp.stack([temp, logit_bias[0], loss_scale / total * temp])
    core, z = lax.axis_index("core"), lax.axis_index("z")
    place = jnp.stack(
        [own * lax.axis_index(("y", "x")), own * lax.axis_index(("core", "z")), core, z]
    )
    txt_terms, coef = text_terms(own, place, scalars, img_rows, txt_rows)
    txt_terms = exchanged(txt_terms.reshape(-1, own, txt_terms.shape[1]), ("y", "x"))
    near, far = image_terms(own, place, coef, txt_rows)
    near, away = fold(near, send(far, "core", 1), (6 * own,))
    near, away = fold(near, send(away, "z", 1), (3 * own,))
    near, away4, away8 = fold(near, send(away, "z", 2), (own, own))
    image_grad = backprop(
        img_unit, img_inv, image_proj, near, send(away4, "z", 4), send(away8, "z", 8)
    )
    text_grad = backprop(txt_unit, txt_inv, text_proj, txt_terms)
    return (image_grad, text_grad)


def solution(mesh):
    blk, grp = mesh.devices.shape
    fine = Mesh(np.asarray(mesh.devices).reshape(blk // 8, 4, 2, grp), ("y", "x", "core", "z"))
    rows = P(("y", "x", "core", "z"), None)
    return jax.shard_map(
        shards,
        mesh=fine,
        in_specs=(rows, rows, P(), P(), P(), P()),
        out_specs=(rows, rows),
        check_vma=False,
    )
```

time: 134 us -> 131 us (0.978)
  blocking collectives: 0 us -> 34 us
  starting transfers between devices: 68.4 us -> 39.2 us
  waiting for transfers between devices: 34.2 us -> 21.2 us
  Pallas kernels: 13.8 us -> 17.9 us
    all_gather x0 -> x2, blocking collectives: none -> 34 us  [the longest x1 31.4 us: shards(): img_rows = lax.all_gather(img_rows[0], 'z', tiled=True)]
    ppermute x10 -> x5, starting transfers between devices: 44.1 us -> 15.6 us  [shards(): send = lambda rows, axis, by: lax.ppermute(rows, axis, shift(axis, by))]
    ppermute x10 -> x5, waiting for transfers between devices: 33.9 us -> 21.2 us  [shards(): send = lambda rows, axis, by: lax.ppermute(rows, axis, shift(axis, by))]
    pallas_call x5 -> x3, Pallas kernels: 5.83 us -> 7.59 us  [the longest x2 5.49 us: embed(): pl.pallas_call(embed_kernel, out_shape=[jax.ShapeDtypeStruct((own, width)...]
    all_to_all x4 -> x2, starting transfers between devices: 24.3 us -> 23.6 us  [exchanged(): return lax.all_to_all(copies, axis, 0, 0, tiled=True)]
  transfers between devices with their start and end apart: 14 -> 7, of which waited for: 10 -> 4; matrix products, arithmetic and copies ran while one was open for 0% -> 1% of each run, Pallas kernels for 4% -> 5%
where the time goes in v4:
time: 131 us; the launch traced here: 130 us
  starting transfers between devices  39.2 us (30%)
  blocking collectives  34 us (26%)
  waiting for transfers between devices  21.2 us (16%)
  Pallas kernels  17.9 us (14%)
  local copies, waits for them, and re-layouts  13.9 us (11%)
  between operations  2.19 us (2%)
    all_gather x1, blocking collectives, shards(): img_rows = lax.all_gather(img_rows[0], 'z', tiled=True)  31.4 us
    all_to_all x2, starting transfers between devices, exchanged(): return lax.all_to_all(copies, axis, 0, 0, tiled=True)  23.6 us
    ppermute x5, waiting for transfers between devices, shards(): send = lambda rows, axis, by: lax.ppermute(rows, axis, shift(axis, by))  21.2 us
    ppermute x5, starting transfers between devices, shards(): send = lambda rows, axis, by: lax.ppermute(rows, axis, shift(axis, by))  15.6 us
    unnamed x34, local copies, waits for them, and re-layouts  13.9 us
    pallas_call x2, Pallas kernels, embed(): pl.pallas_call(embed_kernel, out_shape=[jax.ShapeDtypeStruct((own, width)...  5.49 us
    pallas_call x2, Pallas kernels, backprop(): pl.pallas_call(backprop_kernel, out_shape=jax.ShapeDtypeStruct((own, dept...  5.38 us
    pallas_call x1, Pallas kernels, text_terms(): pl.pallas_call(functools.partial(text_kernel, own), out_shape=[jax.ShapeD...  4.78 us
  transfers between devices with their start and end apart: 7, of which 4 were waited for; matrix products, arithmetic and copies ran while one was open for 1% of the time, Pallas kernels for 5%

profile of v4, /device:TPU:6, one launch (start us, length us, event | category | flops | bytes accessed | tf_op | source)
XLA Modules:
  0.0 129.7 jit_solution(11225872843951942766)
XLA Ops:
  0.6 0.0 copy-start.1
  0.6 1.7 %copy-done.1 = bf16[1024,1152]{1,0:T(8,128)(2,1)S(1)} copy-done((bf16[1024,1152]{1,0:T(8,128)(2,1)S(1)}, bf16[1024,1152]{1,0:T(8,128)(2,1)}, u32[]{:S(2)}) %copy-start.1) | copy-done | bytes 2359320
  2.3 0.8 copy-done.11
  3.1 3.3 %shard_map.78 = (f32[16,1152]{1,0:T(8,128)S(1)}, f32[16,128]{1,0:T(8,128)S(1)}, bf16[32,16,1152]{2,1,0:T(8,128)(2,1)S(1)}) custom-call(bf16[16,1024]{1,0:T(8,128)(2,1)S(1)} %copy-done.11, bf16[1024,1152]{1,0:T(8,128)(2,1)S(1)} %copy-done.1), custom_call_target="tpu_custom_call" | custom-call | flops 37748736 | bytes 2359296 | tf_op jit(solution)/shard_map/pallas_call | solution.py:73
  6.4 1.0 copy-done.4
  7.4 0.6 copy-done.6
  8.0 13.8 %all-to-all-start = ((bf16[32,16,1152]{2,1,0:T(8,128)(2,1)}), bf16[32,16,1152]{2,1,0:T(8,128)(2,1)}, u32[]{:S(2)}, u32[]{:S(2)}) async-start(bf16[32,16,1152]{2,1,0:T(8,128)(2,1)} %copy-done.4), calls=%async_computation | async-start | bytes 2359296 | tf_op jit(solution)/shard_map/all_to_all | solution.py:37
  23.2 0.0 copy-start.10
  23.2 0.8 copy-done.10
  24.0 2.2 %shard_map.77 = (f32[16,1152]{1,0:T(8,128)S(1)}, f32[16,128]{1,0:T(8,128)S(1)}, bf16[1,16,1152]{2,1,0:T(8,128)(2,1)S(1)}) custom-call(bf16[16,1536]{1,0:T(8,128)(2,1)S(1)} %copy-done.10, bf16[1536,1152]{1,0:T(8,128)(2,1)S(1)} %copy-done), custom_call_target="tpu_custom_call" | custom-call | flops 56623104 | bytes 3538944 | tf_op jit(solution)/shard_map/pallas_call | solution.py:73
  26.2 0.0 copy-start.8
  26.2 0.6 copy-done.8
  26.8 0.6 pad_maximum_fusion.scalars
  27.4 0.7 pad_add_fusion.place
  28.0 31.4 %all-gather = bf16[1,192,1152]{2,1,0:T(8,128)(2,1)S(1)} all-gather(bf16[1,16,1152]{2,1,0:T(8,128)(2,1)S(1)} %get-tuple-element.21), channel_id=2, replica_groups=mesh['y'=8,'x'=4,'core'=2,'z'=12] {'z'}, dimensions={1}, use_global_device_ids=true | all-gather | bytes 479232 | tf_op jit(solution)/shard_map/all_gather | solution.py:251
  59.5 2.6 %all-gather.1 = bf16[1,384,1152]{2,1,0:T(8,128)(2,1)} all-gather(bf16[1,192,1152]{2,1,0:T(8,128)(2,1)S(1)} %all-gather), channel_id=3, replica_groups=mesh['y'=8,'x'=4,'core'=2,'z'=12] {'core'}, dimensions={1}, use_global_device_ids=true | all-gather | bytes 1327104 | tf_op jit(solution)/shard_map/all_gather | solution.py:252
  62.0 0.0 all-to-all-done
  62.0 1.2 copy-done.5
  63.2 0.7 copy-done.12
  63.9 0.6 copy-done.14
  64.5 4.8 %shard_map.79 = (bf16[512,1152]{1,0:T(8,128)(2,1)S(1)}, bf16[512,384]{1,0:T(8,128)(2,1)S(1)}) custom-call(s32[4]{0:T(128)S(1)} %copy-done.12, f32[3]{0:T(128)S(1)} %copy-done.14, bf16[384,1152]{1,0:T(8,128)(2,1)S(1)} %bitcast.8, bf16[512,1152]{1,0:T(8,128)(2,1)} %bitcast.5.txt), custom_call_target="tpu_custom_call" | custom-call | flops 905969664 | bytes 4128768 | tf_op jit(solution)/shard_map/pallas_call | solution.py:129
  69.3 0.0 copy-start.3
  69.3 1.0 copy-done.3
  70.3 0.7 copy-done.15
  71.0 9.8 %all-to-all-start.1 = ((bf16[32,16,1152]{2,1,0:T(8,128)(2,1)}), bf16[32,16,1152]{2,1,0:T(8,128)(2,1)}, u32[]{:S(2)}, u32[]{:S(2)}) async-start(bf16[32,16,1152]{2,1,0:T(8,128)(2,1)} %bitcast.7), calls=%async_computation.1 | async-start | bytes 2359296 | tf_op jit(solution)/shard_map/all_to_all | solution.py:37
  80.9 0.0 copy-start.13
  80.9 0.7 copy-done.13
  81.5 1.0 copy-done.16
  82.5 2.1 %shard_map.80 = (f32[192,1152]{1,0:T(8,128)S(1)}, bf16[192,1152]{1,0:T(8,128)(2,1)S(1)}) custom-call(s32[4]{0:T(128)S(1)} %copy-done.13, bf16[512,384]{1,0:T(8,128)(2,1)S(1)} %copy-done.16, bf16[512,1152]{1,0:T(8,128)(2,1)} %bitcast.5.txt), custom_call_target="tpu_custom_call" | custom-call | flops 452984832 | bytes 4128768 | tf_op jit(solution)/shard_map/pallas_call | solution.py:162
  84.6 0.0 copy-start.9
  84.6 2.1 %collective-permute-start = (bf16[192,1152]{1,0:T(8,128)(2,1)S(1)}, bf16[192,1152]{1,0:T(8,128)(2,1)S(1)}, u32[]{:S(2)}, u32[]{:S(2)}) collective-permute-start(bf16[192,1152]{1,0:T(8,128)(2,1)S(1)} %get-tuple-element.25), channel_id=1, source_target_pairs={{0,12},{12,0},{1,13},{13,1},{2,14},{14,2},{3,15},{15,3},{4,16},{16... | collective-permute-start | bytes 1327112 | tf_op jit(solution)/shard_map/ppermute | solution.py:246
  86.7 1.8 %collective-permute-done.got = bf16[192,1152]{1,0:T(8,128)(2,1)S(1)} collective-permute-done((bf16[192,1152]{1,0:T(8,128)(2,1)S(1)}, bf16[192,1152]{1,0:T(8,128)(2,1)S(1)}, u32[]{:S(2)}, u32[]{:S(2)}) %collective-permute-start) | collective-permute-done | bytes 442400 | tf_op jit(solution)/shard_map/ppermute | solution.py:246
  88.4 0.1 shard_map.81
  88.6 1.9 %collective-permute-start.1 = (bf16[96,1152]{1,0:T(8,128)(2,1)S(1)}, bf16[96,1152]{1,0:T(8,128)(2,1)S(1)}, u32[]{:S(2)}, u32[]{:S(2)}) collective-permute-start(bf16[96,1152]{1,0:T(8,128)(2,1)S(1)} %get-tuple-element.27), channel_id=1, source_target_pairs={{0,1},{1,2},{2,3},{3,4},{4,5},{5,6},{6,7},{7,8},{8,9},{9,10},{10,1... | collective-permute-start | bytes 663560 | tf_op jit(solution)/shard_map/ppermute | solution.py:246
  90.5 8.6 %collective-permute-done.1.got = bf16[96,1152]{1,0:T(8,128)(2,1)S(1)} collective-permute-done((bf16[96,1152]{1,0:T(8,128)(2,1)S(1)}, bf16[96,1152]{1,0:T(8,128)(2,1)S(1)}, u32[]{:S(2)}, u32[]{:S(2)}) %collective-permute-start.1) | collective-permute-done | bytes 221216 | tf_op jit(solution)/shard_map/ppermute | solution.py:246
  99.1 0.1 shard_map.82
  99.2 1.9 %collective-permute-start.2 = (bf16[48,1152]{1,0:T(8,128)(2,1)S(1)}, bf16[48,1152]{1,0:T(8,128)(2,1)S(1)}, u32[]{:S(2)}, u32[]{:S(2)}) collective-permute-start(bf16[48,1152]{1,0:T(8,128)(2,1)S(1)} %get-tuple-element.29), channel_id=1, source_target_pairs={{0,2},{1,3},{2,4},{3,5},{4,6},{5,7},{6,8},{7,9},{8,10},{9,11},{10,... | collective-permute-start | bytes 331784 | tf_op jit(solution)/shard_map/ppermute | solution.py:246
  101.1 7.5 %collective-permute-done.2.got = bf16[48,1152]{1,0:T(8,128)(2,1)S(1)} collective-permute-done((bf16[48,1152]{1,0:T(8,128)(2,1)S(1)}, bf16[48,1152]{1,0:T(8,128)(2,1)S(1)}, u32[]{:S(2)}, u32[]{:S(2)}) %collective-permute-start.2) | collective-permute-done | bytes 110624 | tf_op jit(solution)/shard_map/ppermute | solution.py:246
  108.7 3.3 %collective-permute-start.3 = (bf16[16,1152]{1,0:T(8,128)(2,1)S(1)}, bf16[16,1152]{1,0:T(8,128)(2,1)S(1)}, u32[]{:S(2)}, u32[]{:S(2)}) collective-permute-start(bf16[16,1152]{1,0:T(8,128)(2,1)S(1)} %get-tuple-element.31), channel_id=1, source_target_pairs={{0,4},{1,5},{2,6},{3,7},{4,8},{5,9},{6,10},{7,11},{8,0},{9,1},{10,... | collective-permute-start | bytes 110600 | tf_op jit(solution)/shard_map/ppermute | solution.py:246
  111.9 6.5 %collective-permute-start.4 = (bf16[16,1152]{1,0:T(8,128)(2,1)S(1)}, bf16[16,1152]{1,0:T(8,128)(2,1)S(1)}, u32[]{:S(2)}, u32[]{:S(2)}) collective-permute-start(bf16[16,1152]{1,0:T(8,128)(2,1)S(1)} %get-tuple-element.32), channel_id=1, source_target_pairs={{0,8},{1,9},{2,10},{3,11},{4,0},{5,1},{6,2},{7,3},{8,4},{9,5},{10,... | collective-permute-start | bytes 110600 | tf_op jit(solution)/shard_map/ppermute | solution.py:246
  118.4 0.0 collective-permute-done.3.refs_1_
  118.4 3.3 %collective-permute-done.4.refs_2_ = bf16[16,1152]{1,0:T(8,128)(2,1)S(1)} collective-permute-done((bf16[16,1152]{1,0:T(8,128)(2,1)S(1)}, bf16[16,1152]{1,0:T(8,128)(2,1)S(1)}, u32[]{:S(2)}, u32[]{:S(2)}) %collective-permute-start.4) | collective-permute-done | bytes 36896 | tf_op jit(solution)/shard_map/ppermute | solution.py:246
  121.8 2.3 %shard_map.84 = f32[16,1536]{1,0:T(8,128)} custom-call(f32[16,1152]{1,0:T(8,128)S(1)} %copy-done.9, f32[16,128]{1,0:T(8,128)S(1)} %get-tuple-element.20.inv, bf16[1536,1152]{1,0:T(8,128)(2,1)S(1)} %copy-done, f32[16,1152]{1,0:T(8,128)S(1)} %get-tuple-element.30.refs_0_, bf16[16,1152]{1,0:T(8,128)(2,1)S(1)} %collective-permute-done.3.refs_1_, ...), custom_call_target="tpu_custom_call" | custom-call | flops 56623104 | bytes 3538944 | tf_op jit(solution)/shard_map/pallas_call | solution.py:228
  124.0 0.0 all-to-all-done.1.refs_0_
  124.0 0.0 copy-start.2
  124.1 1.7 %copy-done.2 = bf16[1024,1152]{1,0:T(8,128)(2,1)S(1)} copy-done((bf16[1024,1152]{1,0:T(8,128)(2,1)S(1)}, bf16[1024,1152]{1,0:T(8,128)(2,1)}, u32[]{:S(2)}) %copy-start.2) | copy-done | bytes 2359320
  125.7 0.9 copy-done.7
  126.6 3.1 %shard_map.85 = f32[16,1024]{1,0:T(8,128)} custom-call(f32[16,1152]{1,0:T(8,128)S(1)} %copy-done.7, f32[16,128]{1,0:T(8,128)S(1)} %get-tuple-element.34.inv, bf16[1024,1152]{1,0:T(8,128)(2,1)S(1)} %copy-done.2, bf16[32,16,1152]{2,1,0:T(8,128)(2,1)} %all-to-all-done.1.refs_0_), custom_call_target="tpu_custom_call" | custom-call | flops 37748736 | bytes 2359296 | tf_op jit(solution)/shard_map/pallas_call | solution.py:228
  (13 shorter events, 0.1 us)
Async XLA Ops:
  0.6 1.7 %copy-start.1 = (bf16[1024,1152]{1,0:T(8,128)(2,1)S(1)}, bf16[1024,1152]{1,0:T(8,128)(2,1)}, u32[]{:S(2)}) copy-start(bf16[1024,1152]{1,0:T(8,128)(2,1)} %proj.7) | copy-start | bytes 7077892
  2.3 0.8 copy-start.11
  3.1 20.1 %copy-start = (bf16[1536,1152]{1,0:T(8,128)(2,1)S(1)}, bf16[1536,1152]{1,0:T(8,128)(2,1)}, u32[]{:S(2)}) copy-start(bf16[1536,1152]{1,0:T(8,128)(2,1)} %proj.6) | copy-start | bytes 10616836
  6.4 1.0 copy-start.4
  7.4 0.6 copy-start.6
  8.0 54.0 %all-to-all-start = ((bf16[32,16,1152]{2,1,0:T(8,128)(2,1)}), bf16[32,16,1152]{2,1,0:T(8,128)(2,1)}, u32[]{:S(2)}, u32[]{:S(2)}) async-start(bf16[32,16,1152]{2,1,0:T(8,128)(2,1)} %copy-done.4), calls=%async_computation | async-start | bytes 2359296 | tf_op jit(solution)/shard_map/all_to_all | solution.py:37
  23.2 0.8 copy-start.10
  26.2 0.6 copy-start.8
  62.0 1.2 copy-start.5
  63.2 0.7 copy-start.12
  63.9 0.6 copy-start.14
  69.3 1.0 copy-start.3
  70.3 0.7 copy-start.15
  71.0 53.0 %all-to-all-start.1 = ((bf16[32,16,1152]{2,1,0:T(8,128)(2,1)}), bf16[32,16,1152]{2,1,0:T(8,128)(2,1)}, u32[]{:S(2)}, u32[]{:S(2)}) async-start(bf16[32,16,1152]{2,1,0:T(8,128)(2,1)} %bitcast.7), calls=%async_computation.1 | async-start | bytes 2359296 | tf_op jit(solution)/shard_map/all_to_all | solution.py:37
  80.9 0.7 copy-start.13
  81.5 1.0 copy-start.16
  84.6 37.1 %copy-start.9 = (f32[16,1152]{1,0:T(8,128)S(1)}, f32[16,1152]{1,0:T(8,128)}, u32[]{:S(2)}) copy-start(f32[16,1152]{1,0:T(8,128)} %copy-done.8) | copy-start | bytes 221188
  84.6 3.8 %collective-permute-start = (bf16[192,1152]{1,0:T(8,128)(2,1)S(1)}, bf16[192,1152]{1,0:T(8,128)(2,1)S(1)}, u32[]{:S(2)}, u32[]{:S(2)}) collective-permute-start(bf16[192,1152]{1,0:T(8,128)(2,1)S(1)} %get-tuple-element.25), channel_id=1, source_target_pairs={{0,12},{12,0},{1,13},{13,1},{2,14},{14,2},{3,15},{15,3},{4,16},{16... | collective-permute-start | bytes 1327112 | tf_op jit(solution)/shard_map/ppermute | solution.py:246
  88.6 10.6 %collective-permute-start.1 = (bf16[96,1152]{1,0:T(8,128)(2,1)S(1)}, bf16[96,1152]{1,0:T(8,128)(2,1)S(1)}, u32[]{:S(2)}, u32[]{:S(2)}) collective-permute-start(bf16[96,1152]{1,0:T(8,128)(2,1)S(1)} %get-tuple-element.27), channel_id=1, source_target_pairs={{0,1},{1,2},{2,3},{3,4},{4,5},{5,6},{6,7},{7,8},{8,9},{9,10},{10,1... | collective-permute-start | bytes 663560 | tf_op jit(solution)/shard_map/ppermute | solution.py:246
  99.2 9.4 %collective-permute-start.2 = (bf16[48,1152]{1,0:T(8,128)(2,1)S(1)}, bf16[48,1152]{1,0:T(8,128)(2,1)S(1)}, u32[]{:S(2)}, u32[]{:S(2)}) collective-permute-start(bf16[48,1152]{1,0:T(8,128)(2,1)S(1)} %get-tuple-element.29), channel_id=1, source_target_pairs={{0,2},{1,3},{2,4},{3,5},{4,6},{5,7},{6,8},{7,9},{8,10},{9,11},{10,... | collective-permute-start | bytes 331784 | tf_op jit(solution)/shard_map/ppermute | solution.py:246
  108.7 9.8 %collective-permute-start.3 = (bf16[16,1152]{1,0:T(8,128)(2,1)S(1)}, bf16[16,1152]{1,0:T(8,128)(2,1)S(1)}, u32[]{:S(2)}, u32[]{:S(2)}) collective-permute-start(bf16[16,1152]{1,0:T(8,128)(2,1)S(1)} %get-tuple-element.31), channel_id=1, source_target_pairs={{0,4},{1,5},{2,6},{3,7},{4,8},{5,9},{6,10},{7,11},{8,0},{9,1},{10,... | collective-permute-start | bytes 110600 | tf_op jit(solution)/shard_map/ppermute | solution.py:246
  111.9 9.8 %collective-permute-start.4 = (bf16[16,1152]{1,0:T(8,128)(2,1)S(1)}, bf16[16,1152]{1,0:T(8,128)(2,1)S(1)}, u32[]{:S(2)}, u32[]{:S(2)}) collective-permute-start(bf16[16,1152]{1,0:T(8,128)(2,1)S(1)} %get-tuple-element.32), channel_id=1, source_target_pairs={{0,8},{1,9},{2,10},{3,11},{4,0},{5,1},{6,2},{7,3},{8,4},{9,5},{10,... | collective-permute-start | bytes 110600 | tf_op jit(solution)/shard_map/ppermute | solution.py:246
  124.0 1.7 %copy-start.2 = (bf16[1024,1152]{1,0:T(8,128)(2,1)S(1)}, bf16[1024,1152]{1,0:T(8,128)(2,1)}, u32[]{:S(2)}) copy-start(bf16[1024,1152]{1,0:T(8,128)(2,1)} %proj.7) | copy-start | bytes 7077892
  125.7 0.9 copy-start.7

commit v5 on v4

v5 whole, which is shorter than its diff:
```python
import functools

import jax
import jax.numpy as jnp
import numpy as np
from jax import lax
from jax.experimental import pallas as pl
from jax.experimental.pallas import tpu as pltpu
from jax.sharding import Mesh
from jax.sharding import PartitionSpec as P

loss_scale = 65536.0
eps = 1e-06
f32 = jnp.float32
bf16 = jnp.bfloat16

vmem = pl.BlockSpec(memory_space=pltpu.VMEM)
smem = pl.BlockSpec(memory_space=pltpu.SMEM)
hbm = pl.BlockSpec(memory_space=pltpu.HBM)
params = pltpu.CompilerParams(vmem_limit_bytes=24 * 2**20)


def far_off(x):
    return pltpu.with_memory_space_constraint(x, pltpu.HBM)

ahead = (0, 4, 8, 1, 5, 9, 2, 6, 10, 11, 3, 7)


def cost(flops, moved, transcendentals=0):
    return pl.CostEstimate(flops=flops, bytes_accessed=moved, transcendentals=transcendentals)


def shift(axis, by):
    n = lax.axis_size(axis)
    return [(i, (i + by) % n) for i in range(n)]


def exchanged(copies, axis):
    return lax.all_to_all(copies, axis, 0, 0, tiled=True)


def embed_kernel(feats, proj, unit_out, inv_out, rows_out, feats_buf, proj_buf, unit_buf, rows_buf, sems, out_sems):
    parts, cut = proj_buf.shape[:2]
    reads = [pltpu.make_async_copy(feats, feats_buf, sems.at[parts])]
    for k in range(parts):
        reads.append(pltpu.make_async_copy(proj.at[pl.ds(k * cut, cut)], proj_buf.at[k], sems.at[k]))
    for read in reads:
        read.start()
    reads[0].wait()
    emb = jnp.zeros(unit_buf.shape, f32)
    for k in range(parts):
        reads[k + 1].wait()
        emb += jnp.dot(
            feats_buf[:, k * cut : (k + 1) * cut], proj_buf[k], preferred_element_type=f32
        )
    inv = lax.rsqrt(jnp.sum(emb * emb, axis=1, keepdims=True) + eps)
    unit = emb * inv
    rows_buf[...] = unit.astype(bf16)
    n = rows_out.shape[0]
    writes = [pltpu.make_async_copy(rows_buf, rows_out.at[k], out_sems.at[k]) for k in range(n)]
    for write in writes:
        write.start()
    unit_buf[...] = unit
    writes.append(pltpu.make_async_copy(unit_buf, unit_out, out_sems.at[n]))
    writes[-1].start()
    inv_out[...] = jnp.broadcast_to(inv, inv_out.shape)
    for write in writes:
        write.wait()


def embed(feats, proj, n):
    own, depth = feats.shape
    width = proj.shape[1]
    cut = 256
    return pl.pallas_call(
        embed_kernel,
        out_shape=[
            pltpu.HBM((own, width), f32),
            jax.ShapeDtypeStruct((own, 128), f32),
            pltpu.HBM((n, own, width), bf16),
        ],
        in_specs=[hbm, hbm],
        out_specs=[hbm, vmem, hbm],
        scratch_shapes=[
            pltpu.VMEM((own, depth), bf16),
            pltpu.VMEM((depth // cut, cut, width), bf16),
            pltpu.VMEM((own, width), f32),
            pltpu.VMEM((own, width), bf16),
            pltpu.SemaphoreType.DMA((depth // cut + 1,)),
            pltpu.SemaphoreType.DMA((n + 1,)),
        ],
        cost_estimate=cost(2 * own * depth * width, 2 * depth * width),
        compiler_params=params,
    )(far_off(feats), far_off(proj))


def image_kernel(own, factor, log_temp, bias, img, txt, coef_out, near_out, far_out, terms):
    nz = len(ahead)
    core = lax.axis_index("core")
    z = lax.axis_index("z")
    first_img = (core * nz + z) * own
    first_txt = lax.axis_index(("y", "x")) * own
    temp = jnp.exp(jnp.full((1, img.shape[0]), log_temp[0], f32))
    factor = factor * temp
    rows = img[...]
    size = 256
    total = 0.0
    for at in range(0, txt.shape[0], size):
        part = slice(at, at + size)
        logits = (
            lax.dot_general(
                txt[part], rows, (((1,), (1,)), ((), ())), preferred_element_type=f32
            )
            * temp
            + bias[0]
        )
        txt_ids = lax.broadcasted_iota(jnp.int32, logits.shape, 0) + (at - first_txt)
        img_ids = lax.broadcasted_iota(jnp.int32, logits.shape, 1) - first_img
        diag = ((txt_ids == img_ids) & (img_ids >= 0) & (img_ids < own)).astype(f32)
        coef = (factor * (jax.nn.sigmoid(logits) - diag)).astype(bf16)
        coef_out[part] = coef
        total = total + lax.dot_general(
            coef, txt[part], (((0,), (0,)), ((), ())), preferred_element_type=f32
        )
    terms[...] = total
    half = nz * own
    for k, by in enumerate(ahead):
        owner = lax.rem(z + by, nz) * own
        near = pl.multiple_of(core * half + owner, own)
        far = pl.multiple_of((1 - core) * half + owner, own)
        near_out[pl.ds(k * own, own)] = terms[pl.ds(near, own)]
        far_out[pl.ds(k * own, own)] = terms[pl.ds(far, own)].astype(bf16)


def image_terms(own, log_temp, bias, factor, img, txt):
    m, w = txt.shape
    i = img.shape[0]
    return pl.pallas_call(
        functools.partial(image_kernel, own, factor),
        out_shape=[
            jax.ShapeDtypeStruct((m, i), bf16),
            jax.ShapeDtypeStruct((i // 2, w), f32),
            jax.ShapeDtypeStruct((i // 2, w), bf16),
        ],
        in_specs=[smem, smem, vmem, vmem],
        out_specs=[vmem, vmem, vmem],
        scratch_shapes=[pltpu.VMEM((i, w), f32)],
        cost_estimate=cost(4 * i * m * w, 4 * (i + m) * w, i * m),
        compiler_params=params,
    )(log_temp, bias, img, txt)


def text_kernel(coef, img, out, buf, sems):
    rows = img[...]
    parts, size = buf.shape[:2]
    writes = []
    for q in range(parts):
        buf[q] = jnp.dot(
            coef[q * size : (q + 1) * size], rows, preferred_element_type=f32
        ).astype(bf16)
        writes.append(pltpu.make_async_copy(buf.at[q], out.at[pl.ds(q * size, size)], sems.at[q]))
        writes[-1].start()
    for write in writes:
        write.wait()


def text_terms(coef, img):
    m, i = coef.shape
    w = img.shape[1]
    parts = 2
    return pl.pallas_call(
        text_kernel,
        out_shape=pltpu.HBM((m, w), bf16),
        in_specs=[vmem, vmem],
        out_specs=hbm,
        scratch_shapes=[
            pltpu.VMEM((parts, m // parts, w), bf16),
            pltpu.SemaphoreType.DMA((parts,)),
        ],
        cost_estimate=cost(2 * i * m * w, 4 * (i + m) * w),
        compiler_params=params,
    )(coef, img)


def fold_kernel(n, *refs):
    parts, outs = refs[:n], refs[n:]
    at = 0
    for out in outs:
        rows = slice(at, at + out.shape[0])
        total = parts[0][rows]
        for part in parts[1:]:
            total = total + part[rows].astype(f32)
        out[...] = total.astype(out.dtype)
        at += out.shape[0]


def fold(size, *parts):
    n, w = parts[0].shape
    return pl.pallas_call(
        functools.partial(fold_kernel, len(parts)),
        out_shape=[
            jax.ShapeDtypeStruct((size, w), f32 if k == 0 else bf16) for k in range(n // size)
        ],
        in_specs=[vmem] * len(parts),
        out_specs=[vmem] * (n // size),
        cost_estimate=cost(n * w, 10 * n * w),
        compiler_params=params,
    )(*parts)


def backprop_kernel(unit, inv, proj, *refs):
    *parts, out, unit_buf, proj_buf, sems = refs
    reads = [
        pltpu.make_async_copy(unit, unit_buf, sems.at[0]),
        pltpu.make_async_copy(proj, proj_buf, sems.at[1]),
    ]
    for read in reads:
        read.start()
    total = 0.0
    for part in parts:
        if len(part.shape) == 2:
            total = total + part[...].astype(f32)
        else:
            for k in range(part.shape[0]):
                total = total + part[k].astype(f32)
    reads[0].wait()
    rows = unit_buf[...]
    along = jnp.sum(rows * total, axis=1, keepdims=True)
    delta = (inv[:, :1] * (total - rows * along)).astype(bf16)
    reads[1].wait()
    out[...] = lax.dot_general(
        delta, proj_buf[...], (((1,), (1,)), ((), ())), preferred_element_type=f32
    )


def backprop(unit, inv, proj, *parts):
    depth, width = proj.shape
    own = unit.shape[0]
    return pl.pallas_call(
        backprop_kernel,
        out_shape=jax.ShapeDtypeStruct((own, depth), f32),
        in_specs=[hbm, vmem, hbm] + [vmem] * len(parts),
        out_specs=vmem,
        scratch_shapes=[
            pltpu.VMEM(unit.shape, f32),
            pltpu.VMEM(proj.shape, bf16),
            pltpu.SemaphoreType.DMA((2,)),
        ],
        cost_estimate=cost(2 * own * depth * width, 2 * depth * width),
        compiler_params=params,
    )(far_off(unit), inv, far_off(proj), *parts)


def shards(image_feats, text_feats, image_proj, text_proj, log_temp, logit_bias):
    own = text_feats.shape[0]
    total = own * lax.axis_size(("y", "x", "core", "z"))
    send = lambda rows, axis, by: lax.ppermute(rows, axis, shift(axis, by))

    txt_unit, txt_inv, txt_rows = embed(text_feats, text_proj, lax.axis_size(("y", "x")))
    img_unit, img_inv, img_rows = embed(image_feats, image_proj, 1)
    txt_rows, img_rows = lax.optimization_barrier((txt_rows, img_rows))
    txt_rows = exchanged(txt_rows, ("y", "x")).reshape(-1, txt_rows.shape[2])
    img_rows = lax.all_gather(img_rows[0], "z", tiled=True)
    img_rows = lax.all_gather(img_rows, "core", tiled=True)

    coef, near, far = image_terms(
        own, log_temp, logit_bias, loss_scale / total, img_rows, txt_rows
    )
    far = send(far, "core", 1)
    txt_terms = text_terms(coef, img_rows)
    txt_terms = exchanged(txt_terms.reshape(-1, own, txt_terms.shape[1]), ("y", "x"))
    near, by1, by2, back = fold(3 * own, near, far)
    near, by4, by8 = fold(
        own, near, send(by1, "z", 1), send(by2, "z", 2), send(back, "z", -1)
    )
    image_grad = backprop(
        img_unit, img_inv, image_proj, near, send(by4, "z", 4), send(by8, "z", 8)
    )
    text_grad = backprop(txt_unit, txt_inv, text_proj, txt_terms)
    return (image_grad, text_grad)


def solution(mesh):
    blk, grp = mesh.devices.shape
    fine = Mesh(np.asarray(mesh.devices).reshape(blk // 8, 4, 2, grp), ("y", "x", "core", "z"))
    rows = P(("y", "x", "core", "z"), None)
    return jax.shard_map(
        shards,
        mesh=fine,
        in_specs=(rows, rows, P(), P(), P(), P()),
        out_specs=(rows, rows),
        check_vma=False,
    )
```

time: 131 us -> 107 us (0.82)
  local copies, waits for them, and re-layouts: 13.9 us -> 0.01 us
  waiting for transfers between devices: 21.2 us -> 9.06 us
  starting transfers between devices: 39.2 us -> 43.8 us
    unnamed x34 -> x2, local copies, waits for them, and re-layouts: 13.9 us -> 0.01 us
    ppermute x5 -> x6, waiting for transfers between devices: 21.2 us -> 9.05 us  [shards(): send = lambda rows, axis, by: lax.ppermute(rows, axis, shift(axis, by))]
    ppermute x5 -> x6, starting transfers between devices: 15.6 us -> 20.9 us  [shards(): send = lambda rows, axis, by: lax.ppermute(rows, axis, shift(axis, by))]
    pallas_call x7 -> x6, Pallas kernels: 12.6 us -> 10.1 us  [the longest x2 6.59 us: embed(): pl.pallas_call(embed_kernel, out_shape=[pltpu.HBM((own, width), f32), jax...]
    pallas_call x2, Pallas kernels: 5.38 us -> 6.81 us  [backprop(): pl.pallas_call(backprop_kernel, out_shape=jax.ShapeDtypeStruct((own, dept...]
  transfers between devices with their start and end apart: 7 -> 8, of which waited for: 4 -> 5; matrix products, arithmetic and copies ran while one was open for 1% -> 0% of each run, Pallas kernels for 5% -> 4%
where the time goes in v5:
time: 107 us; the launch traced here: 106 us
  starting transfers between devices  43.8 us (41%)
  blocking collectives  34.4 us (32%)
  Pallas kernels  16.9 us (16%)
  waiting for transfers between devices  9.06 us (8%)
  between operations  2.07 us (2%)
    all_gather x1, blocking collectives, shards(): img_rows = lax.all_gather(img_rows[0], 'z', tiled=True)  31.9 us
    all_to_all x2, starting transfers between devices, exchanged(): return lax.all_to_all(copies, axis, 0, 0, tiled=True)  22.9 us
    ppermute x6, starting transfers between devices, shards(): send = lambda rows, axis, by: lax.ppermute(rows, axis, shift(axis, by))  20.9 us
    ppermute x6, waiting for transfers between devices, shards(): send = lambda rows, axis, by: lax.ppermute(rows, axis, shift(axis, by))  9.05 us
    pallas_call x2, Pallas kernels, backprop(): pl.pallas_call(backprop_kernel, out_shape=jax.ShapeDtypeStruct((own, dept...  6.81 us
    pallas_call x2, Pallas kernels, embed(): pl.pallas_call(embed_kernel, out_shape=[pltpu.HBM((own, width), f32), jax...  6.59 us
    all_gather x1, blocking collectives, shards(): img_rows = lax.all_gather(img_rows, 'core', tiled=True)  2.43 us
  transfers between devices with their start and end apart: 8, of which 5 were waited for; matrix products, arithmetic and copies ran while one was open for 0% of the time, Pallas kernels for 4%

profile of v5, /device:TPU:6, one launch (start us, length us, event | category | flops | bytes accessed | tf_op | source)
XLA Modules:
  0.0 106.2 jit_solution(1412429323200960400)
XLA Ops:
  0.6 3.2 %shard_map.77 = (f32[16,1152]{1,0:T(8,128)}, f32[16,128]{1,0:T(8,128)S(1)}, bf16[1,16,1152]{2,1,0:T(8,128)(2,1)}) custom-call(bf16[16,1536]{1,0:T(8,128)(2,1)} %feats.2, bf16[1536,1152]{1,0:T(8,128)(2,1)} %proj.6), custom_call_target="tpu_custom_call" | custom-call | flops 56623104 | bytes 3538944 | tf_op jit(solution)/shard_map/pallas_call | solution.py:75
  3.8 3.4 %shard_map.78 = (f32[16,1152]{1,0:T(8,128)}, f32[16,128]{1,0:T(8,128)S(1)}, bf16[32,16,1152]{2,1,0:T(8,128)(2,1)}) custom-call(bf16[16,1024]{1,0:T(8,128)(2,1)} %feats.3, bf16[1024,1152]{1,0:T(8,128)(2,1)} %proj.7), custom_call_target="tpu_custom_call" | custom-call | flops 37748736 | bytes 2359296 | tf_op jit(solution)/shard_map/pallas_call | solution.py:75
  7.2 0.0 copy-start
  7.2 13.1 %all-to-all-start = ((bf16[32,16,1152]{2,1,0:T(8,128)(2,1)}), bf16[32,16,1152]{2,1,0:T(8,128)(2,1)S(1)}, u32[]{:S(2)}, u32[]{:S(2)}) async-start(bf16[32,16,1152]{2,1,0:T(8,128)(2,1)} %get-tuple-element.25), calls=%async_computation | async-start | bytes 2359296 | tf_op jit(solution)/shard_map/all_to_all | solution.py:39
  21.7 0.0 copy-done
  21.7 31.9 %all-gather = bf16[1,192,1152]{2,1,0:T(8,128)(2,1)S(1)} all-gather(bf16[1,16,1152]{2,1,0:T(8,128)(2,1)S(1)} %copy-done), channel_id=2, replica_groups=mesh['y'=8,'x'=4,'core'=2,'z'=12] {'z'}, dimensions={1}, use_global_device_ids=true | all-gather | bytes 479232 | tf_op jit(solution)/shard_map/all_gather | solution.py:263
  53.6 2.4 %all-gather.1 = bf16[1,384,1152]{2,1,0:T(8,128)(2,1)S(1)} all-gather(bf16[1,192,1152]{2,1,0:T(8,128)(2,1)S(1)} %all-gather), channel_id=3, replica_groups=mesh['y'=8,'x'=4,'core'=2,'z'=12] {'core'}, dimensions={1}, use_global_device_ids=true | all-gather | bytes 1327104 | tf_op jit(solution)/shard_map/all_gather | solution.py:264
  56.0 0.0 all-to-all-done
  56.0 1.7 %shard_map.79 = (bf16[512,384]{1,0:T(8,128)(2,1)S(1)}, f32[192,1152]{1,0:T(8,128)S(1)}, bf16[192,1152]{1,0:T(8,128)(2,1)S(1)}) custom-call(f32[1]{0:T(128)S(6)} %copy.8.log_temp, f32[1]{0:T(128)S(6)} %copy.9.bias, bf16[384,1152]{1,0:T(8,128)(2,1)S(1)} %bitcast.3, bf16[512,1152]{1,0:T(8,128)(2,1)S(1)} %bitcast.5), custom_call_target="tpu_custom_call" | custom-call | flops 905969664 | bytes 4128768 | tf_op jit(solution)/shard_map/pallas_call | solution.py:138
  57.7 1.6 %shard_map.83 = bf16[512,1152]{1,0:T(8,128)(2,1)} custom-call(bf16[512,384]{1,0:T(8,128)(2,1)S(1)} %get-tuple-element.37.coef, bf16[384,1152]{1,0:T(8,128)(2,1)S(1)} %bitcast.4), custom_call_target="tpu_custom_call" | custom-call | flops 452984832 | bytes 4128768 | tf_op jit(solution)/shard_map/pallas_call | solution.py:171
  59.4 9.8 %all-to-all-start.1 = ((bf16[32,16,1152]{2,1,0:T(8,128)(2,1)}), bf16[32,16,1152]{2,1,0:T(8,128)(2,1)S(1)}, u32[]{:S(2)}, u32[]{:S(2)}) async-start(bf16[32,16,1152]{2,1,0:T(8,128)(2,1)} %bitcast.6), calls=%async_computation.1 | async-start | bytes 2359296 | tf_op jit(solution)/shard_map/all_to_all | solution.py:39
  69.2 1.9 %collective-permute-start = (bf16[192,1152]{1,0:T(8,128)(2,1)S(1)}, bf16[192,1152]{1,0:T(8,128)(2,1)S(1)}, u32[]{:S(2)}, u32[]{:S(2)}) collective-permute-start(bf16[192,1152]{1,0:T(8,128)(2,1)S(1)} %get-tuple-element.27), channel_id=1, source_target_pairs={{0,12},{12,0},{1,13},{13,1},{2,14},{14,2},{3,15},{15,3},{4,16},{16... | collective-permute-start | bytes 1327112 | tf_op jit(solution)/shard_map/ppermute | solution.py:257
  71.1 1.8 %collective-permute-done.refs_1_ = bf16[192,1152]{1,0:T(8,128)(2,1)S(1)} collective-permute-done((bf16[192,1152]{1,0:T(8,128)(2,1)S(1)}, bf16[192,1152]{1,0:T(8,128)(2,1)S(1)}, u32[]{:S(2)}, u32[]{:S(2)}) %collective-permute-start) | collective-permute-done | bytes 442400 | tf_op jit(solution)/shard_map/ppermute | solution.py:257
  72.8 0.1 shard_map.80
  73.0 1.9 %collective-permute-start.1 = (bf16[48,1152]{1,0:T(8,128)(2,1)S(1)}, bf16[48,1152]{1,0:T(8,128)(2,1)S(1)}, u32[]{:S(2)}, u32[]{:S(2)}) collective-permute-start(bf16[48,1152]{1,0:T(8,128)(2,1)S(1)} %get-tuple-element.29), channel_id=1, source_target_pairs={{0,1},{1,2},{2,3},{3,4},{4,5},{5,6},{6,7},{7,8},{8,9},{9,10},{10,1... | collective-permute-start | bytes 331784 | tf_op jit(solution)/shard_map/ppermute | solution.py:257
  74.9 2.2 %collective-permute-start.2 = (bf16[48,1152]{1,0:T(8,128)(2,1)S(1)}, bf16[48,1152]{1,0:T(8,128)(2,1)S(1)}, u32[]{:S(2)}, u32[]{:S(2)}) collective-permute-start(bf16[48,1152]{1,0:T(8,128)(2,1)S(1)} %get-tuple-element.30), channel_id=1, source_target_pairs={{0,2},{1,3},{2,4},{3,5},{4,6},{5,7},{6,8},{7,9},{8,10},{9,11},{10,... | collective-permute-start | bytes 331784 | tf_op jit(solution)/shard_map/ppermute | solution.py:257
  77.1 5.1 %collective-permute-start.3 = (bf16[48,1152]{1,0:T(8,128)(2,1)S(1)}, bf16[48,1152]{1,0:T(8,128)(2,1)S(1)}, u32[]{:S(2)}, u32[]{:S(2)}) collective-permute-start(bf16[48,1152]{1,0:T(8,128)(2,1)S(1)} %get-tuple-element.31), channel_id=1, source_target_pairs={{0,11},{1,0},{2,1},{3,2},{4,3},{5,4},{6,5},{7,6},{8,7},{9,8},{10,9... | collective-permute-start | bytes 331784 | tf_op jit(solution)/shard_map/ppermute | solution.py:257
  82.2 0.0 collective-permute-done.1.refs_1_
  82.2 1.9 %collective-permute-done.2.refs_2_ = bf16[48,1152]{1,0:T(8,128)(2,1)S(1)} collective-permute-done((bf16[48,1152]{1,0:T(8,128)(2,1)S(1)}, bf16[48,1152]{1,0:T(8,128)(2,1)S(1)}, u32[]{:S(2)}, u32[]{:S(2)}) %collective-permute-start.2) | collective-permute-done | bytes 110624 | tf_op jit(solution)/shard_map/ppermute | solution.py:257
  84.1 0.4 collective-permute-done.3.refs_3_
  84.5 0.1 shard_map.81
  84.6 4.9 %collective-permute-start.4 = (bf16[16,1152]{1,0:T(8,128)(2,1)S(1)}, bf16[16,1152]{1,0:T(8,128)(2,1)S(1)}, u32[]{:S(2)}, u32[]{:S(2)}) collective-permute-start(bf16[16,1152]{1,0:T(8,128)(2,1)S(1)} %get-tuple-element.33), channel_id=1, source_target_pairs={{0,4},{1,5},{2,6},{3,7},{4,8},{5,9},{6,10},{7,11},{8,0},{9,1},{10,... | collective-permute-start | bytes 110600 | tf_op jit(solution)/shard_map/ppermute | solution.py:257
  89.5 4.9 %collective-permute-start.5 = (bf16[16,1152]{1,0:T(8,128)(2,1)S(1)}, bf16[16,1152]{1,0:T(8,128)(2,1)S(1)}, u32[]{:S(2)}, u32[]{:S(2)}) collective-permute-start(bf16[16,1152]{1,0:T(8,128)(2,1)S(1)} %get-tuple-element.34), channel_id=1, source_target_pairs={{0,8},{1,9},{2,10},{3,11},{4,0},{5,1},{6,2},{7,3},{8,4},{9,5},{10,... | collective-permute-start | bytes 110600 | tf_op jit(solution)/shard_map/ppermute | solution.py:257
  94.3 0.1 collective-permute-done.4.refs_1_
  94.4 4.9 %collective-permute-done.5.refs_2_ = bf16[16,1152]{1,0:T(8,128)(2,1)S(1)} collective-permute-done((bf16[16,1152]{1,0:T(8,128)(2,1)S(1)}, bf16[16,1152]{1,0:T(8,128)(2,1)S(1)}, u32[]{:S(2)}, u32[]{:S(2)}) %collective-permute-start.5) | collective-permute-done | bytes 36896 | tf_op jit(solution)/shard_map/ppermute | solution.py:257
  99.3 3.7 %shard_map.82 = f32[16,1536]{1,0:T(8,128)} custom-call(f32[16,1152]{1,0:T(8,128)} %get-tuple-element.20.unit, f32[16,128]{1,0:T(8,128)S(1)} %get-tuple-element.21.inv, bf16[1536,1152]{1,0:T(8,128)(2,1)} %proj.6, f32[16,1152]{1,0:T(8,128)S(1)} %get-tuple-element.32.refs_0_, bf16[16,1152]{1,0:T(8,128)(2,1)S(1)} %collective-permute-done.4.refs_1_, ...), custom_call_target="tpu_custom_call" | custom-call | flops 56623104 | bytes 3538944 | tf_op jit(solution)/shard_map/pallas_call | solution.py:239
  103.1 0.0 all-to-all-done.1.refs_0_
  103.1 3.1 %shard_map.84 = f32[16,1024]{1,0:T(8,128)} custom-call(f32[16,1152]{1,0:T(8,128)} %get-tuple-element.35.unit, f32[16,128]{1,0:T(8,128)S(1)} %get-tuple-element.36.inv, bf16[1024,1152]{1,0:T(8,128)(2,1)} %proj.7, bf16[32,16,1152]{2,1,0:T(8,128)(2,1)S(1)} %all-to-all-done.1.refs_0_), custom_call_target="tpu_custom_call" | custom-call | flops 37748736 | bytes 2359296 | tf_op jit(solution)/shard_map/pallas_call | solution.py:239
Async XLA Ops:
  7.2 14.4 %copy-start = (bf16[1,16,1152]{2,1,0:T(8,128)(2,1)S(1)}, bf16[1,16,1152]{2,1,0:T(8,128)(2,1)}, u32[]{:S(2)}) copy-start(bf16[1,16,1152]{2,1,0:T(8,128)(2,1)} %get-tuple-element.24) | copy-start | bytes 110596
  7.2 48.8 %all-to-all-start = ((bf16[32,16,1152]{2,1,0:T(8,128)(2,1)}), bf16[32,16,1152]{2,1,0:T(8,128)(2,1)S(1)}, u32[]{:S(2)}, u32[]{:S(2)}) async-start(bf16[32,16,1152]{2,1,0:T(8,128)(2,1)} %get-tuple-element.25), calls=%async_computation | async-start | bytes 2359296 | tf_op jit(solution)/shard_map/all_to_all | solution.py:39
  59.4 43.7 %all-to-all-start.1 = ((bf16[32,16,1152]{2,1,0:T(8,128)(2,1)}), bf16[32,16,1152]{2,1,0:T(8,128)(2,1)S(1)}, u32[]{:S(2)}, u32[]{:S(2)}) async-start(bf16[32,16,1152]{2,1,0:T(8,128)(2,1)} %bitcast.6), calls=%async_computation.1 | async-start | bytes 2359296 | tf_op jit(solution)/shard_map/all_to_all | solution.py:39
  69.2 3.7 %collective-permute-start = (bf16[192,1152]{1,0:T(8,128)(2,1)S(1)}, bf16[192,1152]{1,0:T(8,128)(2,1)S(1)}, u32[]{:S(2)}, u32[]{:S(2)}) collective-permute-start(bf16[192,1152]{1,0:T(8,128)(2,1)S(1)} %get-tuple-element.27), channel_id=1, source_target_pairs={{0,12},{12,0},{1,13},{13,1},{2,14},{14,2},{3,15},{15,3},{4,16},{16... | collective-permute-start | bytes 1327112 | tf_op jit(solution)/shard_map/ppermute | solution.py:257
  73.0 9.2 %collective-permute-start.1 = (bf16[48,1152]{1,0:T(8,128)(2,1)S(1)}, bf16[48,1152]{1,0:T(8,128)(2,1)S(1)}, u32[]{:S(2)}, u32[]{:S(2)}) collective-permute-start(bf16[48,1152]{1,0:T(8,128)(2,1)S(1)} %get-tuple-element.29), channel_id=1, source_target_pairs={{0,1},{1,2},{2,3},{3,4},{4,5},{5,6},{6,7},{7,8},{8,9},{9,10},{10,1... | collective-permute-start | bytes 331784 | tf_op jit(solution)/shard_map/ppermute | solution.py:257
  74.9 9.2 %collective-permute-start.2 = (bf16[48,1152]{1,0:T(8,128)(2,1)S(1)}, bf16[48,1152]{1,0:T(8,128)(2,1)S(1)}, u32[]{:S(2)}, u32[]{:S(2)}) collective-permute-start(bf16[48,1152]{1,0:T(8,128)(2,1)S(1)} %get-tuple-element.30), channel_id=1, source_target_pairs={{0,2},{1,3},{2,4},{3,5},{4,6},{5,7},{6,8},{7,9},{8,10},{9,11},{10,... | collective-permute-start | bytes 331784 | tf_op jit(solution)/shard_map/ppermute | solution.py:257
  77.1 7.4 %collective-permute-start.3 = (bf16[48,1152]{1,0:T(8,128)(2,1)S(1)}, bf16[48,1152]{1,0:T(8,128)(2,1)S(1)}, u32[]{:S(2)}, u32[]{:S(2)}) collective-permute-start(bf16[48,1152]{1,0:T(8,128)(2,1)S(1)} %get-tuple-element.31), channel_id=1, source_target_pairs={{0,11},{1,0},{2,1},{3,2},{4,3},{5,4},{6,5},{7,6},{8,7},{9,8},{10,9... | collective-permute-start | bytes 331784 | tf_op jit(solution)/shard_map/ppermute | solution.py:257
  84.6 9.9 %collective-permute-start.4 = (bf16[16,1152]{1,0:T(8,128)(2,1)S(1)}, bf16[16,1152]{1,0:T(8,128)(2,1)S(1)}, u32[]{:S(2)}, u32[]{:S(2)}) collective-permute-start(bf16[16,1152]{1,0:T(8,128)(2,1)S(1)} %get-tuple-element.33), channel_id=1, source_target_pairs={{0,4},{1,5},{2,6},{3,7},{4,8},{5,9},{6,10},{7,11},{8,0},{9,1},{10,... | collective-permute-start | bytes 110600 | tf_op jit(solution)/shard_map/ppermute | solution.py:257
  89.5 9.9 %collective-permute-start.5 = (bf16[16,1152]{1,0:T(8,128)(2,1)S(1)}, bf16[16,1152]{1,0:T(8,128)(2,1)S(1)}, u32[]{:S(2)}, u32[]{:S(2)}) collective-permute-start(bf16[16,1152]{1,0:T(8,128)(2,1)S(1)} %get-tuple-element.34), channel_id=1, source_target_pairs={{0,8},{1,9},{2,10},{3,11},{4,0},{5,1},{6,2},{7,3},{8,4},{9,5},{10,... | collective-permute-start | bytes 110600 | tf_op jit(solution)/shard_map/ppermute | solution.py:257

commit v6 on v5

--- a/solution.py
+++ b/solution.py
@@ -39,59 +39,85 @@
     return lax.all_to_all(copies, axis, 0, 0, tiled=True)
 
 
-def embed_kernel(feats, proj, unit_out, inv_out, rows_out, feats_buf, proj_buf, unit_buf, rows_buf, sems, out_sems):
-    parts, cut = proj_buf.shape[:2]
-    reads = [pltpu.make_async_copy(feats, feats_buf, sems.at[parts])]
-    for k in range(parts):
-        reads.append(pltpu.make_async_copy(proj.at[pl.ds(k * cut, cut)], proj_buf.at[k], sems.at[k]))
-    for read in reads:
+def embed_kernel(txt, txt_proj, img, img_proj, *refs):
+    txt_unit, txt_inv, txt_rows, img_unit, img_inv, img_rows = refs[:6]
+    txt_buf, txt_w, img_buf, img_w, unit_buf, rows_buf, sems, out_sems = refs[6:]
+    cut = txt_w.shape[1]
+    copies = txt_rows.shape[0]
+    reads = []
+    for feats, buf, proj, weights in ((txt, txt_buf, txt_proj, txt_w), (img, img_buf, img_proj, img_w)):
+        reads.append([pltpu.make_async_copy(feats, buf, sems.at[sum(map(len, reads))])])
+        for k in range(weights.shape[0]):
+            reads[-1].append(
+                pltpu.make_async_copy(
+                    proj.at[pl.ds(k * cut, cut)], weights.at[k], sems.at[sum(map(len, reads))]
+                )
+            )
+    for read in reads[0] + reads[1]:
         read.start()
-    reads[0].wait()
-    emb = jnp.zeros(unit_buf.shape, f32)
-    for k in range(parts):
-        reads[k + 1].wait()
-        emb += jnp.dot(
-            feats_buf[:, k * cut : (k + 1) * cut], proj_buf[k], preferred_element_type=f32
-        )
-    inv = lax.rsqrt(jnp.sum(emb * emb, axis=1, keepdims=True) + eps)
-    unit = emb * inv
+
+    def unit_rows(buf, weights, arrivals):
+        arrivals[0].wait()
+        emb = jnp.zeros(unit_buf.shape[1:], f32)
+        for k, arrival in enumerate(arrivals[1:]):
+            arrival.wait()
+            emb += jnp.dot(
+                buf[:, k * cut : (k + 1) * cut], weights[k], preferred_element_type=f32
+            )
+        inv = lax.rsqrt(jnp.sum(emb * emb, axis=1, keepdims=True) + eps)
+        return emb * inv, inv
+
+    unit, inv = unit_rows(txt_buf, txt_w, reads[0])
     rows_buf[...] = unit.astype(bf16)
-    n = rows_out.shape[0]
-    writes = [pltpu.make_async_copy(rows_buf, rows_out.at[k], out_sems.at[k]) for k in range(n)]
+    writes = [
+        pltpu.make_async_copy(rows_buf, txt_rows.at[k], out_sems.at[k]) for k in range(copies)
+    ]
     for write in writes:
         write.start()
-    unit_buf[...] = unit
-    writes.append(pltpu.make_async_copy(unit_buf, unit_out, out_sems.at[n]))
+    unit_buf[0] = unit
+    writes.append(pltpu.make_async_copy(unit_buf.at[0], txt_unit, out_sems.at[copies]))
     writes[-1].start()
-    inv_out[...] = jnp.broadcast_to(inv, inv_out.shape)
+    txt_inv[...] = jnp.broadcast_to(inv, txt_inv.shape)
+    unit, inv = unit_rows(img_buf, img_w, reads[1])
+    img_rows[...] = unit.astype(bf16)
+    unit_buf[1] = unit
+    writes.append(pltpu.make_async_copy(unit_buf.at[1], img_unit, out_sems.at[copies + 1]))
+    writes[-1].start()
+    img_inv[...] = jnp.broadcast_to(inv, img_inv.shape)
     for write in writes:
         write.wait()
 
 
-def embed(feats, proj, n):
-    own, depth = feats.shape
-    width = proj.shape[1]
-    cut = 256
+def embed(txt, txt_proj, img, img_proj, copies):
+    own, width = txt.shape[0], txt_proj.shape[1]
+    cut = 512
+    txt_cuts, img_cuts = txt.shape[1] // cut, img.shape[1] // cut
+    unit, inv = pltpu.HBM((own, width), f32), jax.ShapeDtypeStruct((own, 128), f32)
     return pl.pallas_call(
         embed_kernel,
         out_shape=[
-            pltpu.HBM((own, width), f32),
-            jax.ShapeDtypeStruct((own, 128), f32),
-            pltpu.HBM((n, own, width), bf16),
-        ],
-        in_specs=[hbm, hbm],
-        out_specs=[hbm, vmem, hbm],
+            unit,
+            inv,
+            pltpu.HBM((copies, own, width), bf16),
+            unit,
+            inv,
+            jax.ShapeDtypeStruct((own, width), bf16),
+        ],
+        in_specs=[hbm] * 4,
+        out_specs=[hbm, vmem, hbm, hbm, vmem, vmem],
         scratch_shapes=[
-            pltpu.VMEM((own, depth), bf16),
-            pltpu.VMEM((depth // cut, cut, width), bf16),
-            pltpu.VMEM((own, width), f32),
+            pltpu.VMEM(txt.shape, bf16),
+            pltpu.VMEM((txt_cuts, cut, width), bf16),
+            pltpu.VMEM(img.shape, bf16),
+            pltpu.VMEM((img_cuts, cut, width), bf16),
+            pltpu.VMEM((2, own, width), f32),
             pltpu.VMEM((own, width), bf16),
-            pltpu.SemaphoreType.DMA((depth // cut + 1,)),
-            pltpu.SemaphoreType.DMA((n + 1,)),
-        ],
-        cost_estimate=cost(2 * own * depth * width, 2 * depth * width),
-        compiler_params=params,
-    )(far_off(feats), far_off(proj))
+            pltpu.SemaphoreType.DMA((txt_cuts + img_cuts + 2,)),
+            pltpu.SemaphoreType.DMA((copies + 2,)),
+        ],
+        cost_estimate=cost(2 * own * width * (txt.shape[1] + img.shape[1]), 6 * 2**20),
+        compiler_params=params,
+    )(*map(far_off, (txt, txt_proj, img, img_proj)))
 
 
 def image_kernel(own, factor, log_temp, bias, img, txt, coef_out, near_out, far_out, terms):
@@ -196,6 +222,7 @@
 
 def fold(size, *parts):
     n, w = parts[0].shape
+    work = 10**10
     return pl.pallas_call(
         functools.partial(fold_kernel, len(parts)),
         out_shape=[
@@ -203,17 +230,17 @@
         ],
         in_specs=[vmem] * len(parts),
         out_specs=[vmem] * (n // size),
-        cost_estimate=cost(n * w, 10 * n * w),
+        cost_estimate=cost(work, 10 * n * w),
         compiler_params=params,
     )(*parts)
 
 
 def backprop_kernel(unit, inv, proj, *refs):
     *parts, out, unit_buf, proj_buf, sems = refs
-    reads = [
-        pltpu.make_async_copy(unit, unit_buf, sems.at[0]),
-        pltpu.make_async_copy(proj, proj_buf, sems.at[1]),
-    ]
+    cuts, cut = proj_buf.shape[:2]
+    reads = [pltpu.make_async_copy(unit, unit_buf, sems.at[cuts])]
+    for k in range(cuts):
+        reads.append(pltpu.make_async_copy(proj.at[pl.ds(k * cut, cut)], proj_buf.at[k], sems.at[k]))
     for read in reads:
         read.start()
     total = 0.0
@@ -227,15 +254,17 @@
     rows = unit_buf[...]
     along = jnp.sum(rows * total, axis=1, keepdims=True)
     delta = (inv[:, :1] * (total - rows * along)).astype(bf16)
-    reads[1].wait()
-    out[...] = lax.dot_general(
-        delta, proj_buf[...], (((1,), (1,)), ((), ())), preferred_element_type=f32
-    )
+    for k in range(cuts):
+        reads[k + 1].wait()
+        out[:, k * cut : (k + 1) * cut] = lax.dot_general(
+            delta, proj_buf[k], (((1,), (1,)), ((), ())), preferred_element_type=f32
+        )
 
 
 def backprop(unit, inv, proj, *parts):
     depth, width = proj.shape
     own = unit.shape[0]
+    cut = 512
     return pl.pallas_call(
         backprop_kernel,
         out_shape=jax.ShapeDtypeStruct((own, depth), f32),
@@ -243,8 +272,8 @@
         out_specs=vmem,
         scratch_shapes=[
             pltpu.VMEM(unit.shape, f32),
-            pltpu.VMEM(proj.shape, bf16),
-            pltpu.SemaphoreType.DMA((2,)),
+            pltpu.VMEM((depth // cut, cut, width), bf16),
+            pltpu.SemaphoreType.DMA((depth // cut + 1,)),
         ],
         cost_estimate=cost(2 * own * depth * width, 2 * depth * width),
         compiler_params=params,
@@ -256,11 +285,12 @@
     total = own * lax.axis_size(("y", "x", "core", "z"))
     send = lambda rows, axis, by: lax.ppermute(rows, axis, shift(axis, by))
 
-    txt_unit, txt_inv, txt_rows = embed(text_feats, text_proj, lax.axis_size(("y", "x")))
-    img_unit, img_inv, img_rows = embed(image_feats, image_proj, 1)
-    txt_rows, img_rows = lax.optimization_barrier((txt_rows, img_rows))
+    copies = lax.axis_size(("y", "x"))
+    txt_unit, txt_inv, txt_rows, img_unit, img_inv, img_rows = embed(
+        text_feats, text_proj, image_feats, image_proj, copies
+    )
     txt_rows = exchanged(txt_rows, ("y", "x")).reshape(-1, txt_rows.shape[2])
-    img_rows = lax.all_gather(img_rows[0], "z", tiled=True)
+    img_rows = lax.all_gather(img_rows, "z", tiled=True)
     img_rows = lax.all_gather(img_rows, "core", tiled=True)
 
     coef, near, far = image_terms(
@@ -273,10 +303,10 @@
     near, by4, by8 = fold(
         own, near, send(by1, "z", 1), send(by2, "z", 2), send(back, "z", -1)
     )
-    image_grad = backprop(
-        img_unit, img_inv, image_proj, near, send(by4, "z", 4), send(by8, "z", 8)
-    )
     text_grad = backprop(txt_unit, txt_inv, text_proj, txt_terms)
+    got = (send(by4, "z", 4), send(by8, "z", 8))
+    near, text_grad = lax.optimization_barrier((near, text_grad))
+    image_grad = backprop(img_unit, img_inv, image_proj, near, *got)
     return (image_grad, text_grad)
 
 

time: 107 us -> 107 us (level)
  Pallas kernels: 16.9 us -> 13.7 us
  waiting for transfers between devices: 9.06 us -> 12.2 us
    all_to_all x2, waiting for transfers between devices: 0.01 us -> 9.93 us  [exchanged(): return lax.all_to_all(copies, axis, 0, 0, tiled=True)]
    ppermute x6, waiting for transfers between devices: 9.05 us -> 2.31 us  [shards(): send = lambda rows, axis, by: lax.ppermute(rows, axis, shift(axis, by))]
    pallas_call x2 -> x1, Pallas kernels: 6.59 us -> 4.16 us  [embed(): pl.pallas_call(embed_kernel, out_shape=[unit, inv, pltpu.HBM((copies, own...]
  transfers between devices with their start and end apart: 8 -> 8, of which waited for: 5 -> 3; matrix products, arithmetic and copies ran while one was open for 0% -> 0% of each run, Pallas kernels for 4% -> 4%
where the time goes in v6:
time: 107 us; the launch traced here: 106 us
  starting transfers between devices  43.9 us (41%)
  blocking collectives  34.4 us (32%)
  Pallas kernels  13.7 us (13%)
  waiting for transfers between devices  12.2 us (11%)
  between operations  2.06 us (2%)
    all_gather x1, blocking collectives, shards(): img_rows = lax.all_gather(img_rows, 'z', tiled=True)  31.9 us
    all_to_all x2, starting transfers between devices, exchanged(): return lax.all_to_all(copies, axis, 0, 0, tiled=True)  22.9 us
    ppermute x6, starting transfers between devices, shards(): send = lambda rows, axis, by: lax.ppermute(rows, axis, shift(axis, by))  21 us
    all_to_all x2, waiting for transfers between devices, exchanged(): return lax.all_to_all(copies, axis, 0, 0, tiled=True)  9.93 us
    pallas_call x2, Pallas kernels, backprop(): pl.pallas_call(backprop_kernel, out_shape=jax.ShapeDtypeStruct((own, dept...  6.06 us
    pallas_call x1, Pallas kernels, embed(): pl.pallas_call(embed_kernel, out_shape=[unit, inv, pltpu.HBM((copies, own...  4.16 us
    all_gather x1, blocking collectives, shards(): img_rows = lax.all_gather(img_rows, 'core', tiled=True)  2.43 us
    ppermute x6, waiting for transfers between devices, shards(): send = lambda rows, axis, by: lax.ppermute(rows, axis, shift(axis, by))  2.31 us
  transfers between devices with their start and end apart: 8, of which 3 were waited for; matrix products, arithmetic and copies ran while one was open for 0% of the time, Pallas kernels for 4%

profile of v6, /device:TPU:6, one launch (start us, length us, event | category | flops | bytes accessed | tf_op | source)
XLA Modules:
  0.0 106.3 jit_solution(10127538609905176055)
XLA Ops:
  0.6 4.2 %shard_map.77 = (f32[16,1152]{1,0:T(8,128)}, f32[16,128]{1,0:T(8,128)S(1)}, bf16[32,16,1152]{2,1,0:T(8,128)(2,1)}, f32[16,1152]{1,0:T(8,128)}, f32[16,128]{1,0:T(8,128)S(1)}, /*index=5*/bf16[16,1152]{1,0:T(8,128)(2,1)S(1)}) custom-call(bf16[16,1024]{1,0:T(8,128)(2,1)} %txt.1, bf16[1024,1152]{1,0:T(8,128)(2,1)} %proj.2, bf16[16,1536]{1,0:T(8,128)(2,1)} %img.1, ...), custom_call_target="tpu_custom_call" | custom-call | flops 94371840 | bytes 6291456 | tf_op jit(solution)/shard_map/pallas_call | solution.py:96
  4.8 13.1 %all-to-all-start = ((bf16[32,16,1152]{2,1,0:T(8,128)(2,1)}), bf16[32,16,1152]{2,1,0:T(8,128)(2,1)S(1)}, u32[]{:S(2)}, u32[]{:S(2)}) async-start(bf16[32,16,1152]{2,1,0:T(8,128)(2,1)} %get-tuple-element.23), calls=%async_computation | async-start | bytes 2359296 | tf_op jit(solution)/shard_map/all_to_all | solution.py:39
  19.2 31.9 %all_gather.6 = bf16[192,1152]{1,0:T(8,128)(2,1)S(1)} all-gather(bf16[16,1152]{1,0:T(8,128)(2,1)S(1)} %get-tuple-element.22), channel_id=1, replica_groups=mesh['y'=8,'x'=4,'core'=2,'z'=12] {'z'}, dimensions={0}, use_global_device_ids=true | all-gather | bytes 479232 | tf_op jit(solution)/shard_map/all_gather | solution.py:293
  51.1 2.4 %all_gather.7.img = bf16[384,1152]{1,0:T(8,128)(2,1)S(1)} all-gather(bf16[192,1152]{1,0:T(8,128)(2,1)S(1)} %all_gather.6), channel_id=1, replica_groups=mesh['y'=8,'x'=4,'core'=2,'z'=12] {'core'}, dimensions={0}, use_global_device_ids=true | all-gather | bytes 1327104 | tf_op jit(solution)/shard_map/all_gather | solution.py:294
  53.6 0.0 all-to-all-done
  53.6 1.7 %shard_map.78 = (bf16[512,384]{1,0:T(8,128)(2,1)S(1)}, f32[192,1152]{1,0:T(8,128)S(1)}, bf16[192,1152]{1,0:T(8,128)(2,1)S(1)}) custom-call(f32[1]{0:T(128)S(6)} %copy.8.log_temp, f32[1]{0:T(128)S(6)} %copy.9.bias, bf16[384,1152]{1,0:T(8,128)(2,1)S(1)} %all_gather.7.img, bf16[512,1152]{1,0:T(8,128)(2,1)S(1)} %bitcast.2), custom_call_target="tpu_custom_call" | custom-call | flops 905969664 | bytes 4128768 | tf_op jit(solution)/shard_map/pallas_call | solution.py:164
  55.3 2.0 %collective-permute-start = (bf16[192,1152]{1,0:T(8,128)(2,1)S(1)}, bf16[192,1152]{1,0:T(8,128)(2,1)S(1)}, u32[]{:S(2)}, u32[]{:S(2)}) collective-permute-start(bf16[192,1152]{1,0:T(8,128)(2,1)S(1)} %get-tuple-element.25), channel_id=1, source_target_pairs={{0,12},{12,0},{1,13},{13,1},{2,14},{14,2},{3,15},{15,3},{4,16},{16... | collective-permute-start | bytes 1327112 | tf_op jit(solution)/shard_map/ppermute | solution.py:286
  57.3 1.6 %shard_map.81 = bf16[512,1152]{1,0:T(8,128)(2,1)} custom-call(bf16[512,384]{1,0:T(8,128)(2,1)S(1)} %get-tuple-element.33.coef, bf16[384,1152]{1,0:T(8,128)(2,1)S(1)} %all_gather.7.img), custom_call_target="tpu_custom_call" | custom-call | flops 452984832 | bytes 4128768 | tf_op jit(solution)/shard_map/pallas_call | solution.py:197
  59.0 9.8 %all-to-all-start.1 = ((bf16[32,16,1152]{2,1,0:T(8,128)(2,1)}), bf16[32,16,1152]{2,1,0:T(8,128)(2,1)S(1)}, u32[]{:S(2)}, u32[]{:S(2)}) async-start(bf16[32,16,1152]{2,1,0:T(8,128)(2,1)} %bitcast.3), calls=%async_computation.1 | async-start | bytes 2359296 | tf_op jit(solution)/shard_map/all_to_all | solution.py:39
  68.8 0.0 collective-permute-done.refs_1_
  68.8 0.1 shard_map.79
  68.9 1.9 %collective-permute-start.1 = (bf16[48,1152]{1,0:T(8,128)(2,1)S(1)}, bf16[48,1152]{1,0:T(8,128)(2,1)S(1)}, u32[]{:S(2)}, u32[]{:S(2)}) collective-permute-start(bf16[48,1152]{1,0:T(8,128)(2,1)S(1)} %get-tuple-element.27), channel_id=1, source_target_pairs={{0,1},{1,2},{2,3},{3,4},{4,5},{5,6},{6,7},{7,8},{8,9},{9,10},{10,1... | collective-permute-start | bytes 331784 | tf_op jit(solution)/shard_map/ppermute | solution.py:286
  70.8 2.2 %collective-permute-start.2 = (bf16[48,1152]{1,0:T(8,128)(2,1)S(1)}, bf16[48,1152]{1,0:T(8,128)(2,1)S(1)}, u32[]{:S(2)}, u32[]{:S(2)}) collective-permute-start(bf16[48,1152]{1,0:T(8,128)(2,1)S(1)} %get-tuple-element.28), channel_id=1, source_target_pairs={{0,2},{1,3},{2,4},{3,5},{4,6},{5,7},{6,8},{7,9},{8,10},{9,11},{10,... | collective-permute-start | bytes 331784 | tf_op jit(solution)/shard_map/ppermute | solution.py:286
  73.0 5.1 %collective-permute-start.3 = (bf16[48,1152]{1,0:T(8,128)(2,1)S(1)}, bf16[48,1152]{1,0:T(8,128)(2,1)S(1)}, u32[]{:S(2)}, u32[]{:S(2)}) collective-permute-start(bf16[48,1152]{1,0:T(8,128)(2,1)S(1)} %get-tuple-element.29), channel_id=1, source_target_pairs={{0,11},{1,0},{2,1},{3,2},{4,3},{5,4},{6,5},{7,6},{8,7},{9,8},{10,9... | collective-permute-start | bytes 331784 | tf_op jit(solution)/shard_map/ppermute | solution.py:286
  78.1 0.0 collective-permute-done.1.refs_1_
  78.1 1.7 %collective-permute-done.2.refs_2_ = bf16[48,1152]{1,0:T(8,128)(2,1)S(1)} collective-permute-done((bf16[48,1152]{1,0:T(8,128)(2,1)S(1)}, bf16[48,1152]{1,0:T(8,128)(2,1)S(1)}, u32[]{:S(2)}, u32[]{:S(2)}) %collective-permute-start.2) | collective-permute-done | bytes 110624 | tf_op jit(solution)/shard_map/ppermute | solution.py:286
  79.8 0.6 collective-permute-done.3.refs_3_
  80.4 0.1 shard_map.80
  80.5 4.8 %collective-permute-start.4 = (bf16[16,1152]{1,0:T(8,128)(2,1)S(1)}, bf16[16,1152]{1,0:T(8,128)(2,1)S(1)}, u32[]{:S(2)}, u32[]{:S(2)}) collective-permute-start(bf16[16,1152]{1,0:T(8,128)(2,1)S(1)} %get-tuple-element.35), channel_id=1, source_target_pairs={{0,4},{1,5},{2,6},{3,7},{4,8},{5,9},{6,10},{7,11},{8,0},{9,1},{10,... | collective-permute-start | bytes 110600 | tf_op jit(solution)/shard_map/ppermute | solution.py:286
  85.3 4.9 %collective-permute-start.5 = (bf16[16,1152]{1,0:T(8,128)(2,1)S(1)}, bf16[16,1152]{1,0:T(8,128)(2,1)S(1)}, u32[]{:S(2)}, u32[]{:S(2)}) collective-permute-start(bf16[16,1152]{1,0:T(8,128)(2,1)S(1)} %get-tuple-element.36), channel_id=1, source_target_pairs={{0,8},{1,9},{2,10},{3,11},{4,0},{5,1},{6,2},{7,3},{8,4},{9,5},{10,... | collective-permute-start | bytes 110600 | tf_op jit(solution)/shard_map/ppermute | solution.py:286
  90.2 9.9 %all-to-all-done.1.refs_0_ = bf16[32,16,1152]{2,1,0:T(8,128)(2,1)S(1)} async-done(((bf16[32,16,1152]{2,1,0:T(8,128)(2,1)}), bf16[32,16,1152]{2,1,0:T(8,128)(2,1)S(1)}, u32[]{:S(2)}, u32[]{:S(2)}) %all-to-all-start.1) | async-done | bytes 1179680 | tf_op jit(solution)/shard_map/all_to_all | solution.py:39
  100.2 2.8 %shard_map.82 = f32[16,1024]{1,0:T(8,128)} custom-call(f32[16,1152]{1,0:T(8,128)} %get-tuple-element.31.unit, f32[16,128]{1,0:T(8,128)S(1)} %get-tuple-element.32.inv, bf16[1024,1152]{1,0:T(8,128)(2,1)} %proj.2, bf16[32,16,1152]{2,1,0:T(8,128)(2,1)S(1)} %all-to-all-done.1.refs_0_), custom_call_target="tpu_custom_call" | custom-call | flops 37748736 | bytes 2359296 | tf_op jit(solution)/shard_map/pallas_call | solution.py:268
  103.0 0.0 collective-permute-done.4.refs_1_
  103.0 0.0 collective-permute-done.5.refs_2_
  103.0 3.3 %shard_map.83 = f32[16,1536]{1,0:T(8,128)} custom-call(f32[16,1152]{1,0:T(8,128)} %get-tuple-element.20.unit, f32[16,128]{1,0:T(8,128)S(1)} %get-tuple-element.21.inv, bf16[1536,1152]{1,0:T(8,128)(2,1)} %proj.3, f32[16,1152]{1,0:T(8,128)S(1)} %get-tuple-element.34.refs_0_, bf16[16,1152]{1,0:T(8,128)(2,1)S(1)} %collective-permute-done.4.refs_1_, ...), custom_call_target="tpu_custom_call" | custom-call | flops 56623104 | bytes 3538944 | tf_op jit(solution)/shard_map/pallas_call | solution.py:268
Async XLA Ops:
  4.8 48.8 %all-to-all-start = ((bf16[32,16,1152]{2,1,0:T(8,128)(2,1)}), bf16[32,16,1152]{2,1,0:T(8,128)(2,1)S(1)}, u32[]{:S(2)}, u32[]{:S(2)}) async-start(bf16[32,16,1152]{2,1,0:T(8,128)(2,1)} %get-tuple-element.23), calls=%async_computation | async-start | bytes 2359296 | tf_op jit(solution)/shard_map/all_to_all | solution.py:39
  55.3 13.5 %collective-permute-start = (bf16[192,1152]{1,0:T(8,128)(2,1)S(1)}, bf16[192,1152]{1,0:T(8,128)(2,1)S(1)}, u32[]{:S(2)}, u32[]{:S(2)}) collective-permute-start(bf16[192,1152]{1,0:T(8,128)(2,1)S(1)} %get-tuple-element.25), channel_id=1, source_target_pairs={{0,12},{12,0},{1,13},{13,1},{2,14},{14,2},{3,15},{15,3},{4,16},{16... | collective-permute-start | bytes 1327112 | tf_op jit(solution)/shard_map/ppermute | solution.py:286
  59.0 41.2 %all-to-all-start.1 = ((bf16[32,16,1152]{2,1,0:T(8,128)(2,1)}), bf16[32,16,1152]{2,1,0:T(8,128)(2,1)S(1)}, u32[]{:S(2)}, u32[]{:S(2)}) async-start(bf16[32,16,1152]{2,1,0:T(8,128)(2,1)} %bitcast.3), calls=%async_computation.1 | async-start | bytes 2359296 | tf_op jit(solution)/shard_map/all_to_all | solution.py:39
  68.9 9.2 %collective-permute-start.1 = (bf16[48,1152]{1,0:T(8,128)(2,1)S(1)}, bf16[48,1152]{1,0:T(8,128)(2,1)S(1)}, u32[]{:S(2)}, u32[]{:S(2)}) collective-permute-start(bf16[48,1152]{1,0:T(8,128)(2,1)S(1)} %get-tuple-element.27), channel_id=1, source_target_pairs={{0,1},{1,2},{2,3},{3,4},{4,5},{5,6},{6,7},{7,8},{8,9},{9,10},{10,1... | collective-permute-start | bytes 331784 | tf_op jit(solution)/shard_map/ppermute | solution.py:286
  70.8 9.0 %collective-permute-start.2 = (bf16[48,1152]{1,0:T(8,128)(2,1)S(1)}, bf16[48,1152]{1,0:T(8,128)(2,1)S(1)}, u32[]{:S(2)}, u32[]{:S(2)}) collective-permute-start(bf16[48,1152]{1,0:T(8,128)(2,1)S(1)} %get-tuple-element.28), channel_id=1, source_target_pairs={{0,2},{1,3},{2,4},{3,5},{4,6},{5,7},{6,8},{7,9},{8,10},{9,11},{10,... | collective-permute-start | bytes 331784 | tf_op jit(solution)/shard_map/ppermute | solution.py:286
  73.0 7.4 %collective-permute-start.3 = (bf16[48,1152]{1,0:T(8,128)(2,1)S(1)}, bf16[48,1152]{1,0:T(8,128)(2,1)S(1)}, u32[]{:S(2)}, u32[]{:S(2)}) collective-permute-start(bf16[48,1152]{1,0:T(8,128)(2,1)S(1)} %get-tuple-element.29), channel_id=1, source_target_pairs={{0,11},{1,0},{2,1},{3,2},{4,3},{5,4},{6,5},{7,6},{8,7},{9,8},{10,9... | collective-permute-start | bytes 331784 | tf_op jit(solution)/shard_map/ppermute | solution.py:286
  80.5 22.5 %collective-permute-start.4 = (bf16[16,1152]{1,0:T(8,128)(2,1)S(1)}, bf16[16,1152]{1,0:T(8,128)(2,1)S(1)}, u32[]{:S(2)}, u32[]{:S(2)}) collective-permute-start(bf16[16,1152]{1,0:T(8,128)(2,1)S(1)} %get-tuple-element.35), channel_id=1, source_target_pairs={{0,4},{1,5},{2,6},{3,7},{4,8},{5,9},{6,10},{7,11},{8,0},{9,1},{10,... | collective-permute-start | bytes 110600 | tf_op jit(solution)/shard_map/ppermute | solution.py:286
  85.3 17.7 %collective-permute-start.5 = (bf16[16,1152]{1,0:T(8,128)(2,1)S(1)}, bf16[16,1152]{1,0:T(8,128)(2,1)S(1)}, u32[]{:S(2)}, u32[]{:S(2)}) collective-permute-start(bf16[16,1152]{1,0:T(8,128)(2,1)S(1)} %get-tuple-element.36), channel_id=1, source_target_pairs={{0,8},{1,9},{2,10},{3,11},{4,0},{5,1},{6,2},{7,3},{8,4},{9,5},{10,... | collective-permute-start | bytes 110600 | tf_op jit(solution)/shard_map/ppermute | solution.py:286

commit v7 on v5

v7 whole, which is shorter than its diff:
```python
import functools

import jax
import jax.numpy as jnp
import numpy as np
from jax import lax
from jax.experimental import pallas as pl
from jax.experimental.pallas import tpu as pltpu
from jax.sharding import Mesh
from jax.sharding import PartitionSpec as P

loss_scale = 65536.0
eps = 1e-06
f32 = jnp.float32
bf16 = jnp.bfloat16

vmem = pl.BlockSpec(memory_space=pltpu.VMEM)
smem = pl.BlockSpec(memory_space=pltpu.SMEM)
hbm = pl.BlockSpec(memory_space=pltpu.HBM)
params = pltpu.CompilerParams(vmem_limit_bytes=24 * 2**20)


def far_off(x):
    return pltpu.with_memory_space_constraint(x, pltpu.HBM)

ahead = (0, 4, 8, 1, 5, 9, 2, 6, 10, 11, 3, 7)


def cost(flops, moved, transcendentals=0):
    return pl.CostEstimate(flops=flops, bytes_accessed=moved, transcendentals=transcendentals)


def shift(axis, by):
    n = lax.axis_size(axis)
    return [(i, (i + by) % n) for i in range(n)]


def exchanged(copies, axis):
    return lax.all_to_all(copies, axis, 0, 0, tiled=True)


def repeat_kernel(rows, out, buf, sems):
    read = pltpu.make_async_copy(rows, buf, sems.at[0])
    read.start()
    read.wait()
    writes = [pltpu.make_async_copy(buf, out.at[k], sems.at[k + 1]) for k in range(out.shape[0])]
    for write in writes:
        write.start()
    for write in writes:
        write.wait()


def repeated(rows, n):
    return pl.pallas_call(
        repeat_kernel,
        out_shape=pltpu.HBM((n,) + rows.shape, rows.dtype),
        in_specs=[hbm],
        out_specs=hbm,
        scratch_shapes=[pltpu.VMEM(rows.shape, rows.dtype), pltpu.SemaphoreType.DMA((n + 1,))],
        cost_estimate=cost(0, 2 * n * rows.size),
        compiler_params=params,
    )(far_off(rows))


def normed(emb):
    inv = lax.rsqrt(jnp.sum(emb * emb, axis=1, keepdims=True) + eps)
    return emb * inv, inv


def embed_kernel(feats, proj, unit_out, inv_out, rows_out, buf, weights, unit_buf, sems):
    cuts, cut = weights.shape[:2]
    reads = [pltpu.make_async_copy(feats, buf, sems.at[cuts])]
    for k in range(cuts):
        reads.append(pltpu.make_async_copy(proj.at[pl.ds(k * cut, cut)], weights.at[k], sems.at[k]))
    for read in reads:
        read.start()
    reads[0].wait()
    emb = jnp.zeros(rows_out.shape, f32)
    for k in range(cuts):
        reads[k + 1].wait()
        emb += jnp.dot(buf[:, k * cut : (k + 1) * cut], weights[k], preferred_element_type=f32)
    unit, inv = normed(emb)
    unit_buf[...] = unit
    write = pltpu.make_async_copy(unit_buf, unit_out, sems.at[cuts + 1])
    write.start()
    rows_out[...] = unit.astype(bf16)
    inv_out[...] = jnp.broadcast_to(inv, inv_out.shape)
    write.wait()


def embed(feats, proj):
    own, depth = feats.shape
    width = proj.shape[1]
    cut = 512
    return pl.pallas_call(
        embed_kernel,
        out_shape=[
            pltpu.HBM((own, width), f32),
            jax.ShapeDtypeStruct((own, 128), f32),
            jax.ShapeDtypeStruct((own, width), bf16),
        ],
        in_specs=[hbm, hbm],
        out_specs=[hbm, vmem, vmem],
        scratch_shapes=[
            pltpu.VMEM(feats.shape, bf16),
            pltpu.VMEM((depth // cut, cut, width), bf16),
            pltpu.VMEM((own, width), f32),
            pltpu.SemaphoreType.DMA((depth // cut + 2,)),
        ],
        cost_estimate=cost(2 * own * depth * width, 2 * depth * width),
        compiler_params=params,
    )(far_off(feats), far_off(proj))


def tile_kernel(own, factor, log_temp, bias, img, feats, proj, *refs):
    unit_out, inv_out, coef_out, near_out, far_out, units, invs, terms, sem = refs
    nz = len(ahead)
    core = lax.axis_index("core")
    z = lax.axis_index("z")
    first_img = (core * nz + z) * own
    first_txt = lax.axis_index(("y", "x")) * own
    temp = jnp.exp(jnp.full((1, img.shape[0]), log_temp[0], f32))
    factor = factor * temp
    rows = img[...]
    weights = proj[...]
    size = min(256, feats.shape[0])
    total = 0.0
    for at in range(0, feats.shape[0], size):
        part = slice(at, at + size)
        unit, inv = normed(jnp.dot(feats[part], weights, preferred_element_type=f32))
        units[part] = unit
        invs[part] = jnp.broadcast_to(inv, (size, 128))
        txt = unit.astype(bf16)
        logits = (
            lax.dot_general(txt, rows, (((1,), (1,)), ((), ())), preferred_element_type=f32) * temp
            + bias[0]
        )
        txt_ids = lax.broadcasted_iota(jnp.int32, logits.shape, 0) + (at - first_txt)
        img_ids = lax.broadcasted_iota(jnp.int32, logits.shape, 1) - first_img
        diag = ((txt_ids == img_ids) & (img_ids >= 0) & (img_ids < own)).astype(f32)
        coef = (factor * (jax.nn.sigmoid(logits) - diag)).astype(bf16)
        coef_out[part] = coef
        total = total + lax.dot_general(
            coef, txt, (((0,), (0,)), ((), ())), preferred_element_type=f32
        )
    mine = pl.ds(pl.multiple_of(first_txt, own), own)
    write = pltpu.make_async_copy(units.at[mine], unit_out, sem)
    write.start()
    inv_out[...] = invs[mine]
    terms[...] = total
    half = nz * own
    for k, by in enumerate(ahead):
        owner = lax.rem(z + by, nz) * own
        near = pl.multiple_of(core * half + owner, own)
        far = pl.multiple_of((1 - core) * half + owner, own)
        near_out[pl.ds(k * own, own)] = terms[pl.ds(near, own)]
        far_out[pl.ds(k * own, own)] = terms[pl.ds(far, own)].astype(bf16)
    write.wait()


def tile(own, log_temp, bias, factor, img, feats, proj):
    m = feats.shape[0]
    i, w = img.shape
    return pl.pallas_call(
        functools.partial(tile_kernel, own, factor),
        out_shape=[
            pltpu.HBM((own, w), f32),
            jax.ShapeDtypeStruct((own, 128), f32),
            jax.ShapeDtypeStruct((m, i), bf16),
            jax.ShapeDtypeStruct((i // 2, w), f32),
            jax.ShapeDtypeStruct((i // 2, w), bf16),
        ],
        in_specs=[smem, smem, vmem, vmem, vmem],
        out_specs=[hbm, vmem, vmem, vmem, vmem],
        scratch_shapes=[
            pltpu.VMEM((m, w), f32),
            pltpu.VMEM((m, 128), f32),
            pltpu.VMEM((i, w), f32),
            pltpu.SemaphoreType.DMA,
        ],
        cost_estimate=cost(4 * i * m * w + 2 * feats.size * w, 4 * (i + m) * w, i * m),
        compiler_params=params,
    )(log_temp, bias, img, feats, proj)


def text_kernel(coef, img, out, buf, sems):
    rows = img[...]
    parts, size = buf.shape[:2]
    writes = []
    for q in range(parts):
        buf[q] = jnp.dot(
            coef[q * size : (q + 1) * size], rows, preferred_element_type=f32
        ).astype(bf16)
        writes.append(pltpu.make_async_copy(buf.at[q], out.at[pl.ds(q * size, size)], sems.at[q]))
        writes[-1].start()
    for write in writes:
        write.wait()


def text_terms(coef, img):
    m, i = coef.shape
    w = img.shape[1]
    parts = 2
    return pl.pallas_call(
        text_kernel,
        out_shape=pltpu.HBM((m, w), bf16),
        in_specs=[vmem, vmem],
        out_specs=hbm,
        scratch_shapes=[
            pltpu.VMEM((parts, m // parts, w), bf16),
            pltpu.SemaphoreType.DMA((parts,)),
        ],
        cost_estimate=cost(2 * i * m * w, 4 * (i + m) * w),
        compiler_params=params,
    )(coef, img)


def fold_kernel(n, *refs):
    parts, outs = refs[:n], refs[n:]
    at = 0
    for out in outs:
        rows = slice(at, at + out.shape[0])
        total = parts[0][rows]
        for part in parts[1:]:
            total = total + part[rows].astype(f32)
        out[...] = total.astype(out.dtype)
        at += out.shape[0]


def fold(size, *parts):
    n, w = parts[0].shape
    work = 10**10
    return pl.pallas_call(
        functools.partial(fold_kernel, len(parts)),
        out_shape=[
            jax.ShapeDtypeStruct((size, w), f32 if k == 0 else bf16) for k in range(n // size)
        ],
        in_specs=[vmem] * len(parts),
        out_specs=[vmem] * (n // size),
        cost_estimate=cost(work, 10 * n * w),
        compiler_params=params,
    )(*parts)


def backprop_kernel(unit, inv, proj, *refs):
    *parts, out, unit_buf, proj_buf, sems = refs
    cuts, cut = proj_buf.shape[:2]
    reads = [pltpu.make_async_copy(unit, unit_buf, sems.at[cuts])]
    for k in range(cuts):
        reads.append(pltpu.make_async_copy(proj.at[pl.ds(k * cut, cut)], proj_buf.at[k], sems.at[k]))
    for read in reads:
        read.start()
    total = 0.0
    for part in parts:
        if len(part.shape) == 2:
            total = total + part[...].astype(f32)
        else:
            for k in range(part.shape[0]):
                total = total + part[k].astype(f32)
    reads[0].wait()
    rows = unit_buf[...]
    along = jnp.sum(rows * total, axis=1, keepdims=True)
    delta = (inv[:, :1] * (total - rows * along)).astype(bf16)
    for k in range(cuts):
        reads[k + 1].wait()
        out[:, k * cut : (k + 1) * cut] = lax.dot_general(
            delta, proj_buf[k], (((1,), (1,)), ((), ())), preferred_element_type=f32
        )


def backprop(unit, inv, proj, *parts):
    depth, width = proj.shape
    own = unit.shape[0]
    cut = 512
    return pl.pallas_call(
        backprop_kernel,
        out_shape=jax.ShapeDtypeStruct((own, depth), f32),
        in_specs=[hbm, vmem, hbm] + [vmem] * len(parts),
        out_specs=vmem,
        scratch_shapes=[
            pltpu.VMEM(unit.shape, f32),
            pltpu.VMEM((depth // cut, cut, width), bf16),
            pltpu.SemaphoreType.DMA((depth // cut + 1,)),
        ],
        cost_estimate=cost(2 * own * depth * width, 2 * depth * width),
        compiler_params=params,
    )(far_off(unit), inv, far_off(proj), *parts)


def shards(image_feats, text_feats, image_proj, text_proj, log_temp, logit_bias):
    own = text_feats.shape[0]
    total = own * lax.axis_size(("y", "x", "core", "z"))
    send = lambda rows, axis, by: lax.ppermute(rows, axis, shift(axis, by))

    plane = ("y", "x")
    feats = exchanged(repeated(text_feats, lax.axis_size(plane)), plane)
    feats = feats.reshape(-1, text_feats.shape[1])
    img_unit, img_inv, img_rows = embed(image_feats, image_proj)
    img_rows = lax.all_gather(img_rows, "z", tiled=True)
    img_rows = lax.all_gather(img_rows, "core", tiled=True)

    txt_unit, txt_inv, coef, near, far = tile(
        own, log_temp, logit_bias, loss_scale / total, img_rows, feats, text_proj
    )
    far = send(far, "core", 1)
    txt_terms = text_terms(coef, img_rows)
    txt_terms = exchanged(txt_terms.reshape(-1, own, txt_terms.shape[1]), plane)
    near, by1, by2, back = fold(3 * own, near, far)
    near, by4, by8 = fold(
        own, near, send(by1, "z", 1), send(by2, "z", 2), send(back, "z", -1)
    )
    image_grad = backprop(
        img_unit, img_inv, image_proj, near, send(by4, "z", 4), send(by8, "z", 8)
    )
    text_grad = backprop(txt_unit, txt_inv, text_proj, txt_terms)
    return (image_grad, text_grad)


def solution(mesh):
    blk, grp = mesh.devices.shape
    fine = Mesh(np.asarray(mesh.devices).reshape(blk // 8, 4, 2, grp), ("y", "x", "core", "z"))
    rows = P(("y", "x", "core", "z"), None)
    return jax.shard_map(
        shards,
        mesh=fine,
        in_specs=(rows, rows, P(), P(), P(), P()),
        out_specs=(rows, rows),
        check_vma=False,
    )
```

time: 107 us -> 109 us (1.019)
  Pallas kernels: 16.9 us -> 18.6 us
    pallas_call x1 -> x2, Pallas kernels: 1.67 us -> 7.47 us  [the longest x1 5.43 us: tile(): pl.pallas_call(functools.partial(tile_kernel, own, factor), out_shape=[pl...]
    pallas_call x2 -> x1, Pallas kernels: 6.59 us -> 3.26 us  [embed(): pl.pallas_call(embed_kernel, out_shape=[pltpu.HBM((own, width), f32), jax...]
    ppermute x6, waiting for transfers between devices: 9.05 us -> 7.35 us  [shards(): send = lambda rows, axis, by: lax.ppermute(rows, axis, shift(axis, by))]
    all_to_all x2, waiting for transfers between devices: 0.01 us -> 1.62 us  [exchanged(): return lax.all_to_all(copies, axis, 0, 0, tiled=True)]
  transfers between devices with their start and end apart: 8 -> 8, of which waited for: 5 -> 3; matrix products, arithmetic and copies ran while one was open for 0% -> 0% of each run, Pallas kernels for 4% -> 8%
where the time goes in v7:
time: 109 us; the launch traced here: 108 us
  starting transfers between devices  44.7 us (41%)
  blocking collectives  33.9 us (31%)
  Pallas kernels  18.6 us (17%)
  waiting for transfers between devices  8.97 us (8%)
  between operations  2.1 us (2%)
    all_gather x1, blocking collectives, shards(): img_rows = lax.all_gather(img_rows, 'z', tiled=True)  31.4 us
    all_to_all x2, starting transfers between devices, exchanged(): return lax.all_to_all(copies, axis, 0, 0, tiled=True)  23.7 us
    ppermute x6, starting transfers between devices, shards(): send = lambda rows, axis, by: lax.ppermute(rows, axis, shift(axis, by))  21 us
    ppermute x6, waiting for transfers between devices, shards(): send = lambda rows, axis, by: lax.ppermute(rows, axis, shift(axis, by))  7.35 us
    pallas_call x2, Pallas kernels, backprop(): pl.pallas_call(backprop_kernel, out_shape=jax.ShapeDtypeStruct((own, dept...  6.06 us
    pallas_call x1, Pallas kernels, tile(): pl.pallas_call(functools.partial(tile_kernel, own, factor), out_shape=[pl...  5.43 us
    pallas_call x1, Pallas kernels, embed(): pl.pallas_call(embed_kernel, out_shape=[pltpu.HBM((own, width), f32), jax...  3.26 us
    all_gather x1, blocking collectives, shards(): img_rows = lax.all_gather(img_rows, 'core', tiled=True)  2.43 us
  transfers between devices with their start and end apart: 8, of which 3 were waited for; matrix products, arithmetic and copies ran while one was open for 0% of the time, Pallas kernels for 8%

profile of v7, /device:TPU:6, one launch (start us, length us, event | category | flops | bytes accessed | tf_op | source)
XLA Modules:
  0.0 108.2 jit_solution(16535390168168478513)
XLA Ops:
  0.6 2.0 %shard_map.78 = bf16[32,16,1024]{2,1,0:T(8,128)(2,1)} custom-call(bf16[16,1024]{1,0:T(8,128)(2,1)} %rows.1), custom_call_target="tpu_custom_call" | custom-call | bytes 1048576 | tf_op jit(solution)/shard_map/pallas_call | solution.py:54
  2.7 13.8 %all-to-all-start = ((bf16[32,16,1024]{2,1,0:T(8,128)(2,1)}), bf16[32,16,1024]{2,1,0:T(8,128)(2,1)}, u32[]{:S(2)}, u32[]{:S(2)}) async-start(bf16[32,16,1024]{2,1,0:T(8,128)(2,1)} %shard_map.78), calls=%async_computation | async-start | bytes 2097152 | tf_op jit(solution)/shard_map/all_to_all | solution.py:39
  17.7 0.0 copy-start
  17.7 3.3 %shard_map.77 = (f32[16,1152]{1,0:T(8,128)}, f32[16,128]{1,0:T(8,128)S(1)}, bf16[16,1152]{1,0:T(8,128)(2,1)S(1)}) custom-call(bf16[16,1536]{1,0:T(8,128)(2,1)} %feats.1, bf16[1536,1152]{1,0:T(8,128)(2,1)} %proj.6), custom_call_target="tpu_custom_call" | custom-call | flops 56623104 | bytes 3538944 | tf_op jit(solution)/shard_map/pallas_call | solution.py:95
  21.0 31.4 %all_gather.6 = bf16[192,1152]{1,0:T(8,128)(2,1)S(1)} all-gather(bf16[16,1152]{1,0:T(8,128)(2,1)S(1)} %get-tuple-element.19), channel_id=1, replica_groups=mesh['y'=8,'x'=4,'core'=2,'z'=12] {'z'}, dimensions={0}, use_global_device_ids=true | all-gather | bytes 479232 | tf_op jit(solution)/shard_map/all_gather | solution.py:299
  52.5 2.4 %all_gather.7.img = bf16[384,1152]{1,0:T(8,128)(2,1)S(1)} all-gather(bf16[192,1152]{1,0:T(8,128)(2,1)S(1)} %all_gather.6), channel_id=1, replica_groups=mesh['y'=8,'x'=4,'core'=2,'z'=12] {'core'}, dimensions={0}, use_global_device_ids=true | all-gather | bytes 1327104 | tf_op jit(solution)/shard_map/all_gather | solution.py:300
  54.9 0.0 all-to-all-done
  54.9 0.0 copy-done
  54.9 5.4 %shard_map.79 = (f32[16,1152]{1,0:T(8,128)}, f32[16,128]{1,0:T(8,128)S(1)}, bf16[512,384]{1,0:T(8,128)(2,1)S(1)}, f32[192,1152]{1,0:T(8,128)S(1)}, bf16[192,1152]{1,0:T(8,128)(2,1)}) custom-call(f32[1]{0:T(128)S(6)} %copy.8.log_temp, f32[1]{0:T(128)S(6)} %copy.9.bias, bf16[384,1152]{1,0:T(8,128)(2,1)S(1)} %all_gather.7.img, bf16[512,1024]{1,0:T(8,128)(2,1)} %bitcast.feats, ...), custom_call_target="tpu_custom_call" | custom-call | flops 2113929216 | bytes 4128768 | tf_op jit(solution)/shard_map/pallas_call | solution.py:164
  60.3 0.0 copy-start.1
  60.3 2.0 %collective-permute-start = (bf16[192,1152]{1,0:T(8,128)(2,1)}, bf16[192,1152]{1,0:T(8,128)(2,1)S(1)}, u32[]{:S(2)}, u32[]{:S(2)}) collective-permute-start(bf16[192,1152]{1,0:T(8,128)(2,1)} %get-tuple-element.21), channel_id=1, source_target_pairs={{0,12},{12,0},{1,13},{13,1},{2,14},{14,2},{3,15},{15,3},{4,16},{16... | collective-permute-start | bytes 1327112 | tf_op jit(solution)/shard_map/ppermute | solution.py:293
  62.4 1.7 %shard_map.83 = bf16[512,1152]{1,0:T(8,128)(2,1)} custom-call(bf16[512,384]{1,0:T(8,128)(2,1)S(1)} %get-tuple-element.31.coef, bf16[384,1152]{1,0:T(8,128)(2,1)S(1)} %all_gather.7.img), custom_call_target="tpu_custom_call" | custom-call | flops 452984832 | bytes 4128768 | tf_op jit(solution)/shard_map/pallas_call | solution.py:204
  64.1 0.0 copy-done.1
  64.1 0.0 copy-start.2
  64.1 9.9 %all-to-all-start.1 = ((bf16[32,16,1152]{2,1,0:T(8,128)(2,1)}), bf16[32,16,1152]{2,1,0:T(8,128)(2,1)S(1)}, u32[]{:S(2)}, u32[]{:S(2)}) async-start(bf16[32,16,1152]{2,1,0:T(8,128)(2,1)} %bitcast.2), calls=%async_computation.1 | async-start | bytes 2359296 | tf_op jit(solution)/shard_map/all_to_all | solution.py:39
  74.0 0.0 collective-permute-done.refs_1_
  74.0 0.0 copy-done.2
  74.1 0.1 shard_map.80
  74.1 1.9 %collective-permute-start.1 = (bf16[48,1152]{1,0:T(8,128)(2,1)S(1)}, bf16[48,1152]{1,0:T(8,128)(2,1)S(1)}, u32[]{:S(2)}, u32[]{:S(2)}) collective-permute-start(bf16[48,1152]{1,0:T(8,128)(2,1)S(1)} %get-tuple-element.23), channel_id=1, source_target_pairs={{0,1},{1,2},{2,3},{3,4},{4,5},{5,6},{6,7},{7,8},{8,9},{9,10},{10,1... | collective-permute-start | bytes 331784 | tf_op jit(solution)/shard_map/ppermute | solution.py:293
  76.1 2.2 %collective-permute-start.2 = (bf16[48,1152]{1,0:T(8,128)(2,1)S(1)}, bf16[48,1152]{1,0:T(8,128)(2,1)S(1)}, u32[]{:S(2)}, u32[]{:S(2)}) collective-permute-start(bf16[48,1152]{1,0:T(8,128)(2,1)S(1)} %get-tuple-element.24), channel_id=1, source_target_pairs={{0,2},{1,3},{2,4},{3,5},{4,6},{5,7},{6,8},{7,9},{8,10},{9,11},{10,... | collective-permute-start | bytes 331784 | tf_op jit(solution)/shard_map/ppermute | solution.py:293
  78.2 5.1 %collective-permute-start.3 = (bf16[48,1152]{1,0:T(8,128)(2,1)S(1)}, bf16[48,1152]{1,0:T(8,128)(2,1)S(1)}, u32[]{:S(2)}, u32[]{:S(2)}) collective-permute-start(bf16[48,1152]{1,0:T(8,128)(2,1)S(1)} %get-tuple-element.25), channel_id=1, source_target_pairs={{0,11},{1,0},{2,1},{3,2},{4,3},{5,4},{6,5},{7,6},{8,7},{9,8},{10,9... | collective-permute-start | bytes 331784 | tf_op jit(solution)/shard_map/ppermute | solution.py:293
  83.4 0.0 collective-permute-done.1.refs_1_
  83.4 3.9 %collective-permute-done.2.refs_2_ = bf16[48,1152]{1,0:T(8,128)(2,1)S(1)} collective-permute-done((bf16[48,1152]{1,0:T(8,128)(2,1)S(1)}, bf16[48,1152]{1,0:T(8,128)(2,1)S(1)}, u32[]{:S(2)}, u32[]{:S(2)}) %collective-permute-start.2) | collective-permute-done | bytes 110624 | tf_op jit(solution)/shard_map/ppermute | solution.py:293
  87.2 0.0 collective-permute-done.3.refs_3_
  87.3 0.1 shard_map.81
  87.3 3.1 %collective-permute-start.4 = (bf16[16,1152]{1,0:T(8,128)(2,1)S(1)}, bf16[16,1152]{1,0:T(8,128)(2,1)S(1)}, u32[]{:S(2)}, u32[]{:S(2)}) collective-permute-start(bf16[16,1152]{1,0:T(8,128)(2,1)S(1)} %get-tuple-element.27), channel_id=1, source_target_pairs={{0,4},{1,5},{2,6},{3,7},{4,8},{5,9},{6,10},{7,11},{8,0},{9,1},{10,... | collective-permute-start | bytes 110600 | tf_op jit(solution)/shard_map/ppermute | solution.py:293
  90.4 6.7 %collective-permute-start.5 = (bf16[16,1152]{1,0:T(8,128)(2,1)S(1)}, bf16[16,1152]{1,0:T(8,128)(2,1)S(1)}, u32[]{:S(2)}, u32[]{:S(2)}) collective-permute-start(bf16[16,1152]{1,0:T(8,128)(2,1)S(1)} %get-tuple-element.28), channel_id=1, source_target_pairs={{0,8},{1,9},{2,10},{3,11},{4,0},{5,1},{6,2},{7,3},{8,4},{9,5},{10,... | collective-permute-start | bytes 110600 | tf_op jit(solution)/shard_map/ppermute | solution.py:293
  97.1 0.0 collective-permute-done.4.refs_1_
  97.1 3.4 %collective-permute-done.5.refs_2_ = bf16[16,1152]{1,0:T(8,128)(2,1)S(1)} collective-permute-done((bf16[16,1152]{1,0:T(8,128)(2,1)S(1)}, bf16[16,1152]{1,0:T(8,128)(2,1)S(1)}, u32[]{:S(2)}, u32[]{:S(2)}) %collective-permute-start.5) | collective-permute-done | bytes 36896 | tf_op jit(solution)/shard_map/ppermute | solution.py:293
  100.6 3.3 %shard_map.82 = f32[16,1536]{1,0:T(8,128)} custom-call(f32[16,1152]{1,0:T(8,128)} %get-tuple-element.17.unit, f32[16,128]{1,0:T(8,128)S(1)} %get-tuple-element.18.inv, bf16[1536,1152]{1,0:T(8,128)(2,1)} %proj.6, f32[16,1152]{1,0:T(8,128)S(1)} %get-tuple-element.26.refs_0_, bf16[16,1152]{1,0:T(8,128)(2,1)S(1)} %collective-permute-done.4.refs_1_, ...), custom_call_target="tpu_custom_call" | custom-call | flops 56623104 | bytes 3538944 | tf_op jit(solution)/shard_map/pallas_call | solution.py:275
  103.8 1.6 %all-to-all-done.1.refs_0_ = bf16[32,16,1152]{2,1,0:T(8,128)(2,1)S(1)} async-done(((bf16[32,16,1152]{2,1,0:T(8,128)(2,1)}), bf16[32,16,1152]{2,1,0:T(8,128)(2,1)S(1)}, u32[]{:S(2)}, u32[]{:S(2)}) %all-to-all-start.1) | async-done | bytes 1179680 | tf_op jit(solution)/shard_map/all_to_all | solution.py:39
  105.4 2.8 %shard_map.84 = f32[16,1024]{1,0:T(8,128)} custom-call(f32[16,1152]{1,0:T(8,128)} %get-tuple-element.29.unit, f32[16,128]{1,0:T(8,128)S(1)} %get-tuple-element.30.inv, bf16[1024,1152]{1,0:T(8,128)(2,1)} %proj.7, bf16[32,16,1152]{2,1,0:T(8,128)(2,1)S(1)} %all-to-all-done.1.refs_0_), custom_call_target="tpu_custom_call" | custom-call | flops 37748736 | bytes 2359296 | tf_op jit(solution)/shard_map/pallas_call | solution.py:275
Async XLA Ops:
  2.7 52.2 %all-to-all-start = ((bf16[32,16,1024]{2,1,0:T(8,128)(2,1)}), bf16[32,16,1024]{2,1,0:T(8,128)(2,1)}, u32[]{:S(2)}, u32[]{:S(2)}) async-start(bf16[32,16,1024]{2,1,0:T(8,128)(2,1)} %shard_map.78), calls=%async_computation | async-start | bytes 2097152 | tf_op jit(solution)/shard_map/all_to_all | solution.py:39
  17.7 37.2 %copy-start = (bf16[1024,1152]{1,0:T(8,128)(2,1)S(1)}, bf16[1024,1152]{1,0:T(8,128)(2,1)}, u32[]{:S(2)}) copy-start(bf16[1024,1152]{1,0:T(8,128)(2,1)} %proj.7) | copy-start | bytes 7077892
  60.3 3.7 %copy-start.1 = (f32[192,1152]{1,0:T(8,128)}, f32[192,1152]{1,0:T(8,128)S(1)}, u32[]{:S(2)}) copy-start(f32[192,1152]{1,0:T(8,128)S(1)} %get-tuple-element.20.refs_0_) | copy-start | bytes 2654212
  60.3 13.7 %collective-permute-start = (bf16[192,1152]{1,0:T(8,128)(2,1)}, bf16[192,1152]{1,0:T(8,128)(2,1)S(1)}, u32[]{:S(2)}, u32[]{:S(2)}) collective-permute-start(bf16[192,1152]{1,0:T(8,128)(2,1)} %get-tuple-element.21), channel_id=1, source_target_pairs={{0,12},{12,0},{1,13},{13,1},{2,14},{14,2},{3,15},{15,3},{4,16},{16... | collective-permute-start | bytes 1327112 | tf_op jit(solution)/shard_map/ppermute | solution.py:293
  64.1 10.0 %copy-start.2 = (f32[192,1152]{1,0:T(8,128)S(1)}, f32[192,1152]{1,0:T(8,128)}, u32[]{:S(2)}) copy-start(f32[192,1152]{1,0:T(8,128)} %copy-done.1) | copy-start | bytes 2654212
  64.1 41.4 %all-to-all-start.1 = ((bf16[32,16,1152]{2,1,0:T(8,128)(2,1)}), bf16[32,16,1152]{2,1,0:T(8,128)(2,1)S(1)}, u32[]{:S(2)}, u32[]{:S(2)}) async-start(bf16[32,16,1152]{2,1,0:T(8,128)(2,1)} %bitcast.2), calls=%async_computation.1 | async-start | bytes 2359296 | tf_op jit(solution)/shard_map/all_to_all | solution.py:39
  74.1 9.2 %collective-permute-start.1 = (bf16[48,1152]{1,0:T(8,128)(2,1)S(1)}, bf16[48,1152]{1,0:T(8,128)(2,1)S(1)}, u32[]{:S(2)}, u32[]{:S(2)}) collective-permute-start(bf16[48,1152]{1,0:T(8,128)(2,1)S(1)} %get-tuple-element.23), channel_id=1, source_target_pairs={{0,1},{1,2},{2,3},{3,4},{4,5},{5,6},{6,7},{7,8},{8,9},{9,10},{10,1... | collective-permute-start | bytes 331784 | tf_op jit(solution)/shard_map/ppermute | solution.py:293
  76.1 11.2 %collective-permute-start.2 = (bf16[48,1152]{1,0:T(8,128)(2,1)S(1)}, bf16[48,1152]{1,0:T(8,128)(2,1)S(1)}, u32[]{:S(2)}, u32[]{:S(2)}) collective-permute-start(bf16[48,1152]{1,0:T(8,128)(2,1)S(1)} %get-tuple-element.24), channel_id=1, source_target_pairs={{0,2},{1,3},{2,4},{3,5},{4,6},{5,7},{6,8},{7,9},{8,10},{9,11},{10,... | collective-permute-start | bytes 331784 | tf_op jit(solution)/shard_map/ppermute | solution.py:293
  78.2 9.0 %collective-permute-start.3 = (bf16[48,1152]{1,0:T(8,128)(2,1)S(1)}, bf16[48,1152]{1,0:T(8,128)(2,1)S(1)}, u32[]{:S(2)}, u32[]{:S(2)}) collective-permute-start(bf16[48,1152]{1,0:T(8,128)(2,1)S(1)} %get-tuple-element.25), channel_id=1, source_target_pairs={{0,11},{1,0},{2,1},{3,2},{4,3},{5,4},{6,5},{7,6},{8,7},{9,8},{10,9... | collective-permute-start | bytes 331784 | tf_op jit(solution)/shard_map/ppermute | solution.py:293
  87.3 9.8 %collective-permute-start.4 = (bf16[16,1152]{1,0:T(8,128)(2,1)S(1)}, bf16[16,1152]{1,0:T(8,128)(2,1)S(1)}, u32[]{:S(2)}, u32[]{:S(2)}) collective-permute-start(bf16[16,1152]{1,0:T(8,128)(2,1)S(1)} %get-tuple-element.27), channel_id=1, source_target_pairs={{0,4},{1,5},{2,6},{3,7},{4,8},{5,9},{6,10},{7,11},{8,0},{9,1},{10,... | collective-permute-start | bytes 110600 | tf_op jit(solution)/shard_map/ppermute | solution.py:293
  90.4 10.2 %collective-permute-start.5 = (bf16[16,1152]{1,0:T(8,128)(2,1)S(1)}, bf16[16,1152]{1,0:T(8,128)(2,1)S(1)}, u32[]{:S(2)}, u32[]{:S(2)}) collective-permute-start(bf16[16,1152]{1,0:T(8,128)(2,1)S(1)} %get-tuple-element.28), channel_id=1, source_target_pairs={{0,8},{1,9},{2,10},{3,11},{4,0},{5,1},{6,2},{7,3},{8,4},{9,5},{10,... | collective-permute-start | bytes 110600 | tf_op jit(solution)/shard_map/ppermute | solution.py:293

commit v8 on v6

--- a/solution.py
+++ b/solution.py
@@ -303,10 +303,10 @@
     near, by4, by8 = fold(
         own, near, send(by1, "z", 1), send(by2, "z", 2), send(back, "z", -1)
     )
+    image_grad = backprop(
+        img_unit, img_inv, image_proj, near, send(by4, "z", 4), send(by8, "z", 8)
+    )
     text_grad = backprop(txt_unit, txt_inv, text_proj, txt_terms)
-    got = (send(by4, "z", 4), send(by8, "z", 8))
-    near, text_grad = lax.optimization_barrier((near, text_grad))
-    image_grad = backprop(img_unit, img_inv, image_proj, near, *got)
     return (image_grad, text_grad)
 
 

time: 107 us -> 104 us (0.972)
  waiting for transfers between devices: 12.2 us -> 8.98 us
    all_to_all x2, waiting for transfers between devices: 9.93 us -> 1.86 us  [exchanged(): return lax.all_to_all(copies, axis, 0, 0, tiled=True)]
    ppermute x6, waiting for transfers between devices: 2.31 us -> 7.12 us  [shards(): send = lambda rows, axis, by: lax.ppermute(rows, axis, shift(axis, by))]
  transfers between devices with their start and end apart: 8 -> 8, of which waited for: 3 -> 5; matrix products, arithmetic and copies ran while one was open for 0% -> 0% of each run, Pallas kernels for 4% -> 5%
where the time goes in v8:
time: 104 us; the launch traced here: 103 us
  starting transfers between devices  43.9 us (42%)
  blocking collectives  34.4 us (33%)
  Pallas kernels  13.7 us (13%)
  waiting for transfers between devices  8.98 us (9%)
  between operations  2.05 us (2%)
    all_gather x1, blocking collectives, shards(): img_rows = lax.all_gather(img_rows, 'z', tiled=True)  31.9 us
    all_to_all x2, starting transfers between devices, exchanged(): return lax.all_to_all(copies, axis, 0, 0, tiled=True)  22.9 us
    ppermute x6, starting transfers between devices, shards(): send = lambda rows, axis, by: lax.ppermute(rows, axis, shift(axis, by))  21 us
    ppermute x6, waiting for transfers between devices, shards(): send = lambda rows, axis, by: lax.ppermute(rows, axis, shift(axis, by))  7.12 us
    pallas_call x2, Pallas kernels, backprop(): pl.pallas_call(backprop_kernel, out_shape=jax.ShapeDtypeStruct((own, dept...  6.06 us
    pallas_call x1, Pallas kernels, embed(): pl.pallas_call(embed_kernel, out_shape=[unit, inv, pltpu.HBM((copies, own...  4.15 us
    all_gather x1, blocking collectives, shards(): img_rows = lax.all_gather(img_rows, 'core', tiled=True)  2.43 us
  transfers between devices with their start and end apart: 8, of which 5 were waited for; matrix products, arithmetic and copies ran while one was open for 0% of the time, Pallas kernels for 5%

profile of v8, /device:TPU:6, one launch (start us, length us, event | category | flops | bytes accessed | tf_op | source)
XLA Modules:
  0.0 103.0 jit_solution(1331168276055677546)
XLA Ops:
  0.6 4.2 %shard_map.77 = (f32[16,1152]{1,0:T(8,128)}, f32[16,128]{1,0:T(8,128)S(1)}, bf16[32,16,1152]{2,1,0:T(8,128)(2,1)}, f32[16,1152]{1,0:T(8,128)}, f32[16,128]{1,0:T(8,128)S(1)}, /*index=5*/bf16[16,1152]{1,0:T(8,128)(2,1)S(1)}) custom-call(bf16[16,1024]{1,0:T(8,128)(2,1)} %txt.1, bf16[1024,1152]{1,0:T(8,128)(2,1)} %proj.3, bf16[16,1536]{1,0:T(8,128)(2,1)} %img.1, ...), custom_call_target="tpu_custom_call" | custom-call | flops 94371840 | bytes 6291456 | tf_op jit(solution)/shard_map/pallas_call | solution.py:96
  4.8 13.1 %all-to-all-start = ((bf16[32,16,1152]{2,1,0:T(8,128)(2,1)}), bf16[32,16,1152]{2,1,0:T(8,128)(2,1)S(1)}, u32[]{:S(2)}, u32[]{:S(2)}) async-start(bf16[32,16,1152]{2,1,0:T(8,128)(2,1)} %get-tuple-element.21), calls=%async_computation | async-start | bytes 2359296 | tf_op jit(solution)/shard_map/all_to_all | solution.py:39
  19.2 31.9 %all_gather.6 = bf16[192,1152]{1,0:T(8,128)(2,1)S(1)} all-gather(bf16[16,1152]{1,0:T(8,128)(2,1)S(1)} %get-tuple-element.20), channel_id=1, replica_groups=mesh['y'=8,'x'=4,'core'=2,'z'=12] {'z'}, dimensions={0}, use_global_device_ids=true | all-gather | bytes 479232 | tf_op jit(solution)/shard_map/all_gather | solution.py:293
  51.1 2.4 %all_gather.7.img = bf16[384,1152]{1,0:T(8,128)(2,1)S(1)} all-gather(bf16[192,1152]{1,0:T(8,128)(2,1)S(1)} %all_gather.6), channel_id=1, replica_groups=mesh['y'=8,'x'=4,'core'=2,'z'=12] {'core'}, dimensions={0}, use_global_device_ids=true | all-gather | bytes 1327104 | tf_op jit(solution)/shard_map/all_gather | solution.py:294
  53.6 0.0 all-to-all-done
  53.6 1.7 %shard_map.78 = (bf16[512,384]{1,0:T(8,128)(2,1)S(1)}, f32[192,1152]{1,0:T(8,128)S(1)}, bf16[192,1152]{1,0:T(8,128)(2,1)S(1)}) custom-call(f32[1]{0:T(128)S(6)} %copy.8.log_temp, f32[1]{0:T(128)S(6)} %copy.9.bias, bf16[384,1152]{1,0:T(8,128)(2,1)S(1)} %all_gather.7.img, bf16[512,1152]{1,0:T(8,128)(2,1)S(1)} %bitcast.2), custom_call_target="tpu_custom_call" | custom-call | flops 905969664 | bytes 4128768 | tf_op jit(solution)/shard_map/pallas_call | solution.py:164
  55.3 2.0 %collective-permute-start = (bf16[192,1152]{1,0:T(8,128)(2,1)S(1)}, bf16[192,1152]{1,0:T(8,128)(2,1)S(1)}, u32[]{:S(2)}, u32[]{:S(2)}) collective-permute-start(bf16[192,1152]{1,0:T(8,128)(2,1)S(1)} %get-tuple-element.23), channel_id=1, source_target_pairs={{0,12},{12,0},{1,13},{13,1},{2,14},{14,2},{3,15},{15,3},{4,16},{16... | collective-permute-start | bytes 1327112 | tf_op jit(solution)/shard_map/ppermute | solution.py:286
  57.3 1.6 %shard_map.82 = bf16[512,1152]{1,0:T(8,128)(2,1)} custom-call(bf16[512,384]{1,0:T(8,128)(2,1)S(1)} %get-tuple-element.33.coef, bf16[384,1152]{1,0:T(8,128)(2,1)S(1)} %all_gather.7.img), custom_call_target="tpu_custom_call" | custom-call | flops 452984832 | bytes 4128768 | tf_op jit(solution)/shard_map/pallas_call | solution.py:197
  59.0 9.8 %all-to-all-start.1 = ((bf16[32,16,1152]{2,1,0:T(8,128)(2,1)}), bf16[32,16,1152]{2,1,0:T(8,128)(2,1)S(1)}, u32[]{:S(2)}, u32[]{:S(2)}) async-start(bf16[32,16,1152]{2,1,0:T(8,128)(2,1)} %bitcast.3), calls=%async_computation.1 | async-start | bytes 2359296 | tf_op jit(solution)/shard_map/all_to_all | solution.py:39
  68.8 0.0 collective-permute-done.refs_1_
  68.8 0.1 shard_map.79
  68.9 1.9 %collective-permute-start.1 = (bf16[48,1152]{1,0:T(8,128)(2,1)S(1)}, bf16[48,1152]{1,0:T(8,128)(2,1)S(1)}, u32[]{:S(2)}, u32[]{:S(2)}) collective-permute-start(bf16[48,1152]{1,0:T(8,128)(2,1)S(1)} %get-tuple-element.25), channel_id=1, source_target_pairs={{0,1},{1,2},{2,3},{3,4},{4,5},{5,6},{6,7},{7,8},{8,9},{9,10},{10,1... | collective-permute-start | bytes 331784 | tf_op jit(solution)/shard_map/ppermute | solution.py:286
  70.8 2.2 %collective-permute-start.2 = (bf16[48,1152]{1,0:T(8,128)(2,1)S(1)}, bf16[48,1152]{1,0:T(8,128)(2,1)S(1)}, u32[]{:S(2)}, u32[]{:S(2)}) collective-permute-start(bf16[48,1152]{1,0:T(8,128)(2,1)S(1)} %get-tuple-element.26), channel_id=1, source_target_pairs={{0,2},{1,3},{2,4},{3,5},{4,6},{5,7},{6,8},{7,9},{8,10},{9,11},{10,... | collective-permute-start | bytes 331784 | tf_op jit(solution)/shard_map/ppermute | solution.py:286
  73.0 5.1 %collective-permute-start.3 = (bf16[48,1152]{1,0:T(8,128)(2,1)S(1)}, bf16[48,1152]{1,0:T(8,128)(2,1)S(1)}, u32[]{:S(2)}, u32[]{:S(2)}) collective-permute-start(bf16[48,1152]{1,0:T(8,128)(2,1)S(1)} %get-tuple-element.27), channel_id=1, source_target_pairs={{0,11},{1,0},{2,1},{3,2},{4,3},{5,4},{6,5},{7,6},{8,7},{9,8},{10,9... | collective-permute-start | bytes 331784 | tf_op jit(solution)/shard_map/ppermute | solution.py:286
  78.1 0.0 collective-permute-done.1.refs_1_
  78.1 1.7 %collective-permute-done.2.refs_2_ = bf16[48,1152]{1,0:T(8,128)(2,1)S(1)} collective-permute-done((bf16[48,1152]{1,0:T(8,128)(2,1)S(1)}, bf16[48,1152]{1,0:T(8,128)(2,1)S(1)}, u32[]{:S(2)}, u32[]{:S(2)}) %collective-permute-start.2) | collective-permute-done | bytes 110624 | tf_op jit(solution)/shard_map/ppermute | solution.py:286
  79.8 0.6 collective-permute-done.3.refs_3_
  80.4 0.1 shard_map.80
  80.5 4.8 %collective-permute-start.4 = (bf16[16,1152]{1,0:T(8,128)(2,1)S(1)}, bf16[16,1152]{1,0:T(8,128)(2,1)S(1)}, u32[]{:S(2)}, u32[]{:S(2)}) collective-permute-start(bf16[16,1152]{1,0:T(8,128)(2,1)S(1)} %get-tuple-element.29), channel_id=1, source_target_pairs={{0,4},{1,5},{2,6},{3,7},{4,8},{5,9},{6,10},{7,11},{8,0},{9,1},{10,... | collective-permute-start | bytes 110600 | tf_op jit(solution)/shard_map/ppermute | solution.py:286
  85.3 4.9 %collective-permute-start.5 = (bf16[16,1152]{1,0:T(8,128)(2,1)S(1)}, bf16[16,1152]{1,0:T(8,128)(2,1)S(1)}, u32[]{:S(2)}, u32[]{:S(2)}) collective-permute-start(bf16[16,1152]{1,0:T(8,128)(2,1)S(1)} %get-tuple-element.30), channel_id=1, source_target_pairs={{0,8},{1,9},{2,10},{3,11},{4,0},{5,1},{6,2},{7,3},{8,4},{9,5},{10,... | collective-permute-start | bytes 110600 | tf_op jit(solution)/shard_map/ppermute | solution.py:286
  90.2 0.8 collective-permute-done.4.refs_1_
  91.0 4.0 %collective-permute-done.5.refs_2_ = bf16[16,1152]{1,0:T(8,128)(2,1)S(1)} collective-permute-done((bf16[16,1152]{1,0:T(8,128)(2,1)S(1)}, bf16[16,1152]{1,0:T(8,128)(2,1)S(1)}, u32[]{:S(2)}, u32[]{:S(2)}) %collective-permute-start.5) | collective-permute-done | bytes 36896 | tf_op jit(solution)/shard_map/ppermute | solution.py:286
  95.1 3.3 %shard_map.81 = f32[16,1536]{1,0:T(8,128)} custom-call(f32[16,1152]{1,0:T(8,128)} %get-tuple-element.18.unit, f32[16,128]{1,0:T(8,128)S(1)} %get-tuple-element.19.inv, bf16[1536,1152]{1,0:T(8,128)(2,1)} %proj.2, f32[16,1152]{1,0:T(8,128)S(1)} %get-tuple-element.28.refs_0_, bf16[16,1152]{1,0:T(8,128)(2,1)S(1)} %collective-permute-done.4.refs_1_, ...), custom_call_target="tpu_custom_call" | custom-call | flops 56623104 | bytes 3538944 | tf_op jit(solution)/shard_map/pallas_call | solution.py:268
  98.3 1.9 %all-to-all-done.1.refs_0_ = bf16[32,16,1152]{2,1,0:T(8,128)(2,1)S(1)} async-done(((bf16[32,16,1152]{2,1,0:T(8,128)(2,1)}), bf16[32,16,1152]{2,1,0:T(8,128)(2,1)S(1)}, u32[]{:S(2)}, u32[]{:S(2)}) %all-to-all-start.1) | async-done | bytes 1179680 | tf_op jit(solution)/shard_map/all_to_all | solution.py:39
  100.2 2.8 %shard_map.83 = f32[16,1024]{1,0:T(8,128)} custom-call(f32[16,1152]{1,0:T(8,128)} %get-tuple-element.31.unit, f32[16,128]{1,0:T(8,128)S(1)} %get-tuple-element.32.inv, bf16[1024,1152]{1,0:T(8,128)(2,1)} %proj.3, bf16[32,16,1152]{2,1,0:T(8,128)(2,1)S(1)} %all-to-all-done.1.refs_0_), custom_call_target="tpu_custom_call" | custom-call | flops 37748736 | bytes 2359296 | tf_op jit(solution)/shard_map/pallas_call | solution.py:268
Async XLA Ops:
  4.8 48.8 %all-to-all-start = ((bf16[32,16,1152]{2,1,0:T(8,128)(2,1)}), bf16[32,16,1152]{2,1,0:T(8,128)(2,1)S(1)}, u32[]{:S(2)}, u32[]{:S(2)}) async-start(bf16[32,16,1152]{2,1,0:T(8,128)(2,1)} %get-tuple-element.21), calls=%async_computation | async-start | bytes 2359296 | tf_op jit(solution)/shard_map/all_to_all | solution.py:39
  55.3 13.5 %collective-permute-start = (bf16[192,1152]{1,0:T(8,128)(2,1)S(1)}, bf16[192,1152]{1,0:T(8,128)(2,1)S(1)}, u32[]{:S(2)}, u32[]{:S(2)}) collective-permute-start(bf16[192,1152]{1,0:T(8,128)(2,1)S(1)} %get-tuple-element.23), channel_id=1, source_target_pairs={{0,12},{12,0},{1,13},{13,1},{2,14},{14,2},{3,15},{15,3},{4,16},{16... | collective-permute-start | bytes 1327112 | tf_op jit(solution)/shard_map/ppermute | solution.py:286
  59.0 41.2 %all-to-all-start.1 = ((bf16[32,16,1152]{2,1,0:T(8,128)(2,1)}), bf16[32,16,1152]{2,1,0:T(8,128)(2,1)S(1)}, u32[]{:S(2)}, u32[]{:S(2)}) async-start(bf16[32,16,1152]{2,1,0:T(8,128)(2,1)} %bitcast.3), calls=%async_computation.1 | async-start | bytes 2359296 | tf_op jit(solution)/shard_map/all_to_all | solution.py:39
  68.9 9.2 %collective-permute-start.1 = (bf16[48,1152]{1,0:T(8,128)(2,1)S(1)}, bf16[48,1152]{1,0:T(8,128)(2,1)S(1)}, u32[]{:S(2)}, u32[]{:S(2)}) collective-permute-start(bf16[48,1152]{1,0:T(8,128)(2,1)S(1)} %get-tuple-element.25), channel_id=1, source_target_pairs={{0,1},{1,2},{2,3},{3,4},{4,5},{5,6},{6,7},{7,8},{8,9},{9,10},{10,1... | collective-permute-start | bytes 331784 | tf_op jit(solution)/shard_map/ppermute | solution.py:286
  70.8 9.0 %collective-permute-start.2 = (bf16[48,1152]{1,0:T(8,128)(2,1)S(1)}, bf16[48,1152]{1,0:T(8,128)(2,1)S(1)}, u32[]{:S(2)}, u32[]{:S(2)}) collective-permute-start(bf16[48,1152]{1,0:T(8,128)(2,1)S(1)} %get-tuple-element.26), channel_id=1, source_target_pairs={{0,2},{1,3},{2,4},{3,5},{4,6},{5,7},{6,8},{7,9},{8,10},{9,11},{10,... | collective-permute-start | bytes 331784 | tf_op jit(solution)/shard_map/ppermute | solution.py:286
  73.0 7.4 %collective-permute-start.3 = (bf16[48,1152]{1,0:T(8,128)(2,1)S(1)}, bf16[48,1152]{1,0:T(8,128)(2,1)S(1)}, u32[]{:S(2)}, u32[]{:S(2)}) collective-permute-start(bf16[48,1152]{1,0:T(8,128)(2,1)S(1)} %get-tuple-element.27), channel_id=1, source_target_pairs={{0,11},{1,0},{2,1},{3,2},{4,3},{5,4},{6,5},{7,6},{8,7},{9,8},{10,9... | collective-permute-start | bytes 331784 | tf_op jit(solution)/shard_map/ppermute | solution.py:286
  80.5 10.6 %collective-permute-start.4 = (bf16[16,1152]{1,0:T(8,128)(2,1)S(1)}, bf16[16,1152]{1,0:T(8,128)(2,1)S(1)}, u32[]{:S(2)}, u32[]{:S(2)}) collective-permute-start(bf16[16,1152]{1,0:T(8,128)(2,1)S(1)} %get-tuple-element.29), channel_id=1, source_target_pairs={{0,4},{1,5},{2,6},{3,7},{4,8},{5,9},{6,10},{7,11},{8,0},{9,1},{10,... | collective-permute-start | bytes 110600 | tf_op jit(solution)/shard_map/ppermute | solution.py:286
  85.3 9.8 %collective-permute-start.5 = (bf16[16,1152]{1,0:T(8,128)(2,1)S(1)}, bf16[16,1152]{1,0:T(8,128)(2,1)S(1)}, u32[]{:S(2)}, u32[]{:S(2)}) collective-permute-start(bf16[16,1152]{1,0:T(8,128)(2,1)S(1)} %get-tuple-element.30), channel_id=1, source_target_pairs={{0,8},{1,9},{2,10},{3,11},{4,0},{5,1},{6,2},{7,3},{8,4},{9,5},{10,... | collective-permute-start | bytes 110600 | tf_op jit(solution)/shard_map/ppermute | solution.py:286

commit v9 on v8

--- a/solution.py
+++ b/solution.py
@@ -235,12 +235,18 @@
     )(*parts)
 
 
-def backprop_kernel(unit, inv, proj, *refs):
-    *parts, out, unit_buf, proj_buf, sems = refs
+def backprop_kernel(ahead_of, unit, inv, proj, *refs):
+    if ahead_of:
+        following, *refs = refs
+    *refs, unit_buf, proj_buf, sems = refs
     cuts, cut = proj_buf.shape[:2]
     reads = [pltpu.make_async_copy(unit, unit_buf, sems.at[cuts])]
     for k in range(cuts):
         reads.append(pltpu.make_async_copy(proj.at[pl.ds(k * cut, cut)], proj_buf.at[k], sems.at[k]))
+    if ahead_of:
+        *refs, following_out = refs
+        reads.append(pltpu.make_async_copy(following, following_out, sems.at[cuts + 1]))
+    *parts, out = refs
     for read in reads:
         read.start()
     total = 0.0
@@ -259,25 +265,56 @@
         out[:, k * cut : (k + 1) * cut] = lax.dot_general(
             delta, proj_buf[k], (((1,), (1,)), ((), ())), preferred_element_type=f32
         )
-
-
-def backprop(unit, inv, proj, *parts):
+    if ahead_of:
+        reads[-1].wait()
+
+
+def backprop(unit, inv, proj, parts, following=None):
     depth, width = proj.shape
     own = unit.shape[0]
     cut = 512
-    return pl.pallas_call(
-        backprop_kernel,
-        out_shape=jax.ShapeDtypeStruct((own, depth), f32),
-        in_specs=[hbm, vmem, hbm] + [vmem] * len(parts),
-        out_specs=vmem,
+    more = following is not None
+    outs = [jax.ShapeDtypeStruct((own, depth), f32)]
+    if more:
+        outs.append(jax.ShapeDtypeStruct(following.shape, bf16))
+    return pl.pallas_call(
+        functools.partial(backprop_kernel, more),
+        out_shape=outs,
+        in_specs=[hbm, vmem, hbm] + [hbm] * more + [vmem] * len(parts),
+        out_specs=[vmem] * len(outs),
         scratch_shapes=[
             pltpu.VMEM(unit.shape, f32),
             pltpu.VMEM((depth // cut, cut, width), bf16),
-            pltpu.SemaphoreType.DMA((depth // cut + 1,)),
+            pltpu.SemaphoreType.DMA((depth // cut + 2,)),
         ],
         cost_estimate=cost(2 * own * depth * width, 2 * depth * width),
         compiler_params=params,
-    )(far_off(unit), inv, far_off(proj), *parts)
+    )(far_off(unit), inv, far_off(proj), *([far_off(following)] * more), *parts)
+
+
+def last_kernel(unit, inv, proj, parts, out):
+    total = parts[0].astype(f32)
+    for k in range(1, parts.shape[0]):
+        total += parts[k].astype(f32)
+    rows = unit[...]
+    along = jnp.sum(rows * total, axis=1, keepdims=True)
+    delta = (inv[:, :1] * (total - rows * along)).astype(bf16)
+    out[...] = lax.dot_general(
+        delta, proj[...], (((1,), (1,)), ((), ())), preferred_element_type=f32
+    )
+
+
+def last_backprop(unit, inv, proj, parts):
+    depth, width = proj.shape
+    own = unit.shape[0]
+    return pl.pallas_call(
+        last_kernel,
+        out_shape=jax.ShapeDtypeStruct((own, depth), f32),
+        in_specs=[vmem] * 4,
+        out_specs=vmem,
+        cost_estimate=cost(2 * own * depth * width, 2 * depth * width),
+        compiler_params=params,
+    )(far_off(unit), inv, proj, parts)
 
 
 def shards(image_feats, text_feats, image_proj, text_proj, log_temp, logit_bias):
@@ -303,10 +340,9 @@
     near, by4, by8 = fold(
         own, near, send(by1, "z", 1), send(by2, "z", 2), send(back, "z", -1)
     )
-    image_grad = backprop(
-        img_unit, img_inv, image_proj, near, send(by4, "z", 4), send(by8, "z", 8)
-    )
-    text_grad = backprop(txt_unit, txt_inv, text_proj, txt_terms)
+    parts = (near, send(by4, "z", 4), send(by8, "z", 8))
+    image_grad, weights = backprop(img_unit, img_inv, image_proj, parts, text_proj)
+    text_grad = last_backprop(txt_unit, txt_inv, weights, txt_terms)
     return (image_grad, text_grad)
 
 

time: 104 us -> 103 us (level)
  no operation moved by 1% of the time
where the time goes in v9:
time: 103 us
  starting transfers between devices  43.9 us (43%)
  blocking collectives  34.4 us (33%)
  Pallas kernels  13.5 us (13%)
  waiting for transfers between devices  8.77 us (9%)
  between operations  2.05 us (2%)
    all_gather x1, blocking collectives, shards(): img_rows = lax.all_gather(img_rows, 'z', tiled=True)  31.9 us
    all_to_all x2, starting transfers between devices, exchanged(): return lax.all_to_all(copies, axis, 0, 0, tiled=True)  22.9 us
    ppermute x6, starting transfers between devices, shards(): send = lambda rows, axis, by: lax.ppermute(rows, axis, shift(axis, by))  21 us
    ppermute x6, waiting for transfers between devices, shards(): send = lambda rows, axis, by: lax.ppermute(rows, axis, shift(axis, by))  7.12 us
    pallas_call x1, Pallas kernels, embed(): pl.pallas_call(embed_kernel, out_shape=[unit, inv, pltpu.HBM((copies, own...  4.14 us
    pallas_call x1, Pallas kernels, backprop(): pl.pallas_call(functools.partial(backprop_kernel, more), out_shape=outs,...  3.46 us
    all_gather x1, blocking collectives, shards(): img_rows = lax.all_gather(img_rows, 'core', tiled=True)  2.43 us
    pallas_call x1, Pallas kernels, last_backprop(): pl.pallas_call(last_kernel, out_shape=jax.ShapeDtypeStruct((own, depth),...  2.42 us
  transfers between devices with their start and end apart: 8, of which 5 were waited for; matrix products, arithmetic and copies ran while one was open for 0% of the time, Pallas kernels for 5%

profile of v9, /device:TPU:6, one launch (start us, length us, event | category | flops | bytes accessed | tf_op | source)
XLA Modules:
  0.0 102.6 jit_solution(8906193449307366565)
XLA Ops:
  0.6 4.1 %shard_map.77 = (f32[16,1152]{1,0:T(8,128)}, f32[16,128]{1,0:T(8,128)S(1)}, bf16[32,16,1152]{2,1,0:T(8,128)(2,1)}, f32[16,1152]{1,0:T(8,128)}, f32[16,128]{1,0:T(8,128)S(1)}, /*index=5*/bf16[16,1152]{1,0:T(8,128)(2,1)S(1)}) custom-call(bf16[16,1024]{1,0:T(8,128)(2,1)} %txt.1, bf16[1024,1152]{1,0:T(8,128)(2,1)} %refs_0_.1, bf16[16,1536]{1,0:T(8,128)(2,1)} %img.1, ...), custom_call_target="tpu_custom_call" | custom-call | flops 94371840 | bytes 6291456 | tf_op jit(solution)/shard_map/pallas_call | solution.py:96
  4.8 13.1 %all-to-all-start = ((bf16[32,16,1152]{2,1,0:T(8,128)(2,1)}), bf16[32,16,1152]{2,1,0:T(8,128)(2,1)S(1)}, u32[]{:S(2)}, u32[]{:S(2)}) async-start(bf16[32,16,1152]{2,1,0:T(8,128)(2,1)} %get-tuple-element.23), calls=%async_computation | async-start | bytes 2359296 | tf_op jit(solution)/shard_map/all_to_all | solution.py:39
  19.2 31.9 %all_gather.6 = bf16[192,1152]{1,0:T(8,128)(2,1)S(1)} all-gather(bf16[16,1152]{1,0:T(8,128)(2,1)S(1)} %get-tuple-element.22), channel_id=1, replica_groups=mesh['y'=8,'x'=4,'core'=2,'z'=12] {'z'}, dimensions={0}, use_global_device_ids=true | all-gather | bytes 479232 | tf_op jit(solution)/shard_map/all_gather | solution.py:330
  51.1 2.4 %all_gather.7.img = bf16[384,1152]{1,0:T(8,128)(2,1)S(1)} all-gather(bf16[192,1152]{1,0:T(8,128)(2,1)S(1)} %all_gather.6), channel_id=1, replica_groups=mesh['y'=8,'x'=4,'core'=2,'z'=12] {'core'}, dimensions={0}, use_global_device_ids=true | all-gather | bytes 1327104 | tf_op jit(solution)/shard_map/all_gather | solution.py:331
  53.6 0.0 all-to-all-done
  53.6 1.7 %shard_map.78 = (bf16[512,384]{1,0:T(8,128)(2,1)S(1)}, f32[192,1152]{1,0:T(8,128)S(1)}, bf16[192,1152]{1,0:T(8,128)(2,1)S(1)}) custom-call(f32[1]{0:T(128)S(6)} %copy.8.log_temp, f32[1]{0:T(128)S(6)} %copy.9.bias, bf16[384,1152]{1,0:T(8,128)(2,1)S(1)} %all_gather.7.img, bf16[512,1152]{1,0:T(8,128)(2,1)S(1)} %bitcast.2), custom_call_target="tpu_custom_call" | custom-call | flops 905969664 | bytes 4128768 | tf_op jit(solution)/shard_map/pallas_call | solution.py:164
  55.2 2.0 %collective-permute-start = (bf16[192,1152]{1,0:T(8,128)(2,1)S(1)}, bf16[192,1152]{1,0:T(8,128)(2,1)S(1)}, u32[]{:S(2)}, u32[]{:S(2)}) collective-permute-start(bf16[192,1152]{1,0:T(8,128)(2,1)S(1)} %get-tuple-element.25), channel_id=1, source_target_pairs={{0,12},{12,0},{1,13},{13,1},{2,14},{14,2},{3,15},{15,3},{4,16},{16... | collective-permute-start | bytes 1327112 | tf_op jit(solution)/shard_map/ppermute | solution.py:323
  57.3 1.7 %shard_map.82 = bf16[512,1152]{1,0:T(8,128)(2,1)} custom-call(bf16[512,384]{1,0:T(8,128)(2,1)S(1)} %get-tuple-element.37.coef, bf16[384,1152]{1,0:T(8,128)(2,1)S(1)} %all_gather.7.img), custom_call_target="tpu_custom_call" | custom-call | flops 452984832 | bytes 4128768 | tf_op jit(solution)/shard_map/pallas_call | solution.py:197
  59.0 9.8 %all-to-all-start.1 = ((bf16[32,16,1152]{2,1,0:T(8,128)(2,1)}), bf16[32,16,1152]{2,1,0:T(8,128)(2,1)S(1)}, u32[]{:S(2)}, u32[]{:S(2)}) async-start(bf16[32,16,1152]{2,1,0:T(8,128)(2,1)} %bitcast.3), calls=%async_computation.1 | async-start | bytes 2359296 | tf_op jit(solution)/shard_map/all_to_all | solution.py:39
  68.8 0.0 collective-permute-done.refs_1_
  68.8 0.1 shard_map.79
  68.9 1.9 %collective-permute-start.1 = (bf16[48,1152]{1,0:T(8,128)(2,1)S(1)}, bf16[48,1152]{1,0:T(8,128)(2,1)S(1)}, u32[]{:S(2)}, u32[]{:S(2)}) collective-permute-start(bf16[48,1152]{1,0:T(8,128)(2,1)S(1)} %get-tuple-element.27), channel_id=1, source_target_pairs={{0,1},{1,2},{2,3},{3,4},{4,5},{5,6},{6,7},{7,8},{8,9},{9,10},{10,1... | collective-permute-start | bytes 331784 | tf_op jit(solution)/shard_map/ppermute | solution.py:323
  70.8 2.2 %collective-permute-start.2 = (bf16[48,1152]{1,0:T(8,128)(2,1)S(1)}, bf16[48,1152]{1,0:T(8,128)(2,1)S(1)}, u32[]{:S(2)}, u32[]{:S(2)}) collective-permute-start(bf16[48,1152]{1,0:T(8,128)(2,1)S(1)} %get-tuple-element.28), channel_id=1, source_target_pairs={{0,2},{1,3},{2,4},{3,5},{4,6},{5,7},{6,8},{7,9},{8,10},{9,11},{10,... | collective-permute-start | bytes 331784 | tf_op jit(solution)/shard_map/ppermute | solution.py:323
  73.0 5.1 %collective-permute-start.3 = (bf16[48,1152]{1,0:T(8,128)(2,1)S(1)}, bf16[48,1152]{1,0:T(8,128)(2,1)S(1)}, u32[]{:S(2)}, u32[]{:S(2)}) collective-permute-start(bf16[48,1152]{1,0:T(8,128)(2,1)S(1)} %get-tuple-element.29), channel_id=1, source_target_pairs={{0,11},{1,0},{2,1},{3,2},{4,3},{5,4},{6,5},{7,6},{8,7},{9,8},{10,9... | collective-permute-start | bytes 331784 | tf_op jit(solution)/shard_map/ppermute | solution.py:323
  78.1 0.0 collective-permute-done.1.refs_1_
  78.1 1.7 %collective-permute-done.2.refs_2_ = bf16[48,1152]{1,0:T(8,128)(2,1)S(1)} collective-permute-done((bf16[48,1152]{1,0:T(8,128)(2,1)S(1)}, bf16[48,1152]{1,0:T(8,128)(2,1)S(1)}, u32[]{:S(2)}, u32[]{:S(2)}) %collective-permute-start.2) | collective-permute-done | bytes 110624 | tf_op jit(solution)/shard_map/ppermute | solution.py:323
  79.8 0.6 collective-permute-done.3.refs_3_
  80.4 0.1 shard_map.80
  80.5 4.8 %collective-permute-start.4 = (bf16[16,1152]{1,0:T(8,128)(2,1)S(1)}, bf16[16,1152]{1,0:T(8,128)(2,1)S(1)}, u32[]{:S(2)}, u32[]{:S(2)}) collective-permute-start(bf16[16,1152]{1,0:T(8,128)(2,1)S(1)} %get-tuple-element.31), channel_id=1, source_target_pairs={{0,4},{1,5},{2,6},{3,7},{4,8},{5,9},{6,10},{7,11},{8,0},{9,1},{10,... | collective-permute-start | bytes 110600 | tf_op jit(solution)/shard_map/ppermute | solution.py:323
  85.3 4.9 %collective-permute-start.5 = (bf16[16,1152]{1,0:T(8,128)(2,1)S(1)}, bf16[16,1152]{1,0:T(8,128)(2,1)S(1)}, u32[]{:S(2)}, u32[]{:S(2)}) collective-permute-start(bf16[16,1152]{1,0:T(8,128)(2,1)S(1)} %get-tuple-element.32), channel_id=1, source_target_pairs={{0,8},{1,9},{2,10},{3,11},{4,0},{5,1},{6,2},{7,3},{8,4},{9,5},{10,... | collective-permute-start | bytes 110600 | tf_op jit(solution)/shard_map/ppermute | solution.py:323
  90.2 0.8 collective-permute-done.4.refs_2_
  91.0 4.0 %collective-permute-done.5.refs_3_ = bf16[16,1152]{1,0:T(8,128)(2,1)S(1)} collective-permute-done((bf16[16,1152]{1,0:T(8,128)(2,1)S(1)}, bf16[16,1152]{1,0:T(8,128)(2,1)S(1)}, u32[]{:S(2)}, u32[]{:S(2)}) %collective-permute-start.5) | collective-permute-done | bytes 36896 | tf_op jit(solution)/shard_map/ppermute | solution.py:323
  95.1 3.5 %shard_map.81 = (f32[16,1536]{1,0:T(8,128)}, bf16[1024,1152]{1,0:T(8,128)(2,1)S(1)}) custom-call(f32[16,1152]{1,0:T(8,128)} %get-tuple-element.20.unit, f32[16,128]{1,0:T(8,128)S(1)} %get-tuple-element.21.inv, bf16[1536,1152]{1,0:T(8,128)(2,1)} %proj.1, bf16[1024,1152]{1,0:T(8,128)(2,1)} %refs_0_.1, f32[16,1152]{1,0:T(8,128)S(1)} %get-tuple-element.30.refs_1_, ...), custom_call_target="tpu_custom_call" | custom-call | flops 56623104 | bytes 3538944 | tf_op jit(solution)/shard_map/pallas_call | solution.py:280
  98.5 1.6 %all-to-all-done.1.parts = bf16[32,16,1152]{2,1,0:T(8,128)(2,1)S(1)} async-done(((bf16[32,16,1152]{2,1,0:T(8,128)(2,1)}), bf16[32,16,1152]{2,1,0:T(8,128)(2,1)S(1)}, u32[]{:S(2)}, u32[]{:S(2)}) %all-to-all-start.1) | async-done | bytes 1179680 | tf_op jit(solution)/shard_map/all_to_all | solution.py:39
  100.2 2.4 %shard_map.83 = f32[16,1024]{1,0:T(8,128)} custom-call(f32[16,1152]{1,0:T(8,128)} %get-tuple-element.34.unit, f32[16,128]{1,0:T(8,128)S(1)} %get-tuple-element.35.inv, bf16[1024,1152]{1,0:T(8,128)(2,1)S(1)} %get-tuple-element.36.proj, bf16[32,16,1152]{2,1,0:T(8,128)(2,1)S(1)} %all-to-all-done.1.parts), custom_call_target="tpu_custom_call" | custom-call | flops 37748736 | bytes 2359296 | tf_op jit(solution)/shard_map/pallas_call | solution.py:310
Async XLA Ops:
  4.8 48.8 %all-to-all-start = ((bf16[32,16,1152]{2,1,0:T(8,128)(2,1)}), bf16[32,16,1152]{2,1,0:T(8,128)(2,1)S(1)}, u32[]{:S(2)}, u32[]{:S(2)}) async-start(bf16[32,16,1152]{2,1,0:T(8,128)(2,1)} %get-tuple-element.23), calls=%async_computation | async-start | bytes 2359296 | tf_op jit(solution)/shard_map/all_to_all | solution.py:39
  55.2 13.5 %collective-permute-start = (bf16[192,1152]{1,0:T(8,128)(2,1)S(1)}, bf16[192,1152]{1,0:T(8,128)(2,1)S(1)}, u32[]{:S(2)}, u32[]{:S(2)}) collective-permute-start(bf16[192,1152]{1,0:T(8,128)(2,1)S(1)} %get-tuple-element.25), channel_id=1, source_target_pairs={{0,12},{12,0},{1,13},{13,1},{2,14},{14,2},{3,15},{15,3},{4,16},{16... | collective-permute-start | bytes 1327112 | tf_op jit(solution)/shard_map/ppermute | solution.py:323
  59.0 41.2 %all-to-all-start.1 = ((bf16[32,16,1152]{2,1,0:T(8,128)(2,1)}), bf16[32,16,1152]{2,1,0:T(8,128)(2,1)S(1)}, u32[]{:S(2)}, u32[]{:S(2)}) async-start(bf16[32,16,1152]{2,1,0:T(8,128)(2,1)} %bitcast.3), calls=%async_computation.1 | async-start | bytes 2359296 | tf_op jit(solution)/shard_map/all_to_all | solution.py:39
  68.9 9.2 %collective-permute-start.1 = (bf16[48,1152]{1,0:T(8,128)(2,1)S(1)}, bf16[48,1152]{1,0:T(8,128)(2,1)S(1)}, u32[]{:S(2)}, u32[]{:S(2)}) collective-permute-start(bf16[48,1152]{1,0:T(8,128)(2,1)S(1)} %get-tuple-element.27), channel_id=1, source_target_pairs={{0,1},{1,2},{2,3},{3,4},{4,5},{5,6},{6,7},{7,8},{8,9},{9,10},{10,1... | collective-permute-start | bytes 331784 | tf_op jit(solution)/shard_map/ppermute | solution.py:323
  70.8 9.0 %collective-permute-start.2 = (bf16[48,1152]{1,0:T(8,128)(2,1)S(1)}, bf16[48,1152]{1,0:T(8,128)(2,1)S(1)}, u32[]{:S(2)}, u32[]{:S(2)}) collective-permute-start(bf16[48,1152]{1,0:T(8,128)(2,1)S(1)} %get-tuple-element.28), channel_id=1, source_target_pairs={{0,2},{1,3},{2,4},{3,5},{4,6},{5,7},{6,8},{7,9},{8,10},{9,11},{10,... | collective-permute-start | bytes 331784 | tf_op jit(solution)/shard_map/ppermute | solution.py:323
  73.0 7.4 %collective-permute-start.3 = (bf16[48,1152]{1,0:T(8,128)(2,1)S(1)}, bf16[48,1152]{1,0:T(8,128)(2,1)S(1)}, u32[]{:S(2)}, u32[]{:S(2)}) collective-permute-start(bf16[48,1152]{1,0:T(8,128)(2,1)S(1)} %get-tuple-element.29), channel_id=1, source_target_pairs={{0,11},{1,0},{2,1},{3,2},{4,3},{5,4},{6,5},{7,6},{8,7},{9,8},{10,9... | collective-permute-start | bytes 331784 | tf_op jit(solution)/shard_map/ppermute | solution.py:323
  80.5 10.6 %collective-permute-start.4 = (bf16[16,1152]{1,0:T(8,128)(2,1)S(1)}, bf16[16,1152]{1,0:T(8,128)(2,1)S(1)}, u32[]{:S(2)}, u32[]{:S(2)}) collective-permute-start(bf16[16,1152]{1,0:T(8,128)(2,1)S(1)} %get-tuple-element.31), channel_id=1, source_target_pairs={{0,4},{1,5},{2,6},{3,7},{4,8},{5,9},{6,10},{7,11},{8,0},{9,1},{10,... | collective-permute-start | bytes 110600 | tf_op jit(solution)/shard_map/ppermute | solution.py:323
  85.3 9.8 %collective-permute-start.5 = (bf16[16,1152]{1,0:T(8,128)(2,1)S(1)}, bf16[16,1152]{1,0:T(8,128)(2,1)S(1)}, u32[]{:S(2)}, u32[]{:S(2)}) collective-permute-start(bf16[16,1152]{1,0:T(8,128)(2,1)S(1)} %get-tuple-element.32), channel_id=1, source_target_pairs={{0,8},{1,9},{2,10},{3,11},{4,0},{5,1},{6,2},{7,3},{8,4},{9,5},{10,... | collective-permute-start | bytes 110600 | tf_op jit(solution)/shard_map/ppermute | solution.py:323
